TPU v7x, 32 devices: a whole 2x2x4 slice. The times are simulated.
32 devices in a mesh: seq: 4 (over y, x), res: 8 (over z, core).
Axes of the slice: x: 2, y: 2, z: 4, core: 2. Of those that a mesh axis runs over, the one named last changes fastest.
Arguments:
- alignment: bfloat16 [256, 64, 256], P(('seq', 'res')), may hold values from -6 to 6
- layer_norm_gain: float32 [256], replicated, may hold values from 0.1 to 1.9
- layer_norm_bias: float32 [256], replicated, may hold values from -0.6 to 0.6
- left_projection_weight: bfloat16 [256, 32], replicated, may hold values from -0.375 to 0.375
- left_bias: float32 [32], replicated, may hold values from -0.6 to 0.6
- right_projection_weight: bfloat16 [256, 32], replicated, may hold values from -0.375 to 0.375
- right_bias: float32 [32], replicated, may hold values from -0.6 to 0.6
- out_weight: bfloat16 [1024, 128], replicated, may hold values from -6 to 6
- out_bias: float32 [128], replicated, may hold values from -3 to 3
Outputs:
- pair_update: bfloat16 [64, 64, 128], P('res', 'seq')
All inputs are finite; a program needn't handle non-finite values.
Results may differ from a plain program's by a relative error of at most 0.022.
Values may be sent and summed in bfloat16 or wider, within the bound.
No kernel may reach another device: no remote copies, remote signals or barrier semaphores. Data moves between devices by JAX's collectives and lax.ppermute only.
A program may use at most 64 MiB of HBM per device.

v0:
```python
import jax
import jax.numpy as jnp
from jax import lax
from jax.sharding import PartitionSpec as P


def normalize_project(alignment, layer_norm_gain, layer_norm_bias, weight, bias):
    values = alignment.astype(jnp.float32)
    centre = jnp.mean(values, axis=-1, keepdims=True)
    spread = jnp.mean((values - centre) ** 2, axis=-1, keepdims=True)
    normed = (
        (values - centre) * lax.rsqrt(spread + 1e-05) * layer_norm_gain + layer_norm_bias
    ).astype(jnp.bfloat16)
    flat = normed.reshape(-1, normed.shape[-1])
    result = jnp.dot(flat, weight, preferred_element_type=jnp.float32) + bias
    return result.astype(jnp.bfloat16).reshape(normed.shape[:-1] + (weight.shape[1],))


def body(
    alignment,
    layer_norm_gain,
    layer_norm_bias,
    left_projection_weight,
    left_bias,
    right_projection_weight,
    right_bias,
    out_weight,
    out_bias,
):
    res_count = lax.axis_size("res")
    seq_count = lax.axis_size("seq")
    row_count, res_total, chan_count = alignment.shape
    res_block = res_total // res_count
    hidden_width = left_projection_weight.shape[1]
    pair_width = out_weight.shape[1]
    both_weights = jnp.concatenate([left_projection_weight, right_projection_weight], axis=1)
    both_biases = jnp.concatenate([left_bias, right_bias], axis=0)
    arrived = lax.all_to_all(
        alignment.reshape(row_count, res_count, res_block * chan_count),
        "res",
        split_axis=1,
        concat_axis=0,
        tiled=True,
    )
    projected = normalize_project(
        arrived.reshape(row_count * res_count, res_block, chan_count),
        layer_norm_gain,
        layer_norm_bias,
        both_weights,
        both_biases,
    )
    seq_local = projected.shape[0]
    seq_total = seq_local * seq_count
    left_cols = projected[:, :, :hidden_width].reshape(seq_local, res_block * hidden_width)
    right_cols = projected[:, :, hidden_width:].reshape(seq_local, res_block * hidden_width)
    col_piece = lax.all_gather(right_cols, "res", axis=1, tiled=True)
    col_res = col_piece.shape[1] // hidden_width
    outer_block = lax.dot_general(
        left_cols, col_piece, (((0,), (0,)), ((), ())), preferred_element_type=jnp.float32
    ) / float(seq_total)
    outer_block = outer_block.astype(jnp.bfloat16).reshape(
        res_block, hidden_width, col_res, hidden_width
    )
    outer_block = outer_block.transpose(0, 2, 1, 3).reshape(
        res_block * col_res, hidden_width * hidden_width
    )
    term_block = jnp.dot(outer_block, out_weight, preferred_element_type=jnp.float32)
    partial_terms = term_block.reshape(res_block, col_res, pair_width)
    summed = lax.psum_scatter(
        partial_terms.astype(jnp.bfloat16), "seq", scatter_dimension=1, tiled=True
    ).astype(jnp.float32)
    return (summed + out_bias).astype(jnp.bfloat16)


def solution(mesh):
    in_specs = (P(("seq", "res"), None, None), P(), P(), P(), P(), P(), P(), P(), P())
    out_specs = P("res", "seq", None)
    return jax.shard_map(body, mesh=mesh, in_specs=in_specs, out_specs=out_specs, check_vma=False)
```

profile of v0, /device:TPU:0, one launch (start us, length us, event | category | flops | bytes accessed | tf_op | source)
XLA Modules:
  0.0 82.4 jit_solution(13433922102964827573)
XLA Ops:
  6.5 0.0 copy-start
  6.5 1.1 %reshape.64 = bf16[8,8,2048]{2,1,0:T(8,128)(2,1)S(1)} reshape(bf16[8,64,256]{2,1,0:T(8,128)(2,1)} %param.9) | data formatting | bytes 524288 | tf_op jit(solution)/shard_map/reshape | solution.py:39
  7.7 0.8 %copy.11 = bf16[8,8,2048]{2,0,1:T(8,128)(2,1)} copy(bf16[8,8,2048]{2,1,0:T(8,128)(2,1)S(1)} %reshape.64) | data formatting | bytes 524288 | tf_op jit(solution)/shard_map/reshape | solution.py:39
  8.5 6.3 %all-to-all-start = ((bf16[8,8,2048]{2,0,1:T(8,128)(2,1)}), bf16[8,8,2048]{2,0,1:T(8,128)(2,1)S(1)}, u32[]{:S(2)}, u32[]{:S(2)}) async-start(bf16[8,8,2048]{2,0,1:T(8,128)(2,1)} %copy.11), calls=%async_computation | async-start | bytes 524288 | tf_op jit(solution)/shard_map/all_to_all | solution.py:38
  14.8 0.0 reduce-scatter.2.cloned.1.call-start
  14.9 0.7 pad_maximum_fusion
  15.6 0.0 copy-start.2
  15.6 0.0 copy-start.3
  15.6 0.0 copy-start.4
  15.6 0.0 copy-start.5
  15.6 8.9 %all-to-all-done = bf16[8,8,2048]{2,0,1:T(8,128)(2,1)S(1)} async-done(((bf16[8,8,2048]{2,0,1:T(8,128)(2,1)}), bf16[8,8,2048]{2,0,1:T(8,128)(2,1)S(1)}, u32[]{:S(2)}, u32[]{:S(2)}) %all-to-all-start) | async-done | bytes 262176 | tf_op jit(solution)/shard_map/all_to_all | solution.py:38
  24.6 0.1 bitcast_convert_fusion
  24.6 0.2 copy.18
  24.8 0.1 reduce_sum.18
  25.0 0.2 multiply_reduce_fusion
  25.2 0.1 div.15
  25.3 0.1 rsqrt.12
  25.4 0.1 reshape.69
  25.5 0.0 copy-done.2
  25.5 0.0 copy-done.3
  25.5 0.0 copy-done.4
  25.5 0.0 copy-done.5
  25.5 0.3 fusion.1
  25.9 0.1 copy.12
  26.0 0.1 fusion.12
  26.1 0.1 copy.14
  26.3 0.1 copy.13
  26.4 15.0 %all_gather.3 = bf16[64,2048]{0,1:T(8,128)(2,1)S(1)} all-gather(bf16[64,256]{0,1:T(8,128)(2,1)S(1)} %bitcast.33), channel_id=1, replica_groups=mesh['seq'=4,'res'=8] {'res'}, dimensions={1}, use_global_device_ids=true | all-gather | bytes 294912 | tf_op jit(solution)/shard_map/all_gather | solution.py:56
  41.4 0.4 fusion
  41.8 4.4 %reshape.68 = bf16[8,32,64,32]{3,2,1,0:T(8,128)(2,1)} reshape(bf16[256,2048]{1,0:T(8,128)(2,1)S(1)} %fusion) | data formatting | bytes 2097152 | tf_op jit(solution)/shard_map/reshape | solution.py:61
  46.2 3.7 %copy.15 = bf16[8,64,32,32]{1,3,2,0:T(8,128)(2,1)S(1)} copy(bf16[8,64,32,32]{3,1,2,0:T(8,128)(2,1)} %bitcast.27) | data formatting | bytes 2097152 | tf_op jit(solution)/shard_map/transpose | solution.py:64
  49.9 0.0 copy-start.1
  50.0 0.0 copy-done
  50.0 1.4 %convolution_convert_fusion = bf16[8,64,128]{2,1,0:T(8,128)(2,1)} fusion(bf16[8,64,1024]{1,2,0:T(8,128)(2,1)S(1)} %bitcast.28, bf16[1024,128]{1,0:T(8,128)(2,1)S(1)} %copy-done), kind=kOutput, calls=%fused_computation.2 | convolution fusion | flops 134283264 | bytes 1441792 | tf_op jit(solution)/shard_map/dot_general | solution.py:67
  51.4 0.0 reduce-scatter.2.cloned.1.call-update
  51.4 22.7 %reduce-scatter.2.cloned.1.call-done = bf16[8,16,128]{2,1,0:T(8,128)(2,1)} async-done(((bf16[8,64,128]{2,1,0:T(8,128)(2,1)}), bf16[8,16,128]{2,1,0:T(8,128)(2,1)}) %reduce-scatter.2.cloned.1.call-update) | async-done | bytes 32784 | tf_op jit(solution)/shard_map/reduce_scatter | solution.py:69
  74.2 0.0 copy-done.1
  74.2 1.4 %add_convert_fusion.2 = bf16[8,16,128]{2,1,0:T(8,128)(2,1)} fusion(bf16[8,16,128]{2,1,0:T(8,128)(2,1)} %reduce-scatter.2.cloned.1.call-done, f32[128]{0:T(128)S(1)} %copy-done.1), kind=kLoop, calls=%fused_computation.14 | loop fusion | flops 49152 | bytes 66048 | tf_op jit(solution)/shard_map/convert_element_type | solution.py:72
  (2 shorter events, 0.0 us)
Async XLA Ops:
  6.5 43.4 %copy-start = (bf16[1024,128]{1,0:T(8,128)(2,1)S(1)}, bf16[1024,128]{1,0:T(8,128)(2,1)}, u32[]{:S(2)}) copy-start(bf16[1024,128]{1,0:T(8,128)(2,1)} %param.16) | copy-start | bytes 786436
  8.5 16.1 %all-to-all-start = ((bf16[8,8,2048]{2,0,1:T(8,128)(2,1)}), bf16[8,8,2048]{2,0,1:T(8,128)(2,1)S(1)}, u32[]{:S(2)}, u32[]{:S(2)}) async-start(bf16[8,8,2048]{2,0,1:T(8,128)(2,1)} %copy.11), calls=%async_computation | async-start | bytes 524288 | tf_op jit(solution)/shard_map/all_to_all | solution.py:38
  14.8 59.3 %reduce-scatter.2.cloned.1.call-start = ((), (), s32[]{:S(2)}) async-start(), calls=%async_computation.2 | async-start | bytes 163840 | tf_op jit(solution)/shard_map/reduce_scatter | solution.py:69
  15.6 9.9 %copy-start.2 = (bf16[256,32]{0,1:T(8,128)(2,1)S(1)}, bf16[256,32]{0,1:T(8,128)(2,1)}, u32[]{:S(2)}) copy-start(bf16[256,32]{0,1:T(8,128)(2,1)} %param.14) | copy-start | bytes 49156
  15.6 9.9 %copy-start.3 = (bf16[256,32]{0,1:T(8,128)(2,1)S(1)}, bf16[256,32]{0,1:T(8,128)(2,1)}, u32[]{:S(2)}) copy-start(bf16[256,32]{0,1:T(8,128)(2,1)} %param.12) | copy-start | bytes 49156
  15.6 9.9 %copy-start.4 = (f32[256]{0:T(256)S(1)}, f32[256]{0:T(256)}, u32[]{:S(2)}) copy-start(f32[256]{0:T(256)} %param.11) | copy-start | bytes 3076
  15.6 9.9 %copy-start.5 = (f32[256]{0:T(256)S(1)}, f32[256]{0:T(256)}, u32[]{:S(2)}) copy-start(f32[256]{0:T(256)} %param.10) | copy-start | bytes 3076
  49.9 24.2 %copy-start.1 = (f32[128]{0:T(128)S(1)}, f32[128]{0:T(128)}, u32[]{:S(2)}) copy-start(f32[128]{0:T(128)} %param.17) | copy-start | bytes 1540
Sparse Core Ops, SparseCore 0:
  51.5 22.5 reduce-scatter.1
where the time goes:
time: 82.8 us; the launch traced here: 82.4 us
  waiting for transfers between devices  31.7 us (38%)
  blocking collectives  15 us (18%)
  between operations  13.5 us (16%)
  local copies, waits for them, and re-layouts  11 us (13%)
  starting transfers between devices  6.36 us (8%)
  other arithmetic  2.58 us (3%)
  matrix products  2.22 us (3%)
    reduce_scatter x1, waiting for transfers between devices, body(): lax.psum_scatter(partial_terms.astype(jnp.bfloat16), 'seq', scatter_dimen...  22.7 us
    all_gather x1, blocking collectives, body(): col_piece = lax.all_gather(right_cols, 'res', axis=1, tiled=True)  15 us
    all_to_all x1, waiting for transfers between devices, body(): lax.all_to_all(alignment.reshape(row_count, res_count, res_block * chan_c...  8.94 us
    all_to_all x1, starting transfers between devices, body(): lax.all_to_all(alignment.reshape(row_count, res_count, res_block * chan_c...  6.33 us
    reshape x1, local copies, waits for them, and re-layouts, body(): outer_block.astype(jnp.bfloat16)  4.43 us
    transpose x1, local copies, waits for them, and re-layouts, body(): outer_block.transpose(0, 2, 1, 3)  3.7 us
    reshape x2, local copies, waits for them, and re-layouts, body(): alignment.reshape(row_count, res_count, res_block * chan_count)  1.96 us
  transfers between devices with their start and end apart: 2, of which 2 were waited for; matrix products, arithmetic and copies ran while one was open for 1% of the time, Pallas kernels for 0%

commit v1 on v0

v1 whole, which is shorter than its diff:
```python
import functools

import jax
import jax.numpy as jnp
from jax import lax
from jax.experimental import pallas as pl
from jax.experimental.pallas import tpu as pltpu
from jax.sharding import PartitionSpec as P

LANES = 128


def project_kernel(
    seq_count,
    res_count,
    align_ref,
    gain_ref,
    offset_ref,
    left_w_ref,
    left_b_ref,
    right_w_ref,
    right_b_ref,
    send_ref,
    proj_ref,
):
    rows, res_total, chan = align_ref.shape
    hidden = left_w_ref.shape[0]
    values = align_ref[...].astype(jnp.float32).reshape(rows * res_total, chan)
    centred = values - jnp.mean(values, axis=-1, keepdims=True)
    spread = jnp.mean(centred * centred, axis=-1, keepdims=True)
    normed = centred * lax.rsqrt(spread + 1e-05) * gain_ref[...] + offset_ref[...]
    weights = jnp.concatenate([left_w_ref[...], right_w_ref[...]], axis=0)
    biases = jnp.concatenate([left_b_ref[...], right_b_ref[...]], axis=1)
    proj_ref[:, : 2 * hidden] = (
        lax.dot_general(
            normed.astype(jnp.bfloat16),
            weights,
            (((1,), (1,)), ((), ())),
            preferred_element_type=jnp.float32,
        )
        + biases
    )
    tiles = [proj_ref[pl.ds(r, rows, stride=res_total), :][:, : 2 * hidden] for r in range(res_total)]
    row_block = res_total // res_count
    col_block = res_total // seq_count
    left = [
        jnp.concatenate([t[:, :hidden] for t in tiles[a * row_block : (a + 1) * row_block]], axis=1)
        for a in range(res_count)
    ]
    right = [
        jnp.concatenate([t[:, hidden:] for t in tiles[b * col_block : (b + 1) * col_block]], axis=1)
        for b in range(seq_count)
    ]
    pieces = [
        jnp.concatenate([left[a], right[b]], axis=1)
        for b in range(seq_count)
        for a in range(res_count)
    ]
    group = max(1, 16 // rows)
    for start in range(0, len(pieces), group):
        block = jnp.concatenate(pieces[start : start + group], axis=0)
        send_ref[pl.ds(start * rows, group * rows), :] = block.astype(jnp.bfloat16)


def pair_kernel(hidden, row_block, col_block, recv_ref, weight_ref, bias_ref, out_ref, outer_ref, term_ref):
    seq_total = recv_ref.shape[0]
    left = recv_ref[:, : row_block * hidden]
    right = recv_ref[:, row_block * hidden :]
    outer = lax.dot_general(
        left, right, (((0,), (0,)), ((), ())), preferred_element_type=jnp.float32
    )
    for g in range(outer_ref.shape[0]):
        outer_ref[g] = outer[:, g * LANES : (g + 1) * LANES]
    per_group = LANES // hidden
    terms = []
    for g in range(outer_ref.shape[0]):
        slabs = [outer_ref[g, pl.ds(c, row_block, stride=hidden), :] for c in range(hidden)]
        for j in range(per_group):
            flat = jnp.concatenate([s[:, j * hidden : (j + 1) * hidden] for s in slabs], axis=1)
            terms.append(flat)
    flat = jnp.concatenate(terms, axis=0).astype(jnp.bfloat16)
    term = jnp.dot(flat, weight_ref[...], preferred_element_type=jnp.float32)
    term_ref[...] = term * (1.0 / float(seq_total)) + bias_ref[...]
    for i in range(row_block):
        out_ref[i] = term_ref[pl.ds(i, col_block, stride=row_block), :].astype(jnp.bfloat16)


def body(
    alignment,
    layer_norm_gain,
    layer_norm_bias,
    left_projection_weight,
    left_bias,
    right_projection_weight,
    right_bias,
    out_weight,
    out_bias,
):
    res_count = lax.axis_size("res")
    seq_count = lax.axis_size("seq")
    rows, res_total, chan = alignment.shape
    hidden = left_projection_weight.shape[1]
    pair_width = out_weight.shape[1]
    row_block = res_total // res_count
    col_block = res_total // seq_count
    device_count = seq_count * res_count
    width = (row_block + col_block) * hidden
    vmem = pl.BlockSpec(memory_space=pltpu.VMEM)
    send = pl.pallas_call(
        functools.partial(project_kernel, seq_count, res_count),
        out_shape=jax.ShapeDtypeStruct((device_count * rows, width), jnp.bfloat16),
        in_specs=[vmem] * 7,
        out_specs=vmem,
        scratch_shapes=[pltpu.VMEM((rows * res_total, LANES), jnp.float32)],
        compiler_params=pltpu.CompilerParams(vmem_limit_bytes=32 * 1024 * 1024),
    )(
        alignment,
        layer_norm_gain.reshape(1, chan),
        layer_norm_bias.reshape(1, chan),
        left_projection_weight.T,
        left_bias.reshape(1, hidden),
        right_projection_weight.T,
        right_bias.reshape(1, hidden),
    )
    recv = lax.all_to_all(send, ("seq", "res"), split_axis=0, concat_axis=0, tiled=True)
    return pl.pallas_call(
        functools.partial(pair_kernel, hidden, row_block, col_block),
        out_shape=jax.ShapeDtypeStruct((row_block, col_block, pair_width), jnp.bfloat16),
        in_specs=[vmem] * 3,
        out_specs=vmem,
        scratch_shapes=[
            pltpu.VMEM((col_block * hidden // LANES, row_block * hidden, LANES), jnp.float32),
            pltpu.VMEM((row_block * col_block, pair_width), jnp.float32),
        ],
        compiler_params=pltpu.CompilerParams(vmem_limit_bytes=32 * 1024 * 1024),
    )(recv, out_weight, out_bias.reshape(1, pair_width))


def solution(mesh):
    in_specs = (P(("seq", "res"), None, None), P(), P(), P(), P(), P(), P(), P(), P())
    out_specs = P("res", "seq", None)
    return jax.shard_map(body, mesh=mesh, in_specs=in_specs, out_specs=out_specs, check_vma=False)
```

time: 82.8 us -> 26.8 us (0.32)
  waiting for transfers between devices: 31.7 us -> 0 us
  between operations: 13.5 us -> 0.02 us
  local copies, waits for them, and re-layouts: 11 us -> 3.75 us
  starting transfers between devices: 6.36 us -> 0 us
  blocking collectives: 15 us -> 20.6 us
  other arithmetic: 2.58 us -> 0 us
  matrix products: 2.22 us -> 0 us
  Pallas kernels: 0 us -> 1.96 us
    reduce_scatter x1 -> x0, waiting for transfers between devices: 22.7 us -> none  [body(): lax.psum_scatter(partial_terms.astype(jnp.bfloat16), 'seq', scatter_dimen...]
    all_to_all x0 -> x1, blocking collectives: none -> 20.6 us  [body(): lax.all_to_all(send, ('seq', 'res'), split_axis=0, concat_axis=0, tiled=T...]
    all_gather x1 -> x0, blocking collectives: 15 us -> none  [body(): col_piece = lax.all_gather(right_cols, 'res', axis=1, tiled=True)]
    all_to_all x1 -> x0, waiting for transfers between devices: 8.94 us -> none  [body(): lax.all_to_all(alignment.reshape(row_count, res_count, res_block * chan_c...]
    reshape x3 -> x0, local copies, waits for them, and re-layouts: 6.38 us -> none  [the longest x1 4.43 us: body(): outer_block.astype(jnp.bfloat16)]
    all_to_all x1 -> x0, starting transfers between devices: 6.33 us -> none  [body(): lax.all_to_all(alignment.reshape(row_count, res_count, res_block * chan_c...]
    transpose x1 -> x0, local copies, waits for them, and re-layouts: 3.7 us -> none  [body(): outer_block.transpose(0, 2, 1, 3)]
    unnamed x13 -> x18, local copies, waits for them, and re-layouts: 0.19 us -> 3.75 us
  transfers between devices with their start and end apart: 2 -> 0, of which waited for: 2 -> 0; matrix products, arithmetic and copies ran while one was open for 1% -> 0% of each run, Pallas kernels for 0% -> 0%
where the time goes in v1:
time: 26.8 us; the launch traced here: 26.4 us
  blocking collectives  20.6 us (77%)
  local copies, waits for them, and re-layouts  3.75 us (14%)
  Pallas kernels  1.96 us (7%)
    all_to_all x1, blocking collectives, body(): lax.all_to_all(send, ('seq', 'res'), split_axis=0, concat_axis=0, tiled=T...  20.6 us
    unnamed x18, local copies, waits for them, and re-layouts  3.75 us
    pallas_call x1, Pallas kernels, body(): pl.pallas_call(functools.partial(pair_kernel, hidden, row_block, col_bloc...  1.4 us
    pallas_call x1, Pallas kernels, body(): pl.pallas_call(functools.partial(project_kernel, seq_count, res_count), o...  0.57 us

profile of v1, /device:TPU:0, one launch (start us, length us, event | category | flops | bytes accessed | tf_op | source)
XLA Modules:
  0.0 26.4 jit_solution(8514229726672834074)
XLA Ops:
  0.0 0.0 copy-start.5
  0.0 0.0 copy-start.8
  0.0 0.0 copy-start.4
  0.0 0.0 copy-start.7
  0.0 0.7 %copy-done.5 = f32[256]{0:T(256)S(1)} copy-done((f32[256]{0:T(256)S(1)}, f32[256]{0:T(256)}, u32[]{:S(2)}) %copy-start.5) | copy-done | bytes 1048
  0.7 0.0 copy-done.8
  0.7 0.0 copy-done.4
  0.7 0.0 copy-done.7
  0.7 0.0 copy-start
  0.7 0.9 %copy-done = bf16[8,64,256]{2,1,0:T(8,128)(2,1)S(1)} copy-done((bf16[8,64,256]{2,1,0:T(8,128)(2,1)S(1)}, bf16[8,64,256]{2,1,0:T(8,128)(2,1)}, u32[]{:S(2)}) %copy-start) | copy-done | bytes 262168
  1.7 0.0 copy-start.2
  1.7 0.7 %copy-done.2 = bf16[256,32]{0,1:T(8,128)(2,1)S(1)} copy-done((bf16[256,32]{0,1:T(8,128)(2,1)S(1)}, bf16[256,32]{0,1:T(8,128)(2,1)}, u32[]{:S(2)}) %copy-start.2) | copy-done | bytes 16408
  2.4 0.0 copy-start.3
  2.4 0.7 %copy-done.3 = bf16[256,32]{0,1:T(8,128)(2,1)S(1)} copy-done((bf16[256,32]{0,1:T(8,128)(2,1)S(1)}, bf16[256,32]{0,1:T(8,128)(2,1)}, u32[]{:S(2)}) %copy-start.3) | copy-done | bytes 16408
  3.1 0.6 %shard_map.91 = bf16[256,768]{1,0:T(8,128)(2,1)S(1)} custom-call(bf16[8,64,256]{2,1,0:T(8,128)(2,1)S(1)} %copy-done, f32[1,256]{1,0:T(1,128)S(1)} %bitcast.13, f32[1,256]{1,0:T(1,128)S(1)} %bitcast.14, bf16[32,256]{1,0:T(8,128)(2,1)S(1)} %bitcast.11, f32[1,32]{1,0:T(1,128)S(1)} %bitcast.16, bf16[32,256]{1,0:T(8,128)(2,1)S(1)} %bitcast.12, f32[1,32]{1,0:T(1,128)S(1)} %bitcast.17), custom_call_target="tpu_custom_call" | custom-call | tf_op jit(solution)/shard_map/pallas_call | solution.py:109
  3.7 0.0 copy-start.1
  3.7 20.6 %all_to_all.11 = bf16[32,8,768]{2,1,0:T(8,128)(2,1)S(1)} all-to-all(bf16[32,8,768]{2,1,0:T(8,128)(2,1)S(1)} %bitcast.10), channel_id=1, replica_groups=mesh['seq'=4,'res'=8] {'seq','res'}, dimensions={0} | all-to-all | bytes 786432 | tf_op jit(solution)/shard_map/all_to_all | solution.py:125
  24.3 0.0 copy-start.6
  24.3 0.0 copy-done.1
  24.3 0.7 %copy-done.6 = f32[128]{0:T(128)S(1)} copy-done((f32[128]{0:T(128)S(1)}, f32[128]{0:T(128)}, u32[]{:S(2)}) %copy-start.6) | copy-done | bytes 536
  25.0 1.4 %shard_map.92 = bf16[8,16,128]{2,1,0:T(8,128)(2,1)} custom-call(bf16[256,768]{1,0:T(8,128)(2,1)S(1)} %bitcast.9, bf16[1024,128]{1,0:T(8,128)(2,1)S(1)} %copy-done.1, f32[1,128]{1,0:T(1,128)S(1)} %bitcast.15), custom_call_target="tpu_custom_call" | custom-call | tf_op jit(solution)/shard_map/pallas_call | solution.py:126
Async XLA Ops:
  0.0 0.7 %copy-start.5 = (f32[256]{0:T(256)S(1)}, f32[256]{0:T(256)}, u32[]{:S(2)}) copy-start(f32[256]{0:T(256)} %param.11) | copy-start | bytes 3076
  0.0 0.7 %copy-start.8 = (f32[32]{0:T(128)S(1)}, f32[32]{0:T(128)}, u32[]{:S(2)}) copy-start(f32[32]{0:T(128)} %param.15) | copy-start | bytes 388
  0.0 0.7 %copy-start.4 = (f32[256]{0:T(256)S(1)}, f32[256]{0:T(256)}, u32[]{:S(2)}) copy-start(f32[256]{0:T(256)} %param.10) | copy-start | bytes 3076
  0.0 0.7 %copy-start.7 = (f32[32]{0:T(128)S(1)}, f32[32]{0:T(128)}, u32[]{:S(2)}) copy-start(f32[32]{0:T(128)} %param.13) | copy-start | bytes 388
  0.7 1.0 %copy-start = (bf16[8,64,256]{2,1,0:T(8,128)(2,1)S(1)}, bf16[8,64,256]{2,1,0:T(8,128)(2,1)}, u32[]{:S(2)}) copy-start(bf16[8,64,256]{2,1,0:T(8,128)(2,1)} %align_ref.1) | copy-start | bytes 786436
  1.7 0.7 %copy-start.2 = (bf16[256,32]{0,1:T(8,128)(2,1)S(1)}, bf16[256,32]{0,1:T(8,128)(2,1)}, u32[]{:S(2)}) copy-start(bf16[256,32]{0,1:T(8,128)(2,1)} %param.12) | copy-start | bytes 49156
  2.4 0.7 %copy-start.3 = (bf16[256,32]{0,1:T(8,128)(2,1)S(1)}, bf16[256,32]{0,1:T(8,128)(2,1)}, u32[]{:S(2)}) copy-start(bf16[256,32]{0,1:T(8,128)(2,1)} %param.14) | copy-start | bytes 49156
  3.7 20.7 %copy-start.1 = (bf16[1024,128]{1,0:T(8,128)(2,1)S(1)}, bf16[1024,128]{1,0:T(8,128)(2,1)}, u32[]{:S(2)}) copy-start(bf16[1024,128]{1,0:T(8,128)(2,1)} %weight_ref.1) | copy-start | bytes 786436
  24.3 0.7 %copy-start.6 = (f32[128]{0:T(128)S(1)}, f32[128]{0:T(128)}, u32[]{:S(2)}) copy-start(f32[128]{0:T(128)} %param.17) | copy-start | bytes 1540

commit v2 on v1

--- a/solution.py
+++ b/solution.py
@@ -13,6 +13,14 @@
 def project_kernel(
     seq_count,
     res_count,
+    align_hbm,
+    gain_hbm,
+    offset_hbm,
+    left_w_hbm,
+    left_b_hbm,
+    right_w_hbm,
+    right_b_hbm,
+    send_ref,
     align_ref,
     gain_ref,
     offset_ref,
@@ -20,9 +28,27 @@
     left_b_ref,
     right_w_ref,
     right_b_ref,
-    send_ref,
     proj_ref,
+    sems,
 ):
+    copies = [
+        pltpu.make_async_copy(source, target, sems.at[n])
+        for n, (source, target) in enumerate(
+            [
+                (align_hbm, align_ref),
+                (gain_hbm, gain_ref),
+                (offset_hbm, offset_ref),
+                (left_w_hbm, left_w_ref),
+                (left_b_hbm, left_b_ref),
+                (right_w_hbm, right_w_ref),
+                (right_b_hbm, right_b_ref),
+            ]
+        )
+    ]
+    for copy in copies:
+        copy.start()
+    for copy in copies:
+        copy.wait()
     rows, res_total, chan = align_ref.shape
     hidden = left_w_ref.shape[0]
     values = align_ref[...].astype(jnp.float32).reshape(rows * res_total, chan)
@@ -62,7 +88,21 @@
         send_ref[pl.ds(start * rows, group * rows), :] = block.astype(jnp.bfloat16)
 
 
-def pair_kernel(hidden, row_block, col_block, recv_ref, weight_ref, bias_ref, out_ref, outer_ref, term_ref):
+def pair_kernel(
+    hidden,
+    row_block,
+    col_block,
+    recv_ref,
+    weight_ref,
+    bias_hbm,
+    out_ref,
+    bias_ref,
+    outer_ref,
+    term_ref,
+    sem,
+):
+    bias_copy = pltpu.make_async_copy(bias_hbm, bias_ref, sem)
+    bias_copy.start()
     seq_total = recv_ref.shape[0]
     left = recv_ref[:, : row_block * hidden]
     right = recv_ref[:, row_block * hidden :]
@@ -80,9 +120,14 @@
             terms.append(flat)
     flat = jnp.concatenate(terms, axis=0).astype(jnp.bfloat16)
     term = jnp.dot(flat, weight_ref[...], preferred_element_type=jnp.float32)
+    bias_copy.wait()
     term_ref[...] = term * (1.0 / float(seq_total)) + bias_ref[...]
     for i in range(row_block):
         out_ref[i] = term_ref[pl.ds(i, col_block, stride=row_block), :].astype(jnp.bfloat16)
+
+
+def in_hbm(array):
+    return pltpu.with_memory_space_constraint(array, pltpu.HBM)
 
 
 def body(
@@ -106,34 +151,47 @@
     device_count = seq_count * res_count
     width = (row_block + col_block) * hidden
     vmem = pl.BlockSpec(memory_space=pltpu.VMEM)
+    hbm = pl.BlockSpec(memory_space=pltpu.HBM)
     send = pl.pallas_call(
         functools.partial(project_kernel, seq_count, res_count),
         out_shape=jax.ShapeDtypeStruct((device_count * rows, width), jnp.bfloat16),
-        in_specs=[vmem] * 7,
+        in_specs=[hbm] * 7,
         out_specs=vmem,
-        scratch_shapes=[pltpu.VMEM((rows * res_total, LANES), jnp.float32)],
+        scratch_shapes=[
+            pltpu.VMEM((rows, res_total, chan), jnp.bfloat16),
+            pltpu.VMEM((1, chan), jnp.float32),
+            pltpu.VMEM((1, chan), jnp.float32),
+            pltpu.VMEM((hidden, chan), jnp.bfloat16),
+            pltpu.VMEM((1, hidden), jnp.float32),
+            pltpu.VMEM((hidden, chan), jnp.bfloat16),
+            pltpu.VMEM((1, hidden), jnp.float32),
+            pltpu.VMEM((rows * res_total, LANES), jnp.float32),
+            pltpu.SemaphoreType.DMA((7,)),
+        ],
         compiler_params=pltpu.CompilerParams(vmem_limit_bytes=32 * 1024 * 1024),
     )(
-        alignment,
-        layer_norm_gain.reshape(1, chan),
-        layer_norm_bias.reshape(1, chan),
-        left_projection_weight.T,
-        left_bias.reshape(1, hidden),
-        right_projection_weight.T,
-        right_bias.reshape(1, hidden),
+        in_hbm(alignment),
+        in_hbm(layer_norm_gain.reshape(1, chan)),
+        in_hbm(layer_norm_bias.reshape(1, chan)),
+        in_hbm(left_projection_weight.T),
+        in_hbm(left_bias.reshape(1, hidden)),
+        in_hbm(right_projection_weight.T),
+        in_hbm(right_bias.reshape(1, hidden)),
     )
     recv = lax.all_to_all(send, ("seq", "res"), split_axis=0, concat_axis=0, tiled=True)
     return pl.pallas_call(
         functools.partial(pair_kernel, hidden, row_block, col_block),
         out_shape=jax.ShapeDtypeStruct((row_block, col_block, pair_width), jnp.bfloat16),
-        in_specs=[vmem] * 3,
+        in_specs=[vmem, vmem, hbm],
         out_specs=vmem,
         scratch_shapes=[
+            pltpu.VMEM((1, pair_width), jnp.float32),
             pltpu.VMEM((col_block * hidden // LANES, row_block * hidden, LANES), jnp.float32),
             pltpu.VMEM((row_block * col_block, pair_width), jnp.float32),
+            pltpu.SemaphoreType.DMA,
         ],
         compiler_params=pltpu.CompilerParams(vmem_limit_bytes=32 * 1024 * 1024),
-    )(recv, out_weight, out_bias.reshape(1, pair_width))
+    )(recv, out_weight, in_hbm(out_bias.reshape(1, pair_width)))
 
 
 def solution(mesh):

time: 26.8 us -> 24.3 us (0.907)
  local copies, waits for them, and re-layouts: 3.75 us -> 0.01 us
  Pallas kernels: 1.96 us -> 3.47 us
    unnamed x18 -> x2, local copies, waits for them, and re-layouts: 3.75 us -> 0.01 us
    pallas_call x1, Pallas kernels: 0.57 us -> 1.6 us  [body(): pl.pallas_call(functools.partial(project_kernel, seq_count, res_count), o...]
    pallas_call x1, Pallas kernels: 1.4 us -> 1.87 us  [body(): pl.pallas_call(functools.partial(pair_kernel, hidden, row_block, col_bloc...]
where the time goes in v2:
time: 24.3 us; the launch traced here: 24.1 us
  blocking collectives  20.6 us (85%)
  Pallas kernels  3.47 us (14%)
    all_to_all x1, blocking collectives, body(): lax.all_to_all(send, ('seq', 'res'), split_axis=0, concat_axis=0, tiled=T...  20.6 us
    pallas_call x1, Pallas kernels, body(): pl.pallas_call(functools.partial(pair_kernel, hidden, row_block, col_bloc...  1.87 us
    pallas_call x1, Pallas kernels, body(): pl.pallas_call(functools.partial(project_kernel, seq_count, res_count), o...  1.6 us

profile of v2, /device:TPU:0, one launch (start us, length us, event | category | flops | bytes accessed | tf_op | source)
XLA Modules:
  0.0 24.1 jit_solution(5525459059891744022)
XLA Ops:
  0.0 1.6 %shard_map.91 = bf16[256,768]{1,0:T(8,128)(2,1)S(1)} custom-call(bf16[8,64,256]{2,1,0:T(8,128)(2,1)} %align_hbm.1, f32[1,256]{1,0:T(1,128)} %bitcast.13, f32[1,256]{1,0:T(1,128)} %bitcast.14, bf16[32,256]{1,0:T(8,128)(2,1)} %bitcast.11, f32[1,32]{1,0:T(1,128)} %bitcast.16, bf16[32,256]{1,0:T(8,128)(2,1)} %bitcast.12, f32[1,32]{1,0:T(1,128)} %bitcast.17), custom_call_target="tpu_custom_call" | custom-call | tf_op jit(solution)/shard_map/pallas_call | solution.py:155
  1.6 0.0 copy-start
  1.6 20.6 %all_to_all.11 = bf16[32,8,768]{2,1,0:T(8,128)(2,1)S(1)} all-to-all(bf16[32,8,768]{2,1,0:T(8,128)(2,1)S(1)} %bitcast.10), channel_id=1, replica_groups=mesh['seq'=4,'res'=8] {'seq','res'}, dimensions={0} | all-to-all | bytes 786432 | tf_op jit(solution)/shard_map/all_to_all | solution.py:181
  22.3 0.0 copy-done
  22.3 1.9 %shard_map.92 = bf16[8,16,128]{2,1,0:T(8,128)(2,1)} custom-call(bf16[256,768]{1,0:T(8,128)(2,1)S(1)} %bitcast.9, bf16[1024,128]{1,0:T(8,128)(2,1)S(1)} %copy-done, f32[1,128]{1,0:T(1,128)} %bitcast.15), custom_call_target="tpu_custom_call" | custom-call | tf_op jit(solution)/shard_map/pallas_call | solution.py:182
Async XLA Ops:
  1.6 20.7 %copy-start = (bf16[1024,128]{1,0:T(8,128)(2,1)S(1)}, bf16[1024,128]{1,0:T(8,128)(2,1)}, u32[]{:S(2)}) copy-start(bf16[1024,128]{1,0:T(8,128)(2,1)} %weight_ref.1) | copy-start | bytes 786436

commit v3 on v2

--- a/solution.py
+++ b/solution.py
@@ -20,17 +20,23 @@
     left_b_hbm,
     right_w_hbm,
     right_b_hbm,
-    send_ref,
-    align_ref,
-    gain_ref,
-    offset_ref,
-    left_w_ref,
-    left_b_ref,
-    right_w_ref,
-    right_b_ref,
-    proj_ref,
-    sems,
+    out_b_hbm,
+    *refs,
 ):
+    out_b_ref, *send_refs = refs[: 1 + seq_count * res_count]
+    (
+        align_ref,
+        gain_ref,
+        offset_ref,
+        left_w_ref,
+        left_b_ref,
+        right_w_ref,
+        right_b_ref,
+        proj_ref,
+        left_ref,
+        right_ref,
+        sems,
+    ) = refs[1 + seq_count * res_count :]
     copies = [
         pltpu.make_async_copy(source, target, sems.at[n])
         for n, (source, target) in enumerate(
@@ -42,6 +48,7 @@
                 (left_b_hbm, left_b_ref),
                 (right_w_hbm, right_w_ref),
                 (right_b_hbm, right_b_ref),
+                (out_b_hbm, out_b_ref),
             ]
         )
     ]
@@ -69,43 +76,28 @@
     tiles = [proj_ref[pl.ds(r, rows, stride=res_total), :][:, : 2 * hidden] for r in range(res_total)]
     row_block = res_total // res_count
     col_block = res_total // seq_count
-    left = [
-        jnp.concatenate([t[:, :hidden] for t in tiles[a * row_block : (a + 1) * row_block]], axis=1)
-        for a in range(res_count)
-    ]
-    right = [
-        jnp.concatenate([t[:, hidden:] for t in tiles[b * col_block : (b + 1) * col_block]], axis=1)
-        for b in range(seq_count)
-    ]
-    pieces = [
-        jnp.concatenate([left[a], right[b]], axis=1)
-        for b in range(seq_count)
-        for a in range(res_count)
-    ]
-    group = max(1, 16 // rows)
-    for start in range(0, len(pieces), group):
-        block = jnp.concatenate(pieces[start : start + group], axis=0)
-        send_ref[pl.ds(start * rows, group * rows), :] = block.astype(jnp.bfloat16)
-
-
-def pair_kernel(
-    hidden,
-    row_block,
-    col_block,
-    recv_ref,
-    weight_ref,
-    bias_hbm,
-    out_ref,
-    bias_ref,
-    outer_ref,
-    term_ref,
-    sem,
-):
-    bias_copy = pltpu.make_async_copy(bias_hbm, bias_ref, sem)
-    bias_copy.start()
-    seq_total = recv_ref.shape[0]
-    left = recv_ref[:, : row_block * hidden]
-    right = recv_ref[:, row_block * hidden :]
+    for a in range(res_count):
+        left_ref[a] = jnp.concatenate(
+            [t[:, :hidden] for t in tiles[a * row_block : (a + 1) * row_block]], axis=1
+        )
+    for b in range(seq_count):
+        right_ref[b] = jnp.concatenate(
+            [t[:, hidden:] for t in tiles[b * col_block : (b + 1) * col_block]], axis=1
+        )
+    seq_at = lax.axis_index("seq")
+    res_at = lax.axis_index("res")
+    split = row_block * hidden
+    for k, send_ref in enumerate(send_refs):
+        send_ref[:, :split] = left_ref[res_at ^ (k % res_count)].astype(jnp.bfloat16)
+        send_ref[:, split:] = right_ref[seq_at ^ (k // res_count)].astype(jnp.bfloat16)
+
+
+def pair_kernel(hidden, row_block, col_block, weight_ref, bias_ref, *refs):
+    *recv_refs, out_ref, outer_ref, term_ref = refs
+    recv = jnp.concatenate([ref[...] for ref in recv_refs], axis=0)
+    seq_total = recv.shape[0]
+    left = recv[:, : row_block * hidden]
+    right = recv[:, row_block * hidden :]
     outer = lax.dot_general(
         left, right, (((0,), (0,)), ((), ())), preferred_element_type=jnp.float32
     )
@@ -120,7 +112,6 @@
             terms.append(flat)
     flat = jnp.concatenate(terms, axis=0).astype(jnp.bfloat16)
     term = jnp.dot(flat, weight_ref[...], preferred_element_type=jnp.float32)
-    bias_copy.wait()
     term_ref[...] = term * (1.0 / float(seq_total)) + bias_ref[...]
     for i in range(row_block):
         out_ref[i] = term_ref[pl.ds(i, col_block, stride=row_block), :].astype(jnp.bfloat16)
@@ -152,11 +143,13 @@
     width = (row_block + col_block) * hidden
     vmem = pl.BlockSpec(memory_space=pltpu.VMEM)
     hbm = pl.BlockSpec(memory_space=pltpu.HBM)
-    send = pl.pallas_call(
+    params = pltpu.CompilerParams(vmem_limit_bytes=32 * 1024 * 1024)
+    bias_row, *sends = pl.pallas_call(
         functools.partial(project_kernel, seq_count, res_count),
-        out_shape=jax.ShapeDtypeStruct((device_count * rows, width), jnp.bfloat16),
-        in_specs=[hbm] * 7,
-        out_specs=vmem,
+        out_shape=[jax.ShapeDtypeStruct((1, pair_width), jnp.float32)]
+        + [jax.ShapeDtypeStruct((rows, width), jnp.bfloat16)] * device_count,
+        in_specs=[hbm] * 8,
+        out_specs=[vmem] * (1 + device_count),
         scratch_shapes=[
             pltpu.VMEM((rows, res_total, chan), jnp.bfloat16),
             pltpu.VMEM((1, chan), jnp.float32),
@@ -166,9 +159,11 @@
             pltpu.VMEM((hidden, chan), jnp.bfloat16),
             pltpu.VMEM((1, hidden), jnp.float32),
             pltpu.VMEM((rows * res_total, LANES), jnp.float32),
-            pltpu.SemaphoreType.DMA((7,)),
+            pltpu.VMEM((res_count, rows, row_block * hidden), jnp.float32),
+            pltpu.VMEM((seq_count, rows, col_block * hidden), jnp.float32),
+            pltpu.SemaphoreType.DMA((8,)),
         ],
-        compiler_params=pltpu.CompilerParams(vmem_limit_bytes=32 * 1024 * 1024),
+        compiler_params=params,
     )(
         in_hbm(alignment),
         in_hbm(layer_norm_gain.reshape(1, chan)),
@@ -177,21 +172,29 @@
         in_hbm(left_bias.reshape(1, hidden)),
         in_hbm(right_projection_weight.T),
         in_hbm(right_bias.reshape(1, hidden)),
+        in_hbm(out_bias.reshape(1, pair_width)),
     )
-    recv = lax.all_to_all(send, ("seq", "res"), split_axis=0, concat_axis=0, tiled=True)
+    if device_count <= 32:
+        recvs = [sends[0]]
+        for k in range(1, device_count):
+            pairs = [(n, n ^ k) for n in range(device_count)]
+            recvs.append(lax.ppermute(sends[k], ("seq", "res"), pairs))
+    else:
+        relative = jnp.stack(sends)
+        order = jnp.arange(device_count) ^ lax.axis_index(("seq", "res"))
+        stacked = lax.all_to_all(relative[order], ("seq", "res"), split_axis=0, concat_axis=0, tiled=True)
+        recvs = [stacked.reshape(device_count * rows, width)]
     return pl.pallas_call(
         functools.partial(pair_kernel, hidden, row_block, col_block),
         out_shape=jax.ShapeDtypeStruct((row_block, col_block, pair_width), jnp.bfloat16),
-        in_specs=[vmem, vmem, hbm],
+        in_specs=[vmem] * (2 + len(recvs)),
         out_specs=vmem,
         scratch_shapes=[
-            pltpu.VMEM((1, pair_width), jnp.float32),
             pltpu.VMEM((col_block * hidden // LANES, row_block * hidden, LANES), jnp.float32),
             pltpu.VMEM((row_block * col_block, pair_width), jnp.float32),
-            pltpu.SemaphoreType.DMA,
         ],
-        compiler_params=pltpu.CompilerParams(vmem_limit_bytes=32 * 1024 * 1024),
-    )(recv, out_weight, in_hbm(out_bias.reshape(1, pair_width)))
+        compiler_params=params,
+    )(out_weight, bias_row, *recvs)
 
 
 def solution(mesh):

time: 24.3 us -> 60.5 us (2.49)
  starting transfers between devices: 0 us -> 50.4 us
  blocking collectives: 20.6 us -> 0 us
  waiting for transfers between devices: 0 us -> 6.75 us
    ppermute x0 -> x31, starting transfers between devices: none -> 50.4 us  [body(): recvs.append(lax.ppermute(sends[k], ('seq', 'res'), pairs))]
    all_to_all x1 -> x0, blocking collectives: 20.6 us -> none  [body(): lax.all_to_all(send, ('seq', 'res'), split_axis=0, concat_axis=0, tiled=T...]
    ppermute x0 -> x31, waiting for transfers between devices: none -> 6.75 us  [body(): recvs.append(lax.ppermute(sends[k], ('seq', 'res'), pairs))]
  transfers between devices with their start and end apart: 0 -> 31, of which waited for: 0 -> 4; matrix products, arithmetic and copies ran while one was open for 0% -> 0% of each run, Pallas kernels for 0% -> 0%
where the time goes in v3:
time: 60.5 us; the launch traced here: 60.3 us
  starting transfers between devices  50.4 us (83%)
  waiting for transfers between devices  6.75 us (11%)
  Pallas kernels  3.09 us (5%)
    ppermute x31, starting transfers between devices, body(): recvs.append(lax.ppermute(sends[k], ('seq', 'res'), pairs))  50.4 us
    ppermute x31, waiting for transfers between devices, body(): recvs.append(lax.ppermute(sends[k], ('seq', 'res'), pairs))  6.75 us
    pallas_call x1, Pallas kernels, body(): pl.pallas_call(functools.partial(project_kernel, seq_count, res_count), o...  1.68 us
    pallas_call x1, Pallas kernels, body(): pl.pallas_call(functools.partial(pair_kernel, hidden, row_block, col_bloc...  1.41 us
  transfers between devices with their start and end apart: 31, of which 4 were waited for; matrix products, arithmetic and copies ran while one was open for 0% of the time, Pallas kernels for 0%

profile of v3, /device:TPU:0, one launch (start us, length us, event | category | flops | bytes accessed | tf_op | source)
XLA Modules:
  0.0 60.3 jit_solution(6055562346275408483)
XLA Ops:
  0.0 1.7 %shard_map.91 = (f32[1,128]{1,0:T(1,128)S(1)}, bf16[8,768]{1,0:T(8,128)(2,1)S(1)}, bf16[8,768]{1,0:T(8,128)(2,1)S(1)}, bf16[8,768]{1,0:T(8,128)(2,1)S(1)}, bf16[...) custom-call(bf16[8,64,256]{2,1,0:T(8,128)(2,1)} %align_hbm.1, ...), custom_call_target="tpu_custom_call" | custom-call | tf_op jit(solution)/shard_map/pallas_call | solution.py:147
  1.7 0.5 collective-permute-start
  2.2 2.6 %collective-permute-start.1 = (bf16[8,768]{1,0:T(8,128)(2,1)S(1)}, bf16[8,768]{1,0:T(8,128)(2,1)S(1)}, u32[]{:S(2)}, u32[]{:S(2)}) collective-permute-start(bf16[8,768]{1,0:T(8,128)(2,1)S(1)} %get-tuple-element.41), channel_id=1, source_target_pairs={{0,2},{1,3},{2,0},{3,1},{4,6},{5,7},{6,4},{7,5},{8,10},{9,11},{10,... | collective-permute-start | bytes 36872 | tf_op jit(solution)/shard_map/ppermute | solution.py:181
  4.9 0.1 collective-permute-start.2
  4.9 2.8 %collective-permute-start.3 = (bf16[8,768]{1,0:T(8,128)(2,1)S(1)}, bf16[8,768]{1,0:T(8,128)(2,1)S(1)}, u32[]{:S(2)}, u32[]{:S(2)}) collective-permute-start(bf16[8,768]{1,0:T(8,128)(2,1)S(1)} %get-tuple-element.43), channel_id=1, source_target_pairs={{0,4},{1,5},{2,6},{3,7},{4,0},{5,1},{6,2},{7,3},{8,12},{9,13},{10,... | collective-permute-start | bytes 36872 | tf_op jit(solution)/shard_map/ppermute | solution.py:181
  7.7 0.0 collective-permute-start.4
  7.7 3.6 %collective-permute-start.5 = (bf16[8,768]{1,0:T(8,128)(2,1)S(1)}, bf16[8,768]{1,0:T(8,128)(2,1)S(1)}, u32[]{:S(2)}, u32[]{:S(2)}) collective-permute-start(bf16[8,768]{1,0:T(8,128)(2,1)S(1)} %get-tuple-element.45), channel_id=1, source_target_pairs={{0,6},{1,7},{2,4},{3,5},{4,2},{5,3},{6,0},{7,1},{8,14},{9,15},{10,... | collective-permute-start | bytes 36872 | tf_op jit(solution)/shard_map/ppermute | solution.py:181
  11.3 0.0 collective-permute-done.1.refs_2_
  11.3 0.1 collective-permute-start.6
  11.4 1.5 %collective-permute-start.7 = (bf16[8,768]{1,0:T(8,128)(2,1)S(1)}, bf16[8,768]{1,0:T(8,128)(2,1)S(1)}, u32[]{:S(2)}, u32[]{:S(2)}) collective-permute-start(bf16[8,768]{1,0:T(8,128)(2,1)S(1)} %get-tuple-element.47), channel_id=1, source_target_pairs={{0,8},{1,9},{2,10},{3,11},{4,12},{5,13},{6,14},{7,15},{8,0},{9,1},... | collective-permute-start | bytes 36872 | tf_op jit(solution)/shard_map/ppermute | solution.py:181
  12.9 0.0 collective-permute-done.3.refs_4_
  12.9 0.1 collective-permute-start.8
  13.0 0.0 collective-permute-done.4.refs_5_
  13.0 1.2 %collective-permute-start.9 = (bf16[8,768]{1,0:T(8,128)(2,1)S(1)}, bf16[8,768]{1,0:T(8,128)(2,1)S(1)}, u32[]{:S(2)}, u32[]{:S(2)}) collective-permute-start(bf16[8,768]{1,0:T(8,128)(2,1)S(1)} %get-tuple-element.49), channel_id=1, source_target_pairs={{0,10},{1,11},{2,8},{3,9},{4,14},{5,15},{6,12},{7,13},{8,2},{9,3},... | collective-permute-start | bytes 36872 | tf_op jit(solution)/shard_map/ppermute | solution.py:181
  14.2 0.0 collective-permute-done.5.refs_6_
  14.2 1.6 %collective-permute-start.10 = (bf16[8,768]{1,0:T(8,128)(2,1)S(1)}, bf16[8,768]{1,0:T(8,128)(2,1)S(1)}, u32[]{:S(2)}, u32[]{:S(2)}) collective-permute-start(bf16[8,768]{1,0:T(8,128)(2,1)S(1)} %get-tuple-element.50), channel_id=1, source_target_pairs={{0,11},{1,10},{2,9},{3,8},{4,15},{5,14},{6,13},{7,12},{8,3},{9,2},... | collective-permute-start | bytes 36872 | tf_op jit(solution)/shard_map/ppermute | solution.py:181
  15.8 0.4 collective-permute-done.6.refs_7_
  16.2 2.0 %collective-permute-start.11 = (bf16[8,768]{1,0:T(8,128)(2,1)S(1)}, bf16[8,768]{1,0:T(8,128)(2,1)S(1)}, u32[]{:S(2)}, u32[]{:S(2)}) collective-permute-start(bf16[8,768]{1,0:T(8,128)(2,1)S(1)} %get-tuple-element.51), channel_id=1, source_target_pairs={{0,12},{1,13},{2,14},{3,15},{4,8},{5,9},{6,10},{7,11},{8,4},{9,5},... | collective-permute-start | bytes 36872 | tf_op jit(solution)/shard_map/ppermute | solution.py:181
  18.2 0.0 collective-permute-done.7.refs_8_
  18.2 1.3 %collective-permute-start.12 = (bf16[8,768]{1,0:T(8,128)(2,1)S(1)}, bf16[8,768]{1,0:T(8,128)(2,1)S(1)}, u32[]{:S(2)}, u32[]{:S(2)}) collective-permute-start(bf16[8,768]{1,0:T(8,128)(2,1)S(1)} %get-tuple-element.52), channel_id=1, source_target_pairs={{0,13},{1,12},{2,15},{3,14},{4,9},{5,8},{6,11},{7,10},{8,5},{9,4},... | collective-permute-start | bytes 36872 | tf_op jit(solution)/shard_map/ppermute | solution.py:181
  19.5 0.0 collective-permute-done.8.refs_9_
  19.5 4.2 %collective-permute-start.13 = (bf16[8,768]{1,0:T(8,128)(2,1)S(1)}, bf16[8,768]{1,0:T(8,128)(2,1)S(1)}, u32[]{:S(2)}, u32[]{:S(2)}) collective-permute-start(bf16[8,768]{1,0:T(8,128)(2,1)S(1)} %get-tuple-element.53), channel_id=1, source_target_pairs={{0,14},{1,15},{2,12},{3,13},{4,10},{5,11},{6,8},{7,9},{8,6},{9,7},... | collective-permute-start | bytes 36872 | tf_op jit(solution)/shard_map/ppermute | solution.py:181
  23.7 0.0 collective-permute-done.9.refs_10_
  23.7 0.5 collective-permute-start.14
  24.2 0.0 collective-permute-done.10.refs_11_
  24.2 1.5 %collective-permute-start.15 = (bf16[8,768]{1,0:T(8,128)(2,1)S(1)}, bf16[8,768]{1,0:T(8,128)(2,1)S(1)}, u32[]{:S(2)}, u32[]{:S(2)}) collective-permute-start(bf16[8,768]{1,0:T(8,128)(2,1)S(1)} %get-tuple-element.55), channel_id=1, source_target_pairs={{0,16},{1,17},{2,18},{3,19},{4,20},{5,21},{6,22},{7,23},{8,24},{9,... | collective-permute-start | bytes 36872 | tf_op jit(solution)/shard_map/ppermute | solution.py:181
  25.7 0.0 collective-permute-start.16
  25.8 0.0 collective-permute-done.12.refs_13_
  25.8 0.9 %collective-permute-start.17 = (bf16[8,768]{1,0:T(8,128)(2,1)S(1)}, bf16[8,768]{1,0:T(8,128)(2,1)S(1)}, u32[]{:S(2)}, u32[]{:S(2)}) collective-permute-start(bf16[8,768]{1,0:T(8,128)(2,1)S(1)} %get-tuple-element.57), channel_id=1, source_target_pairs={{0,18},{1,19},{2,16},{3,17},{4,22},{5,23},{6,20},{7,21},{8,26},{9,... | collective-permute-start | bytes 36872 | tf_op jit(solution)/shard_map/ppermute | solution.py:181
  26.7 0.0 collective-permute-done.13.refs_14_
  26.7 1.9 %collective-permute-start.18 = (bf16[8,768]{1,0:T(8,128)(2,1)S(1)}, bf16[8,768]{1,0:T(8,128)(2,1)S(1)}, u32[]{:S(2)}, u32[]{:S(2)}) collective-permute-start(bf16[8,768]{1,0:T(8,128)(2,1)S(1)} %get-tuple-element.58), channel_id=1, source_target_pairs={{0,19},{1,18},{2,17},{3,16},{4,23},{5,22},{6,21},{7,20},{8,27},{9,... | collective-permute-start | bytes 36872 | tf_op jit(solution)/shard_map/ppermute | solution.py:181
  28.6 0.9 %collective-permute-done.14.refs_15_ = bf16[8,768]{1,0:T(8,128)(2,1)S(1)} collective-permute-done((bf16[8,768]{1,0:T(8,128)(2,1)S(1)}, bf16[8,768]{1,0:T(8,128)(2,1)S(1)}, u32[]{:S(2)}, u32[]{:S(2)}) %collective-permute-start.14) | collective-permute-done | bytes 12320 | tf_op jit(solution)/shard_map/ppermute | solution.py:181
  29.5 1.0 %collective-permute-start.19 = (bf16[8,768]{1,0:T(8,128)(2,1)S(1)}, bf16[8,768]{1,0:T(8,128)(2,1)S(1)}, u32[]{:S(2)}, u32[]{:S(2)}) collective-permute-start(bf16[8,768]{1,0:T(8,128)(2,1)S(1)} %get-tuple-element.59), channel_id=1, source_target_pairs={{0,20},{1,21},{2,22},{3,23},{4,16},{5,17},{6,18},{7,19},{8,28},{9,... | collective-permute-start | bytes 36872 | tf_op jit(solution)/shard_map/ppermute | solution.py:181
  30.6 2.3 %collective-permute-start.20 = (bf16[8,768]{1,0:T(8,128)(2,1)S(1)}, bf16[8,768]{1,0:T(8,128)(2,1)S(1)}, u32[]{:S(2)}, u32[]{:S(2)}) collective-permute-start(bf16[8,768]{1,0:T(8,128)(2,1)S(1)} %get-tuple-element.60), channel_id=1, source_target_pairs={{0,21},{1,20},{2,23},{3,22},{4,17},{5,16},{6,19},{7,18},{8,29},{9,... | collective-permute-start | bytes 36872 | tf_op jit(solution)/shard_map/ppermute | solution.py:181
  32.9 0.0 collective-permute-done.16.refs_17_
  32.9 3.3 %collective-permute-start.21 = (bf16[8,768]{1,0:T(8,128)(2,1)S(1)}, bf16[8,768]{1,0:T(8,128)(2,1)S(1)}, u32[]{:S(2)}, u32[]{:S(2)}) collective-permute-start(bf16[8,768]{1,0:T(8,128)(2,1)S(1)} %get-tuple-element.61), channel_id=1, source_target_pairs={{0,22},{1,23},{2,20},{3,21},{4,18},{5,19},{6,16},{7,17},{8,30},{9,... | collective-permute-start | bytes 36872 | tf_op jit(solution)/shard_map/ppermute | solution.py:181
  36.2 0.0 collective-permute-done.17.refs_18_
  36.2 1.4 %collective-permute-start.22 = (bf16[8,768]{1,0:T(8,128)(2,1)S(1)}, bf16[8,768]{1,0:T(8,128)(2,1)S(1)}, u32[]{:S(2)}, u32[]{:S(2)}) collective-permute-start(bf16[8,768]{1,0:T(8,128)(2,1)S(1)} %get-tuple-element.62), channel_id=1, source_target_pairs={{0,23},{1,22},{2,21},{3,20},{4,19},{5,18},{6,17},{7,16},{8,31},{9,... | collective-permute-start | bytes 36872 | tf_op jit(solution)/shard_map/ppermute | solution.py:181
  37.5 1.6 %collective-permute-start.23 = (bf16[8,768]{1,0:T(8,128)(2,1)S(1)}, bf16[8,768]{1,0:T(8,128)(2,1)S(1)}, u32[]{:S(2)}, u32[]{:S(2)}) collective-permute-start(bf16[8,768]{1,0:T(8,128)(2,1)S(1)} %get-tuple-element.63), channel_id=1, source_target_pairs={{0,24},{1,25},{2,26},{3,27},{4,28},{5,29},{6,30},{7,31},{8,16},{9,... | collective-permute-start | bytes 36872 | tf_op jit(solution)/shard_map/ppermute | solution.py:181
  39.1 0.9 %collective-permute-start.24 = (bf16[8,768]{1,0:T(8,128)(2,1)S(1)}, bf16[8,768]{1,0:T(8,128)(2,1)S(1)}, u32[]{:S(2)}, u32[]{:S(2)}) collective-permute-start(bf16[8,768]{1,0:T(8,128)(2,1)S(1)} %get-tuple-element.64), channel_id=1, source_target_pairs={{0,25},{1,24},{2,27},{3,26},{4,29},{5,28},{6,31},{7,30},{8,17},{9,... | collective-permute-start | bytes 36872 | tf_op jit(solution)/shard_map/ppermute | solution.py:181
  40.0 3.8 %collective-permute-start.26 = (bf16[8,768]{1,0:T(8,128)(2,1)S(1)}, bf16[8,768]{1,0:T(8,128)(2,1)S(1)}, u32[]{:S(2)}, u32[]{:S(2)}) collective-permute-start(bf16[8,768]{1,0:T(8,128)(2,1)S(1)} %get-tuple-element.66), channel_id=1, source_target_pairs={{0,27},{1,26},{2,25},{3,24},{4,31},{5,30},{6,29},{7,28},{8,19},{9,... | collective-permute-start | bytes 36872 | tf_op jit(solution)/shard_map/ppermute | solution.py:181
  43.8 1.0 %collective-permute-start.27 = (bf16[8,768]{1,0:T(8,128)(2,1)S(1)}, bf16[8,768]{1,0:T(8,128)(2,1)S(1)}, u32[]{:S(2)}, u32[]{:S(2)}) collective-permute-start(bf16[8,768]{1,0:T(8,128)(2,1)S(1)} %get-tuple-element.67), channel_id=1, source_target_pairs={{0,28},{1,29},{2,30},{3,31},{4,24},{5,25},{6,26},{7,27},{8,20},{9,... | collective-permute-start | bytes 36872 | tf_op jit(solution)/shard_map/ppermute | solution.py:181
  44.8 3.2 %collective-permute-start.28 = (bf16[8,768]{1,0:T(8,128)(2,1)S(1)}, bf16[8,768]{1,0:T(8,128)(2,1)S(1)}, u32[]{:S(2)}, u32[]{:S(2)}) collective-permute-start(bf16[8,768]{1,0:T(8,128)(2,1)S(1)} %get-tuple-element.68), channel_id=1, source_target_pairs={{0,29},{1,28},{2,31},{3,30},{4,25},{5,24},{6,27},{7,26},{8,21},{9,... | collective-permute-start | bytes 36872 | tf_op jit(solution)/shard_map/ppermute | solution.py:181
  48.0 4.2 %collective-permute-start.29 = (bf16[8,768]{1,0:T(8,128)(2,1)S(1)}, bf16[8,768]{1,0:T(8,128)(2,1)S(1)}, u32[]{:S(2)}, u32[]{:S(2)}) collective-permute-start(bf16[8,768]{1,0:T(8,128)(2,1)S(1)} %get-tuple-element.69), channel_id=1, source_target_pairs={{0,30},{1,31},{2,28},{3,29},{4,26},{5,27},{6,24},{7,25},{8,22},{9,... | collective-permute-start | bytes 36872 | tf_op jit(solution)/shard_map/ppermute | solution.py:181
  52.2 1.3 %collective-permute-start.30 = (bf16[8,768]{1,0:T(8,128)(2,1)S(1)}, bf16[8,768]{1,0:T(8,128)(2,1)S(1)}, u32[]{:S(2)}, u32[]{:S(2)}) collective-permute-start(bf16[8,768]{1,0:T(8,128)(2,1)S(1)} %get-tuple-element.70), channel_id=1, source_target_pairs={{0,31},{1,30},{2,29},{3,28},{4,27},{5,26},{6,25},{7,24},{8,23},{9,... | collective-permute-start | bytes 36872 | tf_op jit(solution)/shard_map/ppermute | solution.py:181
  53.6 1.7 %collective-permute-done.29.refs_30_ = bf16[8,768]{1,0:T(8,128)(2,1)S(1)} collective-permute-done((bf16[8,768]{1,0:T(8,128)(2,1)S(1)}, bf16[8,768]{1,0:T(8,128)(2,1)S(1)}, u32[]{:S(2)}, u32[]{:S(2)}) %collective-permute-start.29) | collective-permute-done | bytes 12320 | tf_op jit(solution)/shard_map/ppermute | solution.py:181
  55.3 3.7 %collective-permute-done.30.refs_31_ = bf16[8,768]{1,0:T(8,128)(2,1)S(1)} collective-permute-done((bf16[8,768]{1,0:T(8,128)(2,1)S(1)}, bf16[8,768]{1,0:T(8,128)(2,1)S(1)}, u32[]{:S(2)}, u32[]{:S(2)}) %collective-permute-start.30) | collective-permute-done | bytes 12320 | tf_op jit(solution)/shard_map/ppermute | solution.py:181
  58.9 1.4 %shard_map.92 = bf16[8,16,128]{2,1,0:T(8,128)(2,1)} custom-call(bf16[1024,128]{1,0:T(8,128)(2,1)S(1)} %copy-done, f32[1,128]{1,0:T(1,128)S(1)} %get-tuple-element.38.bias_ref, bf16[8,768]{1,0:T(8,128)(2,1)S(1)} %get-tuple-element.39.refs_0_, bf16[8,768]{1,0:T(8,128)(2,1)S(1)} %collective-permute-done.refs_1_, ...), custom_call_target="tpu_custom_call" | custom-call | tf_op jit(solution)/shard_map/pallas_call | solution.py:187
  (18 shorter events, 0.0 us)
Async XLA Ops:
  0.0 58.9 %copy-start = (bf16[1024,128]{1,0:T(8,128)(2,1)S(1)}, bf16[1024,128]{1,0:T(8,128)(2,1)}, u32[]{:S(2)}) copy-start(bf16[1024,128]{1,0:T(8,128)(2,1)} %weight_ref.1) | copy-start | bytes 786436
  1.7 6.0 %collective-permute-start = (bf16[8,768]{1,0:T(8,128)(2,1)S(1)}, bf16[8,768]{1,0:T(8,128)(2,1)S(1)}, u32[]{:S(2)}, u32[]{:S(2)}) collective-permute-start(bf16[8,768]{1,0:T(8,128)(2,1)S(1)} %get-tuple-element.40), channel_id=1, source_target_pairs={{0,1},{1,0},{2,3},{3,2},{4,5},{5,4},{6,7},{7,6},{8,9},{9,8},{10,11... | collective-permute-start | bytes 36872 | tf_op jit(solution)/shard_map/ppermute | solution.py:181
  2.2 9.1 %collective-permute-start.1 = (bf16[8,768]{1,0:T(8,128)(2,1)S(1)}, bf16[8,768]{1,0:T(8,128)(2,1)S(1)}, u32[]{:S(2)}, u32[]{:S(2)}) collective-permute-start(bf16[8,768]{1,0:T(8,128)(2,1)S(1)} %get-tuple-element.41), channel_id=1, source_target_pairs={{0,2},{1,3},{2,0},{3,1},{4,6},{5,7},{6,4},{7,5},{8,10},{9,11},{10,... | collective-permute-start | bytes 36872 | tf_op jit(solution)/shard_map/ppermute | solution.py:181
  4.9 6.6 %collective-permute-start.2 = (bf16[8,768]{1,0:T(8,128)(2,1)S(1)}, bf16[8,768]{1,0:T(8,128)(2,1)S(1)}, u32[]{:S(2)}, u32[]{:S(2)}) collective-permute-start(bf16[8,768]{1,0:T(8,128)(2,1)S(1)} %get-tuple-element.42), channel_id=1, source_target_pairs={{0,3},{1,2},{2,1},{3,0},{4,7},{5,6},{6,5},{7,4},{8,11},{9,10},{10,... | collective-permute-start | bytes 36872 | tf_op jit(solution)/shard_map/ppermute | solution.py:181
  4.9 8.0 %collective-permute-start.3 = (bf16[8,768]{1,0:T(8,128)(2,1)S(1)}, bf16[8,768]{1,0:T(8,128)(2,1)S(1)}, u32[]{:S(2)}, u32[]{:S(2)}) collective-permute-start(bf16[8,768]{1,0:T(8,128)(2,1)S(1)} %get-tuple-element.43), channel_id=1, source_target_pairs={{0,4},{1,5},{2,6},{3,7},{4,0},{5,1},{6,2},{7,3},{8,12},{9,13},{10,... | collective-permute-start | bytes 36872 | tf_op jit(solution)/shard_map/ppermute | solution.py:181
  7.7 5.3 %collective-permute-start.4 = (bf16[8,768]{1,0:T(8,128)(2,1)S(1)}, bf16[8,768]{1,0:T(8,128)(2,1)S(1)}, u32[]{:S(2)}, u32[]{:S(2)}) collective-permute-start(bf16[8,768]{1,0:T(8,128)(2,1)S(1)} %get-tuple-element.44), channel_id=1, source_target_pairs={{0,5},{1,4},{2,7},{3,6},{4,1},{5,0},{6,3},{7,2},{8,13},{9,12},{10,... | collective-permute-start | bytes 36872 | tf_op jit(solution)/shard_map/ppermute | solution.py:181
  7.7 6.5 %collective-permute-start.5 = (bf16[8,768]{1,0:T(8,128)(2,1)S(1)}, bf16[8,768]{1,0:T(8,128)(2,1)S(1)}, u32[]{:S(2)}, u32[]{:S(2)}) collective-permute-start(bf16[8,768]{1,0:T(8,128)(2,1)S(1)} %get-tuple-element.45), channel_id=1, source_target_pairs={{0,6},{1,7},{2,4},{3,5},{4,2},{5,3},{6,0},{7,1},{8,14},{9,15},{10,... | collective-permute-start | bytes 36872 | tf_op jit(solution)/shard_map/ppermute | solution.py:181
  11.3 4.9 %collective-permute-start.6 = (bf16[8,768]{1,0:T(8,128)(2,1)S(1)}, bf16[8,768]{1,0:T(8,128)(2,1)S(1)}, u32[]{:S(2)}, u32[]{:S(2)}) collective-permute-start(bf16[8,768]{1,0:T(8,128)(2,1)S(1)} %get-tuple-element.46), channel_id=1, source_target_pairs={{0,7},{1,6},{2,5},{3,4},{4,3},{5,2},{6,1},{7,0},{8,15},{9,14},{10,... | collective-permute-start | bytes 36872 | tf_op jit(solution)/shard_map/ppermute | solution.py:181
  11.4 6.8 %collective-permute-start.7 = (bf16[8,768]{1,0:T(8,128)(2,1)S(1)}, bf16[8,768]{1,0:T(8,128)(2,1)S(1)}, u32[]{:S(2)}, u32[]{:S(2)}) collective-permute-start(bf16[8,768]{1,0:T(8,128)(2,1)S(1)} %get-tuple-element.47), channel_id=1, source_target_pairs={{0,8},{1,9},{2,10},{3,11},{4,12},{5,13},{6,14},{7,15},{8,0},{9,1},... | collective-permute-start | bytes 36872 | tf_op jit(solution)/shard_map/ppermute | solution.py:181
  12.9 6.6 %collective-permute-start.8 = (bf16[8,768]{1,0:T(8,128)(2,1)S(1)}, bf16[8,768]{1,0:T(8,128)(2,1)S(1)}, u32[]{:S(2)}, u32[]{:S(2)}) collective-permute-start(bf16[8,768]{1,0:T(8,128)(2,1)S(1)} %get-tuple-element.48), channel_id=1, source_target_pairs={{0,9},{1,8},{2,11},{3,10},{4,13},{5,12},{6,15},{7,14},{8,1},{9,0},... | collective-permute-start | bytes 36872 | tf_op jit(solution)/shard_map/ppermute | solution.py:181
  13.0 10.7 %collective-permute-start.9 = (bf16[8,768]{1,0:T(8,128)(2,1)S(1)}, bf16[8,768]{1,0:T(8,128)(2,1)S(1)}, u32[]{:S(2)}, u32[]{:S(2)}) collective-permute-start(bf16[8,768]{1,0:T(8,128)(2,1)S(1)} %get-tuple-element.49), channel_id=1, source_target_pairs={{0,10},{1,11},{2,8},{3,9},{4,14},{5,15},{6,12},{7,13},{8,2},{9,3},... | collective-permute-start | bytes 36872 | tf_op jit(solution)/shard_map/ppermute | solution.py:181
  14.2 10.0 %collective-permute-start.10 = (bf16[8,768]{1,0:T(8,128)(2,1)S(1)}, bf16[8,768]{1,0:T(8,128)(2,1)S(1)}, u32[]{:S(2)}, u32[]{:S(2)}) collective-permute-start(bf16[8,768]{1,0:T(8,128)(2,1)S(1)} %get-tuple-element.50), channel_id=1, source_target_pairs={{0,11},{1,10},{2,9},{3,8},{4,15},{5,14},{6,13},{7,12},{8,3},{9,2},... | collective-permute-start | bytes 36872 | tf_op jit(solution)/shard_map/ppermute | solution.py:181
  16.2 9.5 %collective-permute-start.11 = (bf16[8,768]{1,0:T(8,128)(2,1)S(1)}, bf16[8,768]{1,0:T(8,128)(2,1)S(1)}, u32[]{:S(2)}, u32[]{:S(2)}) collective-permute-start(bf16[8,768]{1,0:T(8,128)(2,1)S(1)} %get-tuple-element.51), channel_id=1, source_target_pairs={{0,12},{1,13},{2,14},{3,15},{4,8},{5,9},{6,10},{7,11},{8,4},{9,5},... | collective-permute-start | bytes 36872 | tf_op jit(solution)/shard_map/ppermute | solution.py:181
  18.2 7.6 %collective-permute-start.12 = (bf16[8,768]{1,0:T(8,128)(2,1)S(1)}, bf16[8,768]{1,0:T(8,128)(2,1)S(1)}, u32[]{:S(2)}, u32[]{:S(2)}) collective-permute-start(bf16[8,768]{1,0:T(8,128)(2,1)S(1)} %get-tuple-element.52), channel_id=1, source_target_pairs={{0,13},{1,12},{2,15},{3,14},{4,9},{5,8},{6,11},{7,10},{8,5},{9,4},... | collective-permute-start | bytes 36872 | tf_op jit(solution)/shard_map/ppermute | solution.py:181
  19.5 7.1 %collective-permute-start.13 = (bf16[8,768]{1,0:T(8,128)(2,1)S(1)}, bf16[8,768]{1,0:T(8,128)(2,1)S(1)}, u32[]{:S(2)}, u32[]{:S(2)}) collective-permute-start(bf16[8,768]{1,0:T(8,128)(2,1)S(1)} %get-tuple-element.53), channel_id=1, source_target_pairs={{0,14},{1,15},{2,12},{3,13},{4,10},{5,11},{6,8},{7,9},{8,6},{9,7},... | collective-permute-start | bytes 36872 | tf_op jit(solution)/shard_map/ppermute | solution.py:181
  23.7 5.8 %collective-permute-start.14 = (bf16[8,768]{1,0:T(8,128)(2,1)S(1)}, bf16[8,768]{1,0:T(8,128)(2,1)S(1)}, u32[]{:S(2)}, u32[]{:S(2)}) collective-permute-start(bf16[8,768]{1,0:T(8,128)(2,1)S(1)} %get-tuple-element.54), channel_id=1, source_target_pairs={{0,15},{1,14},{2,13},{3,12},{4,11},{5,10},{6,9},{7,8},{8,7},{9,6},... | collective-permute-start | bytes 36872 | tf_op jit(solution)/shard_map/ppermute | solution.py:181
  24.2 6.4 %collective-permute-start.15 = (bf16[8,768]{1,0:T(8,128)(2,1)S(1)}, bf16[8,768]{1,0:T(8,128)(2,1)S(1)}, u32[]{:S(2)}, u32[]{:S(2)}) collective-permute-start(bf16[8,768]{1,0:T(8,128)(2,1)S(1)} %get-tuple-element.55), channel_id=1, source_target_pairs={{0,16},{1,17},{2,18},{3,19},{4,20},{5,21},{6,22},{7,23},{8,24},{9,... | collective-permute-start | bytes 36872 | tf_op jit(solution)/shard_map/ppermute | solution.py:181
  25.7 7.1 %collective-permute-start.16 = (bf16[8,768]{1,0:T(8,128)(2,1)S(1)}, bf16[8,768]{1,0:T(8,128)(2,1)S(1)}, u32[]{:S(2)}, u32[]{:S(2)}) collective-permute-start(bf16[8,768]{1,0:T(8,128)(2,1)S(1)} %get-tuple-element.56), channel_id=1, source_target_pairs={{0,17},{1,16},{2,19},{3,18},{4,21},{5,20},{6,23},{7,22},{8,25},{9,... | collective-permute-start | bytes 36872 | tf_op jit(solution)/shard_map/ppermute | solution.py:181
  25.8 10.4 %collective-permute-start.17 = (bf16[8,768]{1,0:T(8,128)(2,1)S(1)}, bf16[8,768]{1,0:T(8,128)(2,1)S(1)}, u32[]{:S(2)}, u32[]{:S(2)}) collective-permute-start(bf16[8,768]{1,0:T(8,128)(2,1)S(1)} %get-tuple-element.57), channel_id=1, source_target_pairs={{0,18},{1,19},{2,16},{3,17},{4,22},{5,23},{6,20},{7,21},{8,26},{9,... | collective-permute-start | bytes 36872 | tf_op jit(solution)/shard_map/ppermute | solution.py:181
  26.7 10.9 %collective-permute-start.18 = (bf16[8,768]{1,0:T(8,128)(2,1)S(1)}, bf16[8,768]{1,0:T(8,128)(2,1)S(1)}, u32[]{:S(2)}, u32[]{:S(2)}) collective-permute-start(bf16[8,768]{1,0:T(8,128)(2,1)S(1)} %get-tuple-element.58), channel_id=1, source_target_pairs={{0,19},{1,18},{2,17},{3,16},{4,23},{5,22},{6,21},{7,20},{8,27},{9,... | collective-permute-start | bytes 36872 | tf_op jit(solution)/shard_map/ppermute | solution.py:181
  29.5 9.6 %collective-permute-start.19 = (bf16[8,768]{1,0:T(8,128)(2,1)S(1)}, bf16[8,768]{1,0:T(8,128)(2,1)S(1)}, u32[]{:S(2)}, u32[]{:S(2)}) collective-permute-start(bf16[8,768]{1,0:T(8,128)(2,1)S(1)} %get-tuple-element.59), channel_id=1, source_target_pairs={{0,20},{1,21},{2,22},{3,23},{4,16},{5,17},{6,18},{7,19},{8,28},{9,... | collective-permute-start | bytes 36872 | tf_op jit(solution)/shard_map/ppermute | solution.py:181
  30.6 9.4 %collective-permute-start.20 = (bf16[8,768]{1,0:T(8,128)(2,1)S(1)}, bf16[8,768]{1,0:T(8,128)(2,1)S(1)}, u32[]{:S(2)}, u32[]{:S(2)}) collective-permute-start(bf16[8,768]{1,0:T(8,128)(2,1)S(1)} %get-tuple-element.60), channel_id=1, source_target_pairs={{0,21},{1,20},{2,23},{3,22},{4,17},{5,16},{6,19},{7,18},{8,29},{9,... | collective-permute-start | bytes 36872 | tf_op jit(solution)/shard_map/ppermute | solution.py:181
  32.9 7.1 %collective-permute-start.21 = (bf16[8,768]{1,0:T(8,128)(2,1)S(1)}, bf16[8,768]{1,0:T(8,128)(2,1)S(1)}, u32[]{:S(2)}, u32[]{:S(2)}) collective-permute-start(bf16[8,768]{1,0:T(8,128)(2,1)S(1)} %get-tuple-element.61), channel_id=1, source_target_pairs={{0,22},{1,23},{2,20},{3,21},{4,18},{5,19},{6,16},{7,17},{8,30},{9,... | collective-permute-start | bytes 36872 | tf_op jit(solution)/shard_map/ppermute | solution.py:181
  36.2 7.6 %collective-permute-start.22 = (bf16[8,768]{1,0:T(8,128)(2,1)S(1)}, bf16[8,768]{1,0:T(8,128)(2,1)S(1)}, u32[]{:S(2)}, u32[]{:S(2)}) collective-permute-start(bf16[8,768]{1,0:T(8,128)(2,1)S(1)} %get-tuple-element.62), channel_id=1, source_target_pairs={{0,23},{1,22},{2,21},{3,20},{4,19},{5,18},{6,17},{7,16},{8,31},{9,... | collective-permute-start | bytes 36872 | tf_op jit(solution)/shard_map/ppermute | solution.py:181
  37.5 7.3 %collective-permute-start.23 = (bf16[8,768]{1,0:T(8,128)(2,1)S(1)}, bf16[8,768]{1,0:T(8,128)(2,1)S(1)}, u32[]{:S(2)}, u32[]{:S(2)}) collective-permute-start(bf16[8,768]{1,0:T(8,128)(2,1)S(1)} %get-tuple-element.63), channel_id=1, source_target_pairs={{0,24},{1,25},{2,26},{3,27},{4,28},{5,29},{6,30},{7,31},{8,16},{9,... | collective-permute-start | bytes 36872 | tf_op jit(solution)/shard_map/ppermute | solution.py:181
  39.1 8.9 %collective-permute-start.24 = (bf16[8,768]{1,0:T(8,128)(2,1)S(1)}, bf16[8,768]{1,0:T(8,128)(2,1)S(1)}, u32[]{:S(2)}, u32[]{:S(2)}) collective-permute-start(bf16[8,768]{1,0:T(8,128)(2,1)S(1)} %get-tuple-element.64), channel_id=1, source_target_pairs={{0,25},{1,24},{2,27},{3,26},{4,29},{5,28},{6,31},{7,30},{8,17},{9,... | collective-permute-start | bytes 36872 | tf_op jit(solution)/shard_map/ppermute | solution.py:181
  40.0 12.2 %collective-permute-start.25 = (bf16[8,768]{1,0:T(8,128)(2,1)S(1)}, bf16[8,768]{1,0:T(8,128)(2,1)S(1)}, u32[]{:S(2)}, u32[]{:S(2)}) collective-permute-start(bf16[8,768]{1,0:T(8,128)(2,1)S(1)} %get-tuple-element.65), channel_id=1, source_target_pairs={{0,26},{1,27},{2,24},{3,25},{4,30},{5,31},{6,28},{7,29},{8,18},{9,... | collective-permute-start | bytes 36872 | tf_op jit(solution)/shard_map/ppermute | solution.py:181
  40.0 13.6 %collective-permute-start.26 = (bf16[8,768]{1,0:T(8,128)(2,1)S(1)}, bf16[8,768]{1,0:T(8,128)(2,1)S(1)}, u32[]{:S(2)}, u32[]{:S(2)}) collective-permute-start(bf16[8,768]{1,0:T(8,128)(2,1)S(1)} %get-tuple-element.66), channel_id=1, source_target_pairs={{0,27},{1,26},{2,25},{3,24},{4,31},{5,30},{6,29},{7,28},{8,19},{9,... | collective-permute-start | bytes 36872 | tf_op jit(solution)/shard_map/ppermute | solution.py:181
  43.8 9.8 %collective-permute-start.27 = (bf16[8,768]{1,0:T(8,128)(2,1)S(1)}, bf16[8,768]{1,0:T(8,128)(2,1)S(1)}, u32[]{:S(2)}, u32[]{:S(2)}) collective-permute-start(bf16[8,768]{1,0:T(8,128)(2,1)S(1)} %get-tuple-element.67), channel_id=1, source_target_pairs={{0,28},{1,29},{2,30},{3,31},{4,24},{5,25},{6,26},{7,27},{8,20},{9,... | collective-permute-start | bytes 36872 | tf_op jit(solution)/shard_map/ppermute | solution.py:181
  44.8 8.8 %collective-permute-start.28 = (bf16[8,768]{1,0:T(8,128)(2,1)S(1)}, bf16[8,768]{1,0:T(8,128)(2,1)S(1)}, u32[]{:S(2)}, u32[]{:S(2)}) collective-permute-start(bf16[8,768]{1,0:T(8,128)(2,1)S(1)} %get-tuple-element.68), channel_id=1, source_target_pairs={{0,29},{1,28},{2,31},{3,30},{4,25},{5,24},{6,27},{7,26},{8,21},{9,... | collective-permute-start | bytes 36872 | tf_op jit(solution)/shard_map/ppermute | solution.py:181
  48.0 7.3 %collective-permute-start.29 = (bf16[8,768]{1,0:T(8,128)(2,1)S(1)}, bf16[8,768]{1,0:T(8,128)(2,1)S(1)}, u32[]{:S(2)}, u32[]{:S(2)}) collective-permute-start(bf16[8,768]{1,0:T(8,128)(2,1)S(1)} %get-tuple-element.69), channel_id=1, source_target_pairs={{0,30},{1,31},{2,28},{3,29},{4,26},{5,27},{6,24},{7,25},{8,22},{9,... | collective-permute-start | bytes 36872 | tf_op jit(solution)/shard_map/ppermute | solution.py:181
  52.2 6.7 %collective-permute-start.30 = (bf16[8,768]{1,0:T(8,128)(2,1)S(1)}, bf16[8,768]{1,0:T(8,128)(2,1)S(1)}, u32[]{:S(2)}, u32[]{:S(2)}) collective-permute-start(bf16[8,768]{1,0:T(8,128)(2,1)S(1)} %get-tuple-element.70), channel_id=1, source_target_pairs={{0,31},{1,30},{2,29},{3,28},{4,27},{5,26},{6,25},{7,24},{8,23},{9,... | collective-permute-start | bytes 36872 | tf_op jit(solution)/shard_map/ppermute | solution.py:181

commit v4 on v2

v4 whole, which is shorter than its diff:
```python
import functools

import jax
import jax.numpy as jnp
from jax import lax
from jax.experimental import pallas as pl
from jax.experimental.pallas import tpu as pltpu
from jax.sharding import Mesh
from jax.sharding import PartitionSpec as P

LANES = 128


def project_kernel(
    seq_count,
    half_count,
    rest_count,
    align_hbm,
    gain_hbm,
    offset_hbm,
    left_w_hbm,
    left_b_hbm,
    right_w_hbm,
    right_b_hbm,
    out_b_hbm,
    send_ref,
    out_b_ref,
    align_ref,
    gain_ref,
    offset_ref,
    left_w_ref,
    left_b_ref,
    right_w_ref,
    right_b_ref,
    proj_ref,
    sems,
):
    copies = [
        pltpu.make_async_copy(source, target, sems.at[n])
        for n, (source, target) in enumerate(
            [
                (align_hbm, align_ref),
                (gain_hbm, gain_ref),
                (offset_hbm, offset_ref),
                (left_w_hbm, left_w_ref),
                (left_b_hbm, left_b_ref),
                (right_w_hbm, right_w_ref),
                (right_b_hbm, right_b_ref),
                (out_b_hbm, out_b_ref),
            ]
        )
    ]
    for copy in copies:
        copy.start()
    for copy in copies:
        copy.wait()
    rows, res_total, chan = align_ref.shape
    hidden = left_w_ref.shape[0]
    values = align_ref[...].astype(jnp.float32).reshape(rows * res_total, chan)
    centred = values - jnp.mean(values, axis=-1, keepdims=True)
    spread = jnp.mean(centred * centred, axis=-1, keepdims=True)
    normed = centred * lax.rsqrt(spread + 1e-05) * gain_ref[...] + offset_ref[...]
    weights = jnp.concatenate([left_w_ref[...], right_w_ref[...]], axis=0)
    biases = jnp.concatenate([left_b_ref[...], right_b_ref[...]], axis=1)
    proj_ref[:, : 2 * hidden] = (
        lax.dot_general(
            normed.astype(jnp.bfloat16),
            weights,
            (((1,), (1,)), ((), ())),
            preferred_element_type=jnp.float32,
        )
        + biases
    )
    tiles = [proj_ref[pl.ds(r, rows, stride=res_total), :][:, : 2 * hidden] for r in range(res_total)]
    row_block = res_total // (half_count * rest_count)
    col_block = res_total // seq_count
    left = [
        jnp.concatenate([t[:, :hidden] for t in tiles[a * row_block : (a + 1) * row_block]], axis=1)
        for a in range(half_count * rest_count)
    ]
    right = [
        jnp.concatenate([t[:, hidden:] for t in tiles[b * col_block : (b + 1) * col_block]], axis=1)
        for b in range(seq_count)
    ]
    pieces = [
        jnp.concatenate([left[h * rest_count + a] for h in range(half_count)] + [right[b]], axis=1)
        for b in range(seq_count)
        for a in range(rest_count)
    ]
    group = max(1, 16 // rows)
    for start in range(0, len(pieces), group):
        block = jnp.concatenate(pieces[start : start + group], axis=0)
        send_ref[pl.ds(start * rows, group * rows), :] = block.astype(jnp.bfloat16)


def pair_kernel(
    hidden, row_block, col_block, recv_ref, weight_ref, mine_ref, theirs_ref, outer_ref, term_ref
):
    seq_total = 2 * recv_ref.shape[0]
    left = recv_ref[:, : 2 * row_block * hidden]
    right = recv_ref[:, 2 * row_block * hidden :]
    outer = lax.dot_general(
        left, right, (((0,), (0,)), ((), ())), preferred_element_type=jnp.float32
    )
    for g in range(outer_ref.shape[0]):
        outer_ref[g] = outer[:, g * LANES : (g + 1) * LANES]
    per_group = LANES // hidden
    terms = []
    for h in range(2):
        for g in range(outer_ref.shape[0]):
            slabs = [
                outer_ref[g, pl.ds(h * row_block * hidden + c, row_block, stride=hidden), :]
                for c in range(hidden)
            ]
            for j in range(per_group):
                flat = jnp.concatenate([s[:, j * hidden : (j + 1) * hidden] for s in slabs], axis=1)
                terms.append(flat)
    flat = jnp.concatenate(terms, axis=0).astype(jnp.bfloat16)
    term = jnp.dot(flat, weight_ref[...], preferred_element_type=jnp.float32)
    term = term * (1.0 / float(seq_total))
    pairs = row_block * col_block
    term_ref[0] = term[:pairs]
    term_ref[1] = term[pairs:]
    half = lax.axis_index("half")
    mine_ref[...] = term_ref[half]
    theirs_ref[...] = term_ref[1 - half].astype(jnp.bfloat16)


def add_kernel(mine_ref, came_ref, bias_ref, out_ref, term_ref):
    row_block, col_block, _ = out_ref.shape
    term_ref[...] = mine_ref[...] + came_ref[...].astype(jnp.float32) + bias_ref[...]
    for i in range(row_block):
        out_ref[i] = term_ref[pl.ds(i, col_block, stride=row_block), :].astype(jnp.bfloat16)


def in_hbm(array):
    return pltpu.with_memory_space_constraint(array, pltpu.HBM)


def body(
    alignment,
    layer_norm_gain,
    layer_norm_bias,
    left_projection_weight,
    left_bias,
    right_projection_weight,
    right_bias,
    out_weight,
    out_bias,
):
    seq_count = lax.axis_size("seq")
    half_count = lax.axis_size("half")
    rest_count = lax.axis_size("rest")
    rows, res_total, chan = alignment.shape
    hidden = left_projection_weight.shape[1]
    pair_width = out_weight.shape[1]
    row_block = res_total // (half_count * rest_count)
    col_block = res_total // seq_count
    peers = seq_count * rest_count
    width = (half_count * row_block + col_block) * hidden
    pairs = row_block * col_block
    vmem = pl.BlockSpec(memory_space=pltpu.VMEM)
    hbm = pl.BlockSpec(memory_space=pltpu.HBM)
    params = pltpu.CompilerParams(vmem_limit_bytes=32 * 1024 * 1024)
    send, bias_row = pl.pallas_call(
        functools.partial(project_kernel, seq_count, half_count, rest_count),
        out_shape=[
            jax.ShapeDtypeStruct((peers * rows, width), jnp.bfloat16),
            jax.ShapeDtypeStruct((1, pair_width), jnp.float32),
        ],
        in_specs=[hbm] * 8,
        out_specs=[vmem] * 2,
        scratch_shapes=[
            pltpu.VMEM((rows, res_total, chan), jnp.bfloat16),
            pltpu.VMEM((1, chan), jnp.float32),
            pltpu.VMEM((1, chan), jnp.float32),
            pltpu.VMEM((hidden, chan), jnp.bfloat16),
            pltpu.VMEM((1, hidden), jnp.float32),
            pltpu.VMEM((hidden, chan), jnp.bfloat16),
            pltpu.VMEM((1, hidden), jnp.float32),
            pltpu.VMEM((rows * res_total, LANES), jnp.float32),
            pltpu.SemaphoreType.DMA((8,)),
        ],
        compiler_params=params,
    )(
        in_hbm(alignment),
        in_hbm(layer_norm_gain.reshape(1, chan)),
        in_hbm(layer_norm_bias.reshape(1, chan)),
        in_hbm(left_projection_weight.T),
        in_hbm(left_bias.reshape(1, hidden)),
        in_hbm(right_projection_weight.T),
        in_hbm(right_bias.reshape(1, hidden)),
        in_hbm(out_bias.reshape(1, pair_width)),
    )
    recv = lax.all_to_all(send, ("seq", "rest"), split_axis=0, concat_axis=0, tiled=True)
    mine, theirs = pl.pallas_call(
        functools.partial(pair_kernel, hidden, row_block, col_block),
        out_shape=[
            jax.ShapeDtypeStruct((pairs, pair_width), jnp.float32),
            jax.ShapeDtypeStruct((pairs, pair_width), jnp.bfloat16),
        ],
        in_specs=[vmem] * 2,
        out_specs=[vmem] * 2,
        scratch_shapes=[
            pltpu.VMEM((col_block * hidden // LANES, 2 * row_block * hidden, LANES), jnp.float32),
            pltpu.VMEM((2, pairs, pair_width), jnp.float32),
        ],
        compiler_params=params,
    )(recv, out_weight)
    came = lax.ppermute(theirs, "half", [(0, 1), (1, 0)])
    return pl.pallas_call(
        add_kernel,
        out_shape=jax.ShapeDtypeStruct((row_block, col_block, pair_width), jnp.bfloat16),
        in_specs=[vmem] * 3,
        out_specs=vmem,
        scratch_shapes=[pltpu.VMEM((pairs, pair_width), jnp.float32)],
        compiler_params=params,
    )(mine, came, bias_row)


def solution(mesh):
    seq_count, res_count = mesh.devices.shape
    split = Mesh(mesh.devices.reshape(seq_count, 2, res_count // 2), ("seq", "half", "rest"))
    in_specs = (P(("seq", "half", "rest"), None, None), P(), P(), P(), P(), P(), P(), P(), P())
    out_specs = P(("half", "rest"), "seq", None)
    return jax.shard_map(body, mesh=split, in_specs=in_specs, out_specs=out_specs, check_vma=False)
```

time: 24.3 us -> 22.4 us (0.922)
  blocking collectives: 20.6 us -> 14 us
  starting transfers between devices: 0 us -> 2.65 us
  waiting for transfers between devices: 0 us -> 2.22 us
    all_to_all x1, blocking collectives: 20.6 us -> 14 us  [body(): lax.all_to_all(send, ('seq', 'rest'), split_axis=0, concat_axis=0, tiled=...]
    ppermute x0 -> x1, starting transfers between devices: none -> 2.65 us  [body(): came = lax.ppermute(theirs, 'half', [(0, 1), (1, 0)])]
    ppermute x0 -> x1, waiting for transfers between devices: none -> 2.22 us  [body(): came = lax.ppermute(theirs, 'half', [(0, 1), (1, 0)])]
    pallas_call x1, Pallas kernels: 1.87 us -> 1.13 us  [body(): pl.pallas_call(functools.partial(pair_kernel, hidden, row_block, col_bloc...]
    pallas_call x1 -> x2, Pallas kernels: 1.6 us -> 2.25 us  [the longest x1 1.61 us: body(): pl.pallas_call(functools.partial(project_kernel, seq_count, half_count, r...]
  transfers between devices with their start and end apart: 0 -> 1, of which waited for: 0 -> 1; matrix products, arithmetic and copies ran while one was open for 0% -> 0% of each run, Pallas kernels for 0% -> 0%
where the time goes in v4:
time: 22.4 us; the launch traced here: 22.2 us
  blocking collectives  14 us (63%)
  Pallas kernels  3.38 us (15%)
  starting transfers between devices  2.65 us (12%)
  waiting for transfers between devices  2.22 us (10%)
    all_to_all x1, blocking collectives, body(): lax.all_to_all(send, ('seq', 'rest'), split_axis=0, concat_axis=0, tiled=...  14 us
    ppermute x1, starting transfers between devices, body(): came = lax.ppermute(theirs, 'half', [(0, 1), (1, 0)])  2.65 us
    ppermute x1, waiting for transfers between devices, body(): came = lax.ppermute(theirs, 'half', [(0, 1), (1, 0)])  2.22 us
    pallas_call x1, Pallas kernels, body(): pl.pallas_call(functools.partial(project_kernel, seq_count, half_count, r...  1.61 us
    pallas_call x1, Pallas kernels, body(): pl.pallas_call(functools.partial(pair_kernel, hidden, row_block, col_bloc...  1.13 us
    pallas_call x1, Pallas kernels, body(): pl.pallas_call(add_kernel, out_shape=jax.ShapeDtypeStruct((row_block, col...  0.64 us
  transfers between devices with their start and end apart: 1, of which 1 were waited for; matrix products, arithmetic and copies ran while one was open for 0% of the time, Pallas kernels for 0%

profile of v4, /device:TPU:0, one launch (start us, length us, event | category | flops | bytes accessed | tf_op | source)
XLA Modules:
  0.0 22.2 jit_solution(17906743856989895967)
XLA Ops:
  0.0 1.6 %shard_map.91 = (bf16[128,1024]{1,0:T(8,128)(2,1)S(1)}, f32[1,128]{1,0:T(1,128)S(1)}) custom-call(bf16[8,64,256]{2,1,0:T(8,128)(2,1)} %align_hbm.1, f32[1,256]{1,0:T(1,128)} %bitcast.13, f32[1,256]{1,0:T(1,128)} %bitcast.14, bf16[32,256]{1,0:T(8,128)(2,1)} %bitcast.11, f32[1,32]{1,0:T(1,128)} %bitcast.15, bf16[32,256]{1,0:T(8,128)(2,1)} %bitcast.12, ...), custom_call_target="tpu_custom_call" | custom-call | tf_op jit(solution)/shard_map/pallas_call | solution.py:165
  1.6 0.0 copy-start
  1.6 14.0 %all_to_all.11 = bf16[16,8,1024]{2,1,0:T(8,128)(2,1)S(1)} all-to-all(bf16[16,8,1024]{2,1,0:T(8,128)(2,1)S(1)} %bitcast.10), channel_id=1, replica_groups=mesh['seq'=4,'half'=2,'rest'=4] {'seq','rest'}, dimensions={0} | all-to-all | bytes 524288 | tf_op jit(solution)/shard_map/all_to_all | solution.py:195
  15.6 0.0 copy-done
  15.6 1.1 %shard_map.92 = (f32[128,128]{1,0:T(8,128)S(1)}, bf16[128,128]{1,0:T(8,128)(2,1)S(1)}) custom-call(bf16[128,1024]{1,0:T(8,128)(2,1)S(1)} %bitcast.9, bf16[1024,128]{1,0:T(8,128)(2,1)S(1)} %copy-done), custom_call_target="tpu_custom_call" | custom-call | tf_op jit(solution)/shard_map/pallas_call | solution.py:196
  16.7 2.7 %collective-permute-start = (bf16[128,128]{1,0:T(8,128)(2,1)S(1)}, bf16[128,128]{1,0:T(8,128)(2,1)S(1)}, u32[]{:S(2)}, u32[]{:S(2)}) collective-permute-start(bf16[128,128]{1,0:T(8,128)(2,1)S(1)} %get-tuple-element.11), channel_id=1, source_target_pairs={{0,4},{4,0},{1,5},{5,1},{2,6},{6,2},{3,7},{7,3},{8,12},{12,8},{9,1... | collective-permute-start | bytes 98312 | tf_op jit(solution)/shard_map/ppermute | solution.py:210
  19.4 2.2 %collective-permute-done.came_ref = bf16[128,128]{1,0:T(8,128)(2,1)S(1)} collective-permute-done((bf16[128,128]{1,0:T(8,128)(2,1)S(1)}, bf16[128,128]{1,0:T(8,128)(2,1)S(1)}, u32[]{:S(2)}, u32[]{:S(2)}) %collective-permute-start) | collective-permute-done | bytes 32800 | tf_op jit(solution)/shard_map/ppermute | solution.py:210
  21.6 0.6 %shard_map.93 = bf16[8,16,128]{2,1,0:T(8,128)(2,1)} custom-call(f32[128,128]{1,0:T(8,128)S(1)} %get-tuple-element.10.mine_ref, bf16[128,128]{1,0:T(8,128)(2,1)S(1)} %collective-permute-done.came_ref, f32[1,128]{1,0:T(1,128)S(1)} %get-tuple-element.12.bias_ref), custom_call_target="tpu_custom_call" | custom-call | tf_op jit(solution)/shard_map/pallas_call | solution.py:211
Async XLA Ops:
  1.6 14.0 %copy-start = (bf16[1024,128]{1,0:T(8,128)(2,1)S(1)}, bf16[1024,128]{1,0:T(8,128)(2,1)}, u32[]{:S(2)}) copy-start(bf16[1024,128]{1,0:T(8,128)(2,1)} %weight_ref.1) | copy-start | bytes 786436
  16.7 4.9 %collective-permute-start = (bf16[128,128]{1,0:T(8,128)(2,1)S(1)}, bf16[128,128]{1,0:T(8,128)(2,1)S(1)}, u32[]{:S(2)}, u32[]{:S(2)}) collective-permute-start(bf16[128,128]{1,0:T(8,128)(2,1)S(1)} %get-tuple-element.11), channel_id=1, source_target_pairs={{0,4},{4,0},{1,5},{5,1},{2,6},{6,2},{3,7},{7,3},{8,12},{12,8},{9,1... | collective-permute-start | bytes 98312 | tf_op jit(solution)/shard_map/ppermute | solution.py:210

commit v5 on v4

--- a/solution.py
+++ b/solution.py
@@ -13,7 +13,7 @@
 
 def project_kernel(
     seq_count,
-    half_count,
+    core_count,
     rest_count,
     align_hbm,
     gain_hbm,
@@ -72,18 +72,18 @@
         + biases
     )
     tiles = [proj_ref[pl.ds(r, rows, stride=res_total), :][:, : 2 * hidden] for r in range(res_total)]
-    row_block = res_total // (half_count * rest_count)
+    row_block = res_total // (core_count * rest_count)
     col_block = res_total // seq_count
     left = [
         jnp.concatenate([t[:, :hidden] for t in tiles[a * row_block : (a + 1) * row_block]], axis=1)
-        for a in range(half_count * rest_count)
+        for a in range(core_count * rest_count)
     ]
     right = [
         jnp.concatenate([t[:, hidden:] for t in tiles[b * col_block : (b + 1) * col_block]], axis=1)
         for b in range(seq_count)
     ]
     pieces = [
-        jnp.concatenate([left[h * rest_count + a] for h in range(half_count)] + [right[b]], axis=1)
+        jnp.concatenate([left[a * core_count + k] for k in range(core_count)] + [right[b]], axis=1)
         for b in range(seq_count)
         for a in range(rest_count)
     ]
@@ -93,12 +93,13 @@
         send_ref[pl.ds(start * rows, group * rows), :] = block.astype(jnp.bfloat16)
 
 
-def pair_kernel(
-    hidden, row_block, col_block, recv_ref, weight_ref, mine_ref, theirs_ref, outer_ref, term_ref
-):
+def pair_kernel(own, hidden, row_block, col_block, recv_ref, weight_ref, out_ref, outer_ref):
+    core = lax.axis_index("core")
     seq_total = 2 * recv_ref.shape[0]
-    left = recv_ref[:, : 2 * row_block * hidden]
-    right = recv_ref[:, 2 * row_block * hidden :]
+    split = row_block * hidden
+    start = pl.multiple_of((core if own else 1 - core) * split, split)
+    left = recv_ref[:, pl.ds(start, split)]
+    right = recv_ref[:, 2 * split :]
     outer = lax.dot_general(
         left, right, (((0,), (0,)), ((), ())), preferred_element_type=jnp.float32
     )
@@ -106,24 +107,14 @@
         outer_ref[g] = outer[:, g * LANES : (g + 1) * LANES]
     per_group = LANES // hidden
     terms = []
-    for h in range(2):
-        for g in range(outer_ref.shape[0]):
-            slabs = [
-                outer_ref[g, pl.ds(h * row_block * hidden + c, row_block, stride=hidden), :]
-                for c in range(hidden)
-            ]
-            for j in range(per_group):
-                flat = jnp.concatenate([s[:, j * hidden : (j + 1) * hidden] for s in slabs], axis=1)
-                terms.append(flat)
+    for g in range(outer_ref.shape[0]):
+        slabs = [outer_ref[g, pl.ds(c, row_block, stride=hidden), :] for c in range(hidden)]
+        for j in range(per_group):
+            flat = jnp.concatenate([s[:, j * hidden : (j + 1) * hidden] for s in slabs], axis=1)
+            terms.append(flat)
     flat = jnp.concatenate(terms, axis=0).astype(jnp.bfloat16)
     term = jnp.dot(flat, weight_ref[...], preferred_element_type=jnp.float32)
-    term = term * (1.0 / float(seq_total))
-    pairs = row_block * col_block
-    term_ref[0] = term[:pairs]
-    term_ref[1] = term[pairs:]
-    half = lax.axis_index("half")
-    mine_ref[...] = term_ref[half]
-    theirs_ref[...] = term_ref[1 - half].astype(jnp.bfloat16)
+    out_ref[...] = (term * (1.0 / float(seq_total))).astype(out_ref.dtype)
 
 
 def add_kernel(mine_ref, came_ref, bias_ref, out_ref, term_ref):
@@ -149,21 +140,21 @@
     out_bias,
 ):
     seq_count = lax.axis_size("seq")
-    half_count = lax.axis_size("half")
+    core_count = lax.axis_size("core")
     rest_count = lax.axis_size("rest")
     rows, res_total, chan = alignment.shape
     hidden = left_projection_weight.shape[1]
     pair_width = out_weight.shape[1]
-    row_block = res_total // (half_count * rest_count)
+    row_block = res_total // (core_count * rest_count)
     col_block = res_total // seq_count
     peers = seq_count * rest_count
-    width = (half_count * row_block + col_block) * hidden
+    width = (core_count * row_block + col_block) * hidden
     pairs = row_block * col_block
     vmem = pl.BlockSpec(memory_space=pltpu.VMEM)
     hbm = pl.BlockSpec(memory_space=pltpu.HBM)
     params = pltpu.CompilerParams(vmem_limit_bytes=32 * 1024 * 1024)
     send, bias_row = pl.pallas_call(
-        functools.partial(project_kernel, seq_count, half_count, rest_count),
+        functools.partial(project_kernel, seq_count, core_count, rest_count),
         out_shape=[
             jax.ShapeDtypeStruct((peers * rows, width), jnp.bfloat16),
             jax.ShapeDtypeStruct((1, pair_width), jnp.float32),
@@ -193,21 +184,28 @@
         in_hbm(out_bias.reshape(1, pair_width)),
     )
     recv = lax.all_to_all(send, ("seq", "rest"), split_axis=0, concat_axis=0, tiled=True)
-    mine, theirs = pl.pallas_call(
-        functools.partial(pair_kernel, hidden, row_block, col_block),
-        out_shape=[
-            jax.ShapeDtypeStruct((pairs, pair_width), jnp.float32),
-            jax.ShapeDtypeStruct((pairs, pair_width), jnp.bfloat16),
-        ],
-        in_specs=[vmem] * 2,
-        out_specs=[vmem] * 2,
-        scratch_shapes=[
-            pltpu.VMEM((col_block * hidden // LANES, 2 * row_block * hidden, LANES), jnp.float32),
-            pltpu.VMEM((2, pairs, pair_width), jnp.float32),
-        ],
-        compiler_params=params,
-    )(recv, out_weight)
-    came = lax.ppermute(theirs, "half", [(0, 1), (1, 0)])
+    outer_values = pairs * hidden * hidden
+
+    def pair_block(own, dtype):
+        return pl.pallas_call(
+            functools.partial(pair_kernel, own, hidden, row_block, col_block),
+            out_shape=jax.ShapeDtypeStruct((pairs, pair_width), dtype),
+            in_specs=[vmem] * 2,
+            out_specs=vmem,
+            scratch_shapes=[
+                pltpu.VMEM((col_block * hidden // LANES, row_block * hidden, LANES), jnp.float32)
+            ],
+            compiler_params=params,
+            cost_estimate=pl.CostEstimate(
+                flops=2 * outer_values * (recv.shape[0] + pair_width),
+                bytes_accessed=2 * (recv.size + out_weight.size),
+                transcendentals=0,
+            ),
+        )(recv, out_weight)
+
+    theirs = pair_block(False, jnp.bfloat16)
+    came = lax.ppermute(theirs, "core", [(0, 1), (1, 0)])
+    mine = pair_block(True, jnp.float32)
     return pl.pallas_call(
         add_kernel,
         out_shape=jax.ShapeDtypeStruct((row_block, col_block, pair_width), jnp.bfloat16),
@@ -220,7 +218,7 @@
 
 def solution(mesh):
     seq_count, res_count = mesh.devices.shape
-    split = Mesh(mesh.devices.reshape(seq_count, 2, res_count // 2), ("seq", "half", "rest"))
-    in_specs = (P(("seq", "half", "rest"), None, None), P(), P(), P(), P(), P(), P(), P(), P())
-    out_specs = P(("half", "rest"), "seq", None)
+    split = Mesh(mesh.devices.reshape(seq_count, res_count // 2, 2), ("seq", "rest", "core"))
+    in_specs = (P(("seq", "rest", "core"), None, None), P(), P(), P(), P(), P(), P(), P(), P())
+    out_specs = P(("rest", "core"), "seq", None)
     return jax.shard_map(body, mesh=split, in_specs=in_specs, out_specs=out_specs, check_vma=False)

time: 22.4 us -> 23.3 us (1.040)
  blocking collectives: 14 us -> 18.8 us
  starting transfers between devices: 2.65 us -> 0.07 us
  waiting for transfers between devices: 2.22 us -> 0.43 us
  Pallas kernels: 3.38 us -> 3.76 us
    all_to_all x1, blocking collectives: 14 us -> 18.8 us  [body(): lax.all_to_all(send, ('seq', 'rest'), split_axis=0, concat_axis=0, tiled=...]
    ppermute x1, starting transfers between devices: 2.65 us -> 0.07 us  [body(): came = lax.ppermute(theirs, 'core', [(0, 1), (1, 0)])]
    ppermute x1, waiting for transfers between devices: 2.22 us -> 0.43 us  [body(): came = lax.ppermute(theirs, 'core', [(0, 1), (1, 0)])]
    pallas_call x2 -> x3, Pallas kernels: 2.74 us -> 3.12 us  [the longest x1 1.61 us: body(): pl.pallas_call(functools.partial(project_kernel, seq_count, core_count, r...]
  transfers between devices with their start and end apart: 1 -> 1, of which waited for: 1 -> 1; matrix products, arithmetic and copies ran while one was open for 0% -> 0% of each run, Pallas kernels for 0% -> 3%
where the time goes in v5:
time: 23.3 us; the launch traced here: 23.1 us
  blocking collectives  18.8 us (81%)
  Pallas kernels  3.76 us (16%)
  waiting for transfers between devices  0.43 us (2%)
    all_to_all x1, blocking collectives, body(): lax.all_to_all(send, ('seq', 'rest'), split_axis=0, concat_axis=0, tiled=...  18.8 us
    pallas_call x1, Pallas kernels, body(): pl.pallas_call(functools.partial(project_kernel, seq_count, core_count, r...  1.61 us
    pallas_call x2, Pallas kernels, pair_block(): pl.pallas_call(functools.partial(pair_kernel, own, hidden, row_block, col...  1.51 us
    pallas_call x1, Pallas kernels, body(): pl.pallas_call(add_kernel, out_shape=jax.ShapeDtypeStruct((row_block, col...  0.64 us
  transfers between devices with their start and end apart: 1, of which 1 were waited for; matrix products, arithmetic and copies ran while one was open for 0% of the time, Pallas kernels for 3%

profile of v5, /device:TPU:0, one launch (start us, length us, event | category | flops | bytes accessed | tf_op | source)
XLA Modules:
  0.0 23.1 jit_solution(11036178748310041538)
XLA Ops:
  0.0 1.6 %shard_map.91 = (bf16[128,1024]{1,0:T(8,128)(2,1)S(1)}, f32[1,128]{1,0:T(1,128)S(1)}) custom-call(bf16[8,64,256]{2,1,0:T(8,128)(2,1)} %align_hbm.1, f32[1,256]{1,0:T(1,128)} %bitcast.14, f32[1,256]{1,0:T(1,128)} %bitcast.15, bf16[32,256]{1,0:T(8,128)(2,1)} %bitcast.12, f32[1,32]{1,0:T(1,128)} %bitcast.16, bf16[32,256]{1,0:T(8,128)(2,1)} %bitcast.13, ...), custom_call_target="tpu_custom_call" | custom-call | tf_op jit(solution)/shard_map/pallas_call | solution.py:156
  1.6 0.0 copy-start
  1.6 18.8 %all_to_all.11 = bf16[16,8,1024]{2,1,0:T(8,128)(2,1)S(1)} all-to-all(bf16[16,8,1024]{2,1,0:T(8,128)(2,1)S(1)} %bitcast.11), channel_id=1, replica_groups=mesh['seq'=4,'rest'=4,'core'=2] {'seq','rest'}, dimensions={0} | all-to-all | bytes 524288 | tf_op jit(solution)/shard_map/all_to_all | solution.py:186
  20.4 0.0 copy-done
  20.4 0.8 %shard_map.93 = bf16[128,128]{1,0:T(8,128)(2,1)S(1)} custom-call(bf16[128,1024]{1,0:T(8,128)(2,1)S(1)} %bitcast.9, bf16[1024,128]{1,0:T(8,128)(2,1)S(1)} %copy-done), custom_call_target="tpu_custom_call" | custom-call | flops 67108864 | bytes 524288 | tf_op jit(solution)/shard_map/pallas_call | solution.py:190
  21.2 0.1 collective-permute-start
  21.3 0.8 %shard_map.92.mine_ref = f32[128,128]{1,0:T(8,128)S(1)} custom-call(bf16[128,1024]{1,0:T(8,128)(2,1)S(1)} %bitcast.10, bf16[1024,128]{1,0:T(8,128)(2,1)S(1)} %copy-done), custom_call_target="tpu_custom_call" | custom-call | flops 67108864 | bytes 524288 | tf_op jit(solution)/shard_map/pallas_call | solution.py:190
  22.1 0.4 %collective-permute-done.came_ref = bf16[128,128]{1,0:T(8,128)(2,1)S(1)} collective-permute-done((bf16[128,128]{1,0:T(8,128)(2,1)S(1)}, bf16[128,128]{1,0:T(8,128)(2,1)S(1)}, u32[]{:S(2)}, u32[]{:S(2)}) %collective-permute-start) | collective-permute-done | bytes 32800 | tf_op jit(solution)/shard_map/ppermute | solution.py:207
  22.5 0.6 %shard_map.94 = bf16[8,16,128]{2,1,0:T(8,128)(2,1)} custom-call(f32[128,128]{1,0:T(8,128)S(1)} %shard_map.92.mine_ref, bf16[128,128]{1,0:T(8,128)(2,1)S(1)} %collective-permute-done.came_ref, f32[1,128]{1,0:T(1,128)S(1)} %get-tuple-element.8.bias_ref), custom_call_target="tpu_custom_call" | custom-call | tf_op jit(solution)/shard_map/pallas_call | solution.py:209
Async XLA Ops:
  1.6 18.8 %copy-start = (bf16[1024,128]{1,0:T(8,128)(2,1)S(1)}, bf16[1024,128]{1,0:T(8,128)(2,1)}, u32[]{:S(2)}) copy-start(bf16[1024,128]{1,0:T(8,128)(2,1)} %weight_ref.3) | copy-start | bytes 786436
  21.2 1.3 %collective-permute-start = (bf16[128,128]{1,0:T(8,128)(2,1)S(1)}, bf16[128,128]{1,0:T(8,128)(2,1)S(1)}, u32[]{:S(2)}, u32[]{:S(2)}) collective-permute-start(bf16[128,128]{1,0:T(8,128)(2,1)S(1)} %shard_map.93), channel_id=1, source_target_pairs={{0,1},{1,0},{2,3},{3,2},{4,5},{5,4},{6,7},{7,6},{8,9},{9,8},{10,11... | collective-permute-start | bytes 98312 | tf_op jit(solution)/shard_map/ppermute | solution.py:207

commit v6 on v5

--- a/solution.py
+++ b/solution.py
@@ -11,9 +11,14 @@
 LANES = 128
 
 
+def mirror(at, rest_count):
+    pair = 2 - rest_count % 2
+    return (rest_count // pair - 1 - at // pair) * pair + at % pair
+
+
 def project_kernel(
     seq_count,
-    core_count,
+    half_count,
     rest_count,
     align_hbm,
     gain_hbm,
@@ -33,6 +38,7 @@
     right_w_ref,
     right_b_ref,
     proj_ref,
+    left_ref,
     sems,
 ):
     copies = [
@@ -72,18 +78,21 @@
         + biases
     )
     tiles = [proj_ref[pl.ds(r, rows, stride=res_total), :][:, : 2 * hidden] for r in range(res_total)]
-    row_block = res_total // (core_count * rest_count)
+    row_block = res_total // (half_count * rest_count)
     col_block = res_total // seq_count
-    left = [
-        jnp.concatenate([t[:, :hidden] for t in tiles[a * row_block : (a + 1) * row_block]], axis=1)
-        for a in range(core_count * rest_count)
-    ]
+    for a in range(half_count * rest_count):
+        left_ref[a] = jnp.concatenate(
+            [t[:, :hidden] for t in tiles[a * row_block : (a + 1) * row_block]], axis=1
+        )
     right = [
         jnp.concatenate([t[:, hidden:] for t in tiles[b * col_block : (b + 1) * col_block]], axis=1)
         for b in range(seq_count)
     ]
+    half = lax.axis_index("half")
+    own = [left_ref[half * rest_count + a] for a in range(rest_count)]
+    other = [left_ref[(1 - half) * rest_count + mirror(a, rest_count)] for a in range(rest_count)]
     pieces = [
-        jnp.concatenate([left[a * core_count + k] for k in range(core_count)] + [right[b]], axis=1)
+        jnp.concatenate([own[a], other[a], right[b]], axis=1)
         for b in range(seq_count)
         for a in range(rest_count)
     ]
@@ -94,11 +103,9 @@
 
 
 def pair_kernel(own, hidden, row_block, col_block, recv_ref, weight_ref, out_ref, outer_ref):
-    core = lax.axis_index("core")
     seq_total = 2 * recv_ref.shape[0]
     split = row_block * hidden
-    start = pl.multiple_of((core if own else 1 - core) * split, split)
-    left = recv_ref[:, pl.ds(start, split)]
+    left = recv_ref[:, :split] if own else recv_ref[:, split : 2 * split]
     right = recv_ref[:, 2 * split :]
     outer = lax.dot_general(
         left, right, (((0,), (0,)), ((), ())), preferred_element_type=jnp.float32
@@ -140,21 +147,21 @@
     out_bias,
 ):
     seq_count = lax.axis_size("seq")
-    core_count = lax.axis_size("core")
+    half_count = lax.axis_size("half")
     rest_count = lax.axis_size("rest")
     rows, res_total, chan = alignment.shape
     hidden = left_projection_weight.shape[1]
     pair_width = out_weight.shape[1]
-    row_block = res_total // (core_count * rest_count)
+    row_block = res_total // (half_count * rest_count)
     col_block = res_total // seq_count
     peers = seq_count * rest_count
-    width = (core_count * row_block + col_block) * hidden
+    width = (half_count * row_block + col_block) * hidden
     pairs = row_block * col_block
     vmem = pl.BlockSpec(memory_space=pltpu.VMEM)
     hbm = pl.BlockSpec(memory_space=pltpu.HBM)
     params = pltpu.CompilerParams(vmem_limit_bytes=32 * 1024 * 1024)
     send, bias_row = pl.pallas_call(
-        functools.partial(project_kernel, seq_count, core_count, rest_count),
+        functools.partial(project_kernel, seq_count, half_count, rest_count),
         out_shape=[
             jax.ShapeDtypeStruct((peers * rows, width), jnp.bfloat16),
             jax.ShapeDtypeStruct((1, pair_width), jnp.float32),
@@ -170,6 +177,7 @@
             pltpu.VMEM((hidden, chan), jnp.bfloat16),
             pltpu.VMEM((1, hidden), jnp.float32),
             pltpu.VMEM((rows * res_total, LANES), jnp.float32),
+            pltpu.VMEM((half_count * rest_count, rows, row_block * hidden), jnp.float32),
             pltpu.SemaphoreType.DMA((8,)),
         ],
         compiler_params=params,
@@ -204,7 +212,12 @@
         )(recv, out_weight)
 
     theirs = pair_block(False, jnp.bfloat16)
-    came = lax.ppermute(theirs, "core", [(0, 1), (1, 0)])
+    swap = [
+        (h * rest_count + q, (1 - h) * rest_count + mirror(q, rest_count))
+        for h in range(half_count)
+        for q in range(rest_count)
+    ]
+    came = lax.ppermute(theirs, ("half", "rest"), swap)
     mine = pair_block(True, jnp.float32)
     return pl.pallas_call(
         add_kernel,
@@ -218,7 +231,7 @@
 
 def solution(mesh):
     seq_count, res_count = mesh.devices.shape
-    split = Mesh(mesh.devices.reshape(seq_count, res_count // 2, 2), ("seq", "rest", "core"))
-    in_specs = (P(("seq", "rest", "core"), None, None), P(), P(), P(), P(), P(), P(), P(), P())
-    out_specs = P(("rest", "core"), "seq", None)
+    split = Mesh(mesh.devices.reshape(seq_count, 2, res_count // 2), ("seq", "half", "rest"))
+    in_specs = (P(("seq", "half", "rest"), None, None), P(), P(), P(), P(), P(), P(), P(), P())
+    out_specs = P(("half", "rest"), "seq", None)
     return jax.shard_map(body, mesh=split, in_specs=in_specs, out_specs=out_specs, check_vma=False)

time: 23.3 us -> 22.9 us (0.983)
  blocking collectives: 18.8 us -> 14 us
  waiting for transfers between devices: 0.43 us -> 3.33 us
  starting transfers between devices: 0.07 us -> 1.69 us
    all_to_all x1, blocking collectives: 18.8 us -> 14 us  [body(): lax.all_to_all(send, ('seq', 'rest'), split_axis=0, concat_axis=0, tiled=...]
    ppermute x1, waiting for transfers between devices: 0.43 us -> 3.33 us  [body(): came = lax.ppermute(theirs, ('half', 'rest'), swap)]
    ppermute x1, starting transfers between devices: 0.07 us -> 1.69 us  [body(): came = lax.ppermute(theirs, ('half', 'rest'), swap)]
where the time goes in v6:
time: 22.9 us; the launch traced here: 22.8 us
  blocking collectives  14 us (61%)
  Pallas kernels  3.75 us (16%)
  waiting for transfers between devices  3.33 us (15%)
  starting transfers between devices  1.69 us (7%)
    all_to_all x1, blocking collectives, body(): lax.all_to_all(send, ('seq', 'rest'), split_axis=0, concat_axis=0, tiled=...  14 us
    ppermute x1, waiting for transfers between devices, body(): came = lax.ppermute(theirs, ('half', 'rest'), swap)  3.33 us
    ppermute x1, starting transfers between devices, body(): came = lax.ppermute(theirs, ('half', 'rest'), swap)  1.69 us
    pallas_call x1, Pallas kernels, body(): pl.pallas_call(functools.partial(project_kernel, seq_count, half_count, r...  1.62 us
    pallas_call x2, Pallas kernels, pair_block(): pl.pallas_call(functools.partial(pair_kernel, own, hidden, row_block, col...  1.49 us
    pallas_call x1, Pallas kernels, body(): pl.pallas_call(add_kernel, out_shape=jax.ShapeDtypeStruct((row_block, col...  0.64 us
  transfers between devices with their start and end apart: 1, of which 1 were waited for; matrix products, arithmetic and copies ran while one was open for 0% of the time, Pallas kernels for 3%

profile of v6, /device:TPU:0, one launch (start us, length us, event | category | flops | bytes accessed | tf_op | source)
XLA Modules:
  0.0 22.8 jit_solution(1286328816596764685)
XLA Ops:
  0.0 1.6 %shard_map.91 = (bf16[128,1024]{1,0:T(8,128)(2,1)S(1)}, f32[1,128]{1,0:T(1,128)S(1)}) custom-call(bf16[8,64,256]{2,1,0:T(8,128)(2,1)} %align_hbm.1, f32[1,256]{1,0:T(1,128)} %bitcast.14, f32[1,256]{1,0:T(1,128)} %bitcast.15, bf16[32,256]{1,0:T(8,128)(2,1)} %bitcast.12, f32[1,32]{1,0:T(1,128)} %bitcast.16, bf16[32,256]{1,0:T(8,128)(2,1)} %bitcast.13, ...), custom_call_target="tpu_custom_call" | custom-call | tf_op jit(solution)/shard_map/pallas_call | solution.py:163
  1.6 0.0 copy-start
  1.6 14.0 %all_to_all.11 = bf16[16,8,1024]{2,1,0:T(8,128)(2,1)S(1)} all-to-all(bf16[16,8,1024]{2,1,0:T(8,128)(2,1)S(1)} %bitcast.11), channel_id=1, replica_groups=mesh['seq'=4,'half'=2,'rest'=4] {'seq','rest'}, dimensions={0} | all-to-all | bytes 524288 | tf_op jit(solution)/shard_map/all_to_all | solution.py:194
  15.6 0.0 copy-done
  15.6 0.7 %shard_map.93 = bf16[128,128]{1,0:T(8,128)(2,1)S(1)} custom-call(bf16[128,1024]{1,0:T(8,128)(2,1)S(1)} %bitcast.9, bf16[1024,128]{1,0:T(8,128)(2,1)S(1)} %copy-done), custom_call_target="tpu_custom_call" | custom-call | flops 67108864 | bytes 524288 | tf_op jit(solution)/shard_map/pallas_call | solution.py:198
  16.4 1.7 %collective-permute-start = (bf16[128,128]{1,0:T(8,128)(2,1)S(1)}, bf16[128,128]{1,0:T(8,128)(2,1)S(1)}, u32[]{:S(2)}, u32[]{:S(2)}) collective-permute-start(bf16[128,128]{1,0:T(8,128)(2,1)S(1)} %shard_map.93), channel_id=1, source_target_pairs={{0,6},{1,7},{2,4},{3,5},{4,2},{5,3},{6,0},{7,1},{8,14},{9,15},{10,... | collective-permute-start | bytes 98312 | tf_op jit(solution)/shard_map/ppermute | solution.py:220
  18.0 0.7 %shard_map.92.mine_ref = f32[128,128]{1,0:T(8,128)S(1)} custom-call(bf16[128,1024]{1,0:T(8,128)(2,1)S(1)} %bitcast.10, bf16[1024,128]{1,0:T(8,128)(2,1)S(1)} %copy-done), custom_call_target="tpu_custom_call" | custom-call | flops 67108864 | bytes 524288 | tf_op jit(solution)/shard_map/pallas_call | solution.py:198
  18.8 3.3 %collective-permute-done.came_ref = bf16[128,128]{1,0:T(8,128)(2,1)S(1)} collective-permute-done((bf16[128,128]{1,0:T(8,128)(2,1)S(1)}, bf16[128,128]{1,0:T(8,128)(2,1)S(1)}, u32[]{:S(2)}, u32[]{:S(2)}) %collective-permute-start) | collective-permute-done | bytes 32800 | tf_op jit(solution)/shard_map/ppermute | solution.py:220
  22.1 0.6 %shard_map.94 = bf16[8,16,128]{2,1,0:T(8,128)(2,1)} custom-call(f32[128,128]{1,0:T(8,128)S(1)} %shard_map.92.mine_ref, bf16[128,128]{1,0:T(8,128)(2,1)S(1)} %collective-permute-done.came_ref, f32[1,128]{1,0:T(1,128)S(1)} %get-tuple-element.8.bias_ref), custom_call_target="tpu_custom_call" | custom-call | tf_op jit(solution)/shard_map/pallas_call | solution.py:222
Async XLA Ops:
  1.6 14.0 %copy-start = (bf16[1024,128]{1,0:T(8,128)(2,1)S(1)}, bf16[1024,128]{1,0:T(8,128)(2,1)}, u32[]{:S(2)}) copy-start(bf16[1024,128]{1,0:T(8,128)(2,1)} %weight_ref.3) | copy-start | bytes 786436
  16.4 5.8 %collective-permute-start = (bf16[128,128]{1,0:T(8,128)(2,1)S(1)}, bf16[128,128]{1,0:T(8,128)(2,1)S(1)}, u32[]{:S(2)}, u32[]{:S(2)}) collective-permute-start(bf16[128,128]{1,0:T(8,128)(2,1)S(1)} %shard_map.93), channel_id=1, source_target_pairs={{0,6},{1,7},{2,4},{3,5},{4,2},{5,3},{6,0},{7,1},{8,14},{9,15},{10,... | collective-permute-start | bytes 98312 | tf_op jit(solution)/shard_map/ppermute | solution.py:220

commit v7 on v6

--- a/solution.py
+++ b/solution.py
@@ -11,9 +11,10 @@
 LANES = 128
 
 
-def mirror(at, rest_count):
-    pair = 2 - rest_count % 2
-    return (rest_count // pair - 1 - at // pair) * pair + at % pair
+def partner(rest_count):
+    ring = list(range(1, rest_count, 2)) + list(range(0, rest_count, 2))[::-1]
+    step = dict(zip(ring, ring[1:] + ring[:1]))
+    return [step[at] for at in range(rest_count)]
 
 
 def project_kernel(
@@ -41,42 +42,49 @@
     left_ref,
     sems,
 ):
-    copies = [
-        pltpu.make_async_copy(source, target, sems.at[n])
+    rows, res_total, chan = align_ref.shape
+    hidden = left_w_ref.shape[0]
+    step = max(1, rows // 4)
+    cuts = [pl.ds(at, step) for at in range(0, rows, step)]
+    small = [
+        pltpu.make_async_copy(source, target, sems.at[len(cuts) + n])
         for n, (source, target) in enumerate(
             [
-                (align_hbm, align_ref),
+                (left_w_hbm, left_w_ref),
+                (right_w_hbm, right_w_ref),
                 (gain_hbm, gain_ref),
                 (offset_hbm, offset_ref),
-                (left_w_hbm, left_w_ref),
                 (left_b_hbm, left_b_ref),
-                (right_w_hbm, right_w_ref),
                 (right_b_hbm, right_b_ref),
                 (out_b_hbm, out_b_ref),
             ]
         )
     ]
-    for copy in copies:
+    large = [
+        pltpu.make_async_copy(align_hbm.at[cut], align_ref.at[cut], sems.at[n])
+        for n, cut in enumerate(cuts)
+    ]
+    for copy in large[:1] + small + large[1:]:
         copy.start()
-    for copy in copies:
+    for copy in small:
         copy.wait()
-    rows, res_total, chan = align_ref.shape
-    hidden = left_w_ref.shape[0]
-    values = align_ref[...].astype(jnp.float32).reshape(rows * res_total, chan)
-    centred = values - jnp.mean(values, axis=-1, keepdims=True)
-    spread = jnp.mean(centred * centred, axis=-1, keepdims=True)
-    normed = centred * lax.rsqrt(spread + 1e-05) * gain_ref[...] + offset_ref[...]
     weights = jnp.concatenate([left_w_ref[...], right_w_ref[...]], axis=0)
     biases = jnp.concatenate([left_b_ref[...], right_b_ref[...]], axis=1)
-    proj_ref[:, : 2 * hidden] = (
-        lax.dot_general(
-            normed.astype(jnp.bfloat16),
-            weights,
-            (((1,), (1,)), ((), ())),
-            preferred_element_type=jnp.float32,
+    for n, cut in enumerate(cuts):
+        large[n].wait()
+        values = align_ref[cut].astype(jnp.float32).reshape(step * res_total, chan)
+        centred = values - jnp.mean(values, axis=-1, keepdims=True)
+        spread = jnp.mean(centred * centred, axis=-1, keepdims=True)
+        normed = centred * lax.rsqrt(spread + 1e-05) * gain_ref[...] + offset_ref[...]
+        proj_ref[pl.ds(n * step * res_total, step * res_total), : 2 * hidden] = (
+            lax.dot_general(
+                normed.astype(jnp.bfloat16),
+                weights,
+                (((1,), (1,)), ((), ())),
+                preferred_element_type=jnp.float32,
+            )
+            + biases
         )
-        + biases
-    )
     tiles = [proj_ref[pl.ds(r, rows, stride=res_total), :][:, : 2 * hidden] for r in range(res_total)]
     row_block = res_total // (half_count * rest_count)
     col_block = res_total // seq_count
@@ -90,7 +98,10 @@
     ]
     half = lax.axis_index("half")
     own = [left_ref[half * rest_count + a] for a in range(rest_count)]
-    other = [left_ref[(1 - half) * rest_count + mirror(a, rest_count)] for a in range(rest_count)]
+    up = partner(rest_count)
+    other = [
+        left_ref[jnp.where(half == 0, rest_count + up[a], up.index(a))] for a in range(rest_count)
+    ]
     pieces = [
         jnp.concatenate([own[a], other[a], right[b]], axis=1)
         for b in range(seq_count)
@@ -178,7 +189,7 @@
             pltpu.VMEM((1, hidden), jnp.float32),
             pltpu.VMEM((rows * res_total, LANES), jnp.float32),
             pltpu.VMEM((half_count * rest_count, rows, row_block * hidden), jnp.float32),
-            pltpu.SemaphoreType.DMA((8,)),
+            pltpu.SemaphoreType.DMA((7 + rows // max(1, rows // 4),)),
         ],
         compiler_params=params,
     )(
@@ -212,11 +223,8 @@
         )(recv, out_weight)
 
     theirs = pair_block(False, jnp.bfloat16)
-    swap = [
-        (h * rest_count + q, (1 - h) * rest_count + mirror(q, rest_count))
-        for h in range(half_count)
-        for q in range(rest_count)
-    ]
+    across = [(low, rest_count + high) for low, high in enumerate(partner(rest_count))]
+    swap = across + [(high, low) for low, high in across]
     came = lax.ppermute(theirs, ("half", "rest"), swap)
     mine = pair_block(True, jnp.float32)
     return pl.pallas_call(

time: 22.9 us -> 23 us (level)
  Pallas kernels: 3.75 us -> 4.56 us
  waiting for transfers between devices: 3.33 us -> 2.62 us
    pallas_call x1, Pallas kernels: 1.62 us -> 2.42 us  [body(): pl.pallas_call(functools.partial(project_kernel, seq_count, half_count, r...]
    ppermute x1, waiting for transfers between devices: 3.33 us -> 2.62 us  [body(): came = lax.ppermute(theirs, ('half', 'rest'), swap)]
where the time goes in v7:
time: 23 us; the launch traced here: 22.8 us
  blocking collectives  14 us (61%)
  Pallas kernels  4.56 us (20%)
  waiting for transfers between devices  2.62 us (11%)
  starting transfers between devices  1.61 us (7%)
    all_to_all x1, blocking collectives, body(): lax.all_to_all(send, ('seq', 'rest'), split_axis=0, concat_axis=0, tiled=...  14 us
    ppermute x1, waiting for transfers between devices, body(): came = lax.ppermute(theirs, ('half', 'rest'), swap)  2.62 us
    pallas_call x1, Pallas kernels, body(): pl.pallas_call(functools.partial(project_kernel, seq_count, half_count, r...  2.42 us
    ppermute x1, starting transfers between devices, body(): came = lax.ppermute(theirs, ('half', 'rest'), swap)  1.61 us
    pallas_call x2, Pallas kernels, pair_block(): pl.pallas_call(functools.partial(pair_kernel, own, hidden, row_block, col...  1.5 us
    pallas_call x1, Pallas kernels, body(): pl.pallas_call(add_kernel, out_shape=jax.ShapeDtypeStruct((row_block, col...  0.64 us
  transfers between devices with their start and end apart: 1, of which 1 were waited for; matrix products, arithmetic and copies ran while one was open for 0% of the time, Pallas kernels for 3%

profile of v7, /device:TPU:0, one launch (start us, length us, event | category | flops | bytes accessed | tf_op | source)
XLA Modules:
  0.0 22.8 jit_solution(14077554703006377685)
XLA Ops:
  0.0 2.4 %shard_map.91 = (bf16[128,1024]{1,0:T(8,128)(2,1)S(1)}, f32[1,128]{1,0:T(1,128)S(1)}) custom-call(bf16[8,64,256]{2,1,0:T(8,128)(2,1)} %align_hbm.1, f32[1,256]{1,0:T(1,128)} %bitcast.14, f32[1,256]{1,0:T(1,128)} %bitcast.15, bf16[32,256]{1,0:T(8,128)(2,1)} %bitcast.12, f32[1,32]{1,0:T(1,128)} %bitcast.16, bf16[32,256]{1,0:T(8,128)(2,1)} %bitcast.13, ...), custom_call_target="tpu_custom_call" | custom-call | tf_op jit(solution)/shard_map/pallas_call | solution.py:174
  2.4 0.0 copy-start
  2.4 14.0 %all_to_all.11 = bf16[16,8,1024]{2,1,0:T(8,128)(2,1)S(1)} all-to-all(bf16[16,8,1024]{2,1,0:T(8,128)(2,1)S(1)} %bitcast.11), channel_id=1, replica_groups=mesh['seq'=4,'half'=2,'rest'=4] {'seq','rest'}, dimensions={0} | all-to-all | bytes 524288 | tf_op jit(solution)/shard_map/all_to_all | solution.py:205
  16.4 0.0 copy-done
  16.4 0.7 %shard_map.93 = bf16[128,128]{1,0:T(8,128)(2,1)S(1)} custom-call(bf16[128,1024]{1,0:T(8,128)(2,1)S(1)} %bitcast.9, bf16[1024,128]{1,0:T(8,128)(2,1)S(1)} %copy-done), custom_call_target="tpu_custom_call" | custom-call | flops 67108864 | bytes 524288 | tf_op jit(solution)/shard_map/pallas_call | solution.py:209
  17.2 1.6 %collective-permute-start = (bf16[128,128]{1,0:T(8,128)(2,1)S(1)}, bf16[128,128]{1,0:T(8,128)(2,1)S(1)}, u32[]{:S(2)}, u32[]{:S(2)}) collective-permute-start(bf16[128,128]{1,0:T(8,128)(2,1)S(1)} %shard_map.93), channel_id=1, source_target_pairs={{0,5},{1,7},{2,4},{3,6},{5,0},{7,1},{4,2},{6,3},{8,13},{9,15},{10,... | collective-permute-start | bytes 98312 | tf_op jit(solution)/shard_map/ppermute | solution.py:228
  18.8 0.7 %shard_map.92.mine_ref = f32[128,128]{1,0:T(8,128)S(1)} custom-call(bf16[128,1024]{1,0:T(8,128)(2,1)S(1)} %bitcast.10, bf16[1024,128]{1,0:T(8,128)(2,1)S(1)} %copy-done), custom_call_target="tpu_custom_call" | custom-call | flops 67108864 | bytes 524288 | tf_op jit(solution)/shard_map/pallas_call | solution.py:209
  19.5 2.6 %collective-permute-done.came_ref = bf16[128,128]{1,0:T(8,128)(2,1)S(1)} collective-permute-done((bf16[128,128]{1,0:T(8,128)(2,1)S(1)}, bf16[128,128]{1,0:T(8,128)(2,1)S(1)}, u32[]{:S(2)}, u32[]{:S(2)}) %collective-permute-start) | collective-permute-done | bytes 32800 | tf_op jit(solution)/shard_map/ppermute | solution.py:228
  22.1 0.6 %shard_map.94 = bf16[8,16,128]{2,1,0:T(8,128)(2,1)} custom-call(f32[128,128]{1,0:T(8,128)S(1)} %shard_map.92.mine_ref, bf16[128,128]{1,0:T(8,128)(2,1)S(1)} %collective-permute-done.came_ref, f32[1,128]{1,0:T(1,128)S(1)} %get-tuple-element.8.bias_ref), custom_call_target="tpu_custom_call" | custom-call | tf_op jit(solution)/shard_map/pallas_call | solution.py:230
Async XLA Ops:
  2.4 14.0 %copy-start = (bf16[1024,128]{1,0:T(8,128)(2,1)S(1)}, bf16[1024,128]{1,0:T(8,128)(2,1)}, u32[]{:S(2)}) copy-start(bf16[1024,128]{1,0:T(8,128)(2,1)} %weight_ref.3) | copy-start | bytes 786436
  17.2 5.0 %collective-permute-start = (bf16[128,128]{1,0:T(8,128)(2,1)S(1)}, bf16[128,128]{1,0:T(8,128)(2,1)S(1)}, u32[]{:S(2)}, u32[]{:S(2)}) collective-permute-start(bf16[128,128]{1,0:T(8,128)(2,1)S(1)} %shard_map.93), channel_id=1, source_target_pairs={{0,5},{1,7},{2,4},{3,6},{5,0},{7,1},{4,2},{6,3},{8,13},{9,15},{10,... | collective-permute-start | bytes 98312 | tf_op jit(solution)/shard_map/ppermute | solution.py:228

commit v8 on v6

--- a/solution.py
+++ b/solution.py
@@ -11,9 +11,8 @@
 LANES = 128
 
 
-def mirror(at, rest_count):
-    pair = 2 - rest_count % 2
-    return (rest_count // pair - 1 - at // pair) * pair + at % pair
+def peer_order(seq_count, rest_count):
+    return [(b, a) for b in range(seq_count) for a in range(rest_count)][::-1]
 
 
 def project_kernel(
@@ -90,11 +89,10 @@
     ]
     half = lax.axis_index("half")
     own = [left_ref[half * rest_count + a] for a in range(rest_count)]
-    other = [left_ref[(1 - half) * rest_count + mirror(a, rest_count)] for a in range(rest_count)]
+    other = [left_ref[(1 - half) * rest_count + a] for a in range(rest_count)]
     pieces = [
         jnp.concatenate([own[a], other[a], right[b]], axis=1)
-        for b in range(seq_count)
-        for a in range(rest_count)
+        for b, a in peer_order(seq_count, rest_count)
     ]
     group = max(1, 16 // rows)
     for start in range(0, len(pieces), group):
@@ -191,7 +189,18 @@
         in_hbm(right_bias.reshape(1, hidden)),
         in_hbm(out_bias.reshape(1, pair_width)),
     )
-    recv = lax.all_to_all(send, ("seq", "rest"), split_axis=0, concat_axis=0, tiled=True)
+    groups = [
+        [(b * half_count + h) * rest_count + a for b, a in peer_order(seq_count, rest_count)]
+        for h in range(half_count)
+    ]
+    recv = lax.all_to_all(
+        send,
+        ("seq", "half", "rest"),
+        split_axis=0,
+        concat_axis=0,
+        tiled=True,
+        axis_index_groups=groups,
+    )
     outer_values = pairs * hidden * hidden
 
     def pair_block(own, dtype):
@@ -212,12 +221,7 @@
         )(recv, out_weight)
 
     theirs = pair_block(False, jnp.bfloat16)
-    swap = [
-        (h * rest_count + q, (1 - h) * rest_count + mirror(q, rest_count))
-        for h in range(half_count)
-        for q in range(rest_count)
-    ]
-    came = lax.ppermute(theirs, ("half", "rest"), swap)
+    came = lax.ppermute(theirs, "half", [(0, 1), (1, 0)])
     mine = pair_block(True, jnp.float32)
     return pl.pallas_call(
         add_kernel,

time: 22.9 us -> 19.8 us (0.86)
  blocking collectives: 14 us -> 11.5 us
  waiting for transfers between devices: 3.33 us -> 1.7 us
  starting transfers between devices: 1.69 us -> 2.66 us
    all_to_all x1, blocking collectives: 14 us -> 11.5 us  [body(): lax.all_to_all(send, ('seq', 'half', 'rest'), split_axis=0, concat_axis=0...]
    ppermute x1, waiting for transfers between devices: 3.33 us -> 1.7 us  [body(): came = lax.ppermute(theirs, 'half', [(0, 1), (1, 0)])]
    ppermute x1, starting transfers between devices: 1.69 us -> 2.66 us  [body(): came = lax.ppermute(theirs, 'half', [(0, 1), (1, 0)])]
  transfers between devices with their start and end apart: 1 -> 1, of which waited for: 1 -> 1; matrix products, arithmetic and copies ran while one was open for 0% -> 0% of each run, Pallas kernels for 3% -> 4%
where the time goes in v8:
time: 19.8 us; the launch traced here: 19.7 us
  blocking collectives  11.5 us (58%)
  Pallas kernels  3.75 us (19%)
  starting transfers between devices  2.66 us (13%)
  waiting for transfers between devices  1.7 us (9%)
    all_to_all x1, blocking collectives, body(): lax.all_to_all(send, ('seq', 'half', 'rest'), split_axis=0, concat_axis=0...  11.5 us
    ppermute x1, starting transfers between devices, body(): came = lax.ppermute(theirs, 'half', [(0, 1), (1, 0)])  2.66 us
    ppermute x1, waiting for transfers between devices, body(): came = lax.ppermute(theirs, 'half', [(0, 1), (1, 0)])  1.7 us
    pallas_call x1, Pallas kernels, body(): pl.pallas_call(functools.partial(project_kernel, seq_count, half_count, r...  1.62 us
    pallas_call x2, Pallas kernels, pair_block(): pl.pallas_call(functools.partial(pair_kernel, own, hidden, row_block, col...  1.49 us
    pallas_call x1, Pallas kernels, body(): pl.pallas_call(add_kernel, out_shape=jax.ShapeDtypeStruct((row_block, col...  0.64 us
  transfers between devices with their start and end apart: 1, of which 1 were waited for; matrix products, arithmetic and copies ran while one was open for 0% of the time, Pallas kernels for 4%

profile of v8, /device:TPU:0, one launch (start us, length us, event | category | flops | bytes accessed | tf_op | source)
XLA Modules:
  0.0 19.7 jit_solution(13502663369033854257)
XLA Ops:
  0.0 1.6 %shard_map.91 = (bf16[128,1024]{1,0:T(8,128)(2,1)S(1)}, f32[1,128]{1,0:T(1,128)S(1)}) custom-call(bf16[8,64,256]{2,1,0:T(8,128)(2,1)} %align_hbm.1, f32[1,256]{1,0:T(1,128)} %bitcast.14, f32[1,256]{1,0:T(1,128)} %bitcast.15, bf16[32,256]{1,0:T(8,128)(2,1)} %bitcast.12, f32[1,32]{1,0:T(1,128)} %bitcast.16, bf16[32,256]{1,0:T(8,128)(2,1)} %bitcast.13, ...), custom_call_target="tpu_custom_call" | custom-call | tf_op jit(solution)/shard_map/pallas_call | solution.py:161
  1.6 0.0 copy-start
  1.6 11.5 %all_to_all.11 = bf16[16,8,1024]{2,1,0:T(8,128)(2,1)S(1)} all-to-all(bf16[16,8,1024]{2,1,0:T(8,128)(2,1)S(1)} %bitcast.11), channel_id=1, replica_groups={{27,26,25,24,19,18,17,16,11,10,9,8,3,2,1,0},{31,30,29,28,23,22,21,20,15..., dimensions={0} | all-to-all | bytes 524288 | tf_op jit(solution)/shard_map/all_to_all | solution.py:196
  13.1 0.0 copy-done
  13.2 0.7 %shard_map.93 = bf16[128,128]{1,0:T(8,128)(2,1)S(1)} custom-call(bf16[128,1024]{1,0:T(8,128)(2,1)S(1)} %bitcast.9, bf16[1024,128]{1,0:T(8,128)(2,1)S(1)} %copy-done), custom_call_target="tpu_custom_call" | custom-call | flops 67108864 | bytes 524288 | tf_op jit(solution)/shard_map/pallas_call | solution.py:207
  13.9 2.7 %collective-permute-start = (bf16[128,128]{1,0:T(8,128)(2,1)S(1)}, bf16[128,128]{1,0:T(8,128)(2,1)S(1)}, u32[]{:S(2)}, u32[]{:S(2)}) collective-permute-start(bf16[128,128]{1,0:T(8,128)(2,1)S(1)} %shard_map.93), channel_id=1, source_target_pairs={{0,4},{4,0},{1,5},{5,1},{2,6},{6,2},{3,7},{7,3},{8,12},{12,8},{9,1... | collective-permute-start | bytes 98312 | tf_op jit(solution)/shard_map/ppermute | solution.py:224
  16.6 0.7 %shard_map.92.mine_ref = f32[128,128]{1,0:T(8,128)S(1)} custom-call(bf16[128,1024]{1,0:T(8,128)(2,1)S(1)} %bitcast.10, bf16[1024,128]{1,0:T(8,128)(2,1)S(1)} %copy-done), custom_call_target="tpu_custom_call" | custom-call | flops 67108864 | bytes 524288 | tf_op jit(solution)/shard_map/pallas_call | solution.py:207
  17.3 1.7 %collective-permute-done.came_ref = bf16[128,128]{1,0:T(8,128)(2,1)S(1)} collective-permute-done((bf16[128,128]{1,0:T(8,128)(2,1)S(1)}, bf16[128,128]{1,0:T(8,128)(2,1)S(1)}, u32[]{:S(2)}, u32[]{:S(2)}) %collective-permute-start) | collective-permute-done | bytes 32800 | tf_op jit(solution)/shard_map/ppermute | solution.py:224
  19.0 0.6 %shard_map.94 = bf16[8,16,128]{2,1,0:T(8,128)(2,1)} custom-call(f32[128,128]{1,0:T(8,128)S(1)} %shard_map.92.mine_ref, bf16[128,128]{1,0:T(8,128)(2,1)S(1)} %collective-permute-done.came_ref, f32[1,128]{1,0:T(1,128)S(1)} %get-tuple-element.8.bias_ref), custom_call_target="tpu_custom_call" | custom-call | tf_op jit(solution)/shard_map/pallas_call | solution.py:226
Async XLA Ops:
  1.6 11.5 %copy-start = (bf16[1024,128]{1,0:T(8,128)(2,1)S(1)}, bf16[1024,128]{1,0:T(8,128)(2,1)}, u32[]{:S(2)}) copy-start(bf16[1024,128]{1,0:T(8,128)(2,1)} %weight_ref.3) | copy-start | bytes 786436
  13.9 5.1 %collective-permute-start = (bf16[128,128]{1,0:T(8,128)(2,1)S(1)}, bf16[128,128]{1,0:T(8,128)(2,1)S(1)}, u32[]{:S(2)}, u32[]{:S(2)}) collective-permute-start(bf16[128,128]{1,0:T(8,128)(2,1)S(1)} %shard_map.93), channel_id=1, source_target_pairs={{0,4},{4,0},{1,5},{5,1},{2,6},{6,2},{3,7},{7,3},{8,12},{12,8},{9,1... | collective-permute-start | bytes 98312 | tf_op jit(solution)/shard_map/ppermute | solution.py:224

commit v9 on v8

--- a/solution.py
+++ b/solution.py
@@ -12,7 +12,8 @@
 
 
 def peer_order(seq_count, rest_count):
-    return [(b, a) for b in range(seq_count) for a in range(rest_count)][::-1]
+    peers = [(b, a) for b in range(seq_count) for a in range(rest_count)]
+    return peers[-1:] + peers[:-1]
 
 
 def project_kernel(

time: 19.8 us -> 19.5 us (0.985)
  waiting for transfers between devices: 1.7 us -> 1.48 us
    ppermute x1, waiting for transfers between devices: 1.7 us -> 1.48 us  [body(): came = lax.ppermute(theirs, 'half', [(0, 1), (1, 0)])]
where the time goes in v9:
time: 19.5 us; the launch traced here: 19.3 us
  blocking collectives  11.4 us (58%)
  Pallas kernels  3.75 us (19%)
  starting transfers between devices  2.66 us (14%)
  waiting for transfers between devices  1.48 us (8%)
    all_to_all x1, blocking collectives, body(): lax.all_to_all(send, ('seq', 'half', 'rest'), split_axis=0, concat_axis=0...  11.4 us
    ppermute x1, starting transfers between devices, body(): came = lax.ppermute(theirs, 'half', [(0, 1), (1, 0)])  2.66 us
    pallas_call x1, Pallas kernels, body(): pl.pallas_call(functools.partial(project_kernel, seq_count, half_count, r...  1.62 us
    pallas_call x2, Pallas kernels, pair_block(): pl.pallas_call(functools.partial(pair_kernel, own, hidden, row_block, col...  1.49 us
    ppermute x1, waiting for transfers between devices, body(): came = lax.ppermute(theirs, 'half', [(0, 1), (1, 0)])  1.48 us
    pallas_call x1, Pallas kernels, body(): pl.pallas_call(add_kernel, out_shape=jax.ShapeDtypeStruct((row_block, col...  0.64 us
  transfers between devices with their start and end apart: 1, of which 1 were waited for; matrix products, arithmetic and copies ran while one was open for 0% of the time, Pallas kernels for 4%

profile of v9, /device:TPU:0, one launch (start us, length us, event | category | flops | bytes accessed | tf_op | source)
XLA Modules:
  0.0 19.3 jit_solution(16926967990434182460)
XLA Ops:
  0.0 1.6 %shard_map.91 = (bf16[128,1024]{1,0:T(8,128)(2,1)S(1)}, f32[1,128]{1,0:T(1,128)S(1)}) custom-call(bf16[8,64,256]{2,1,0:T(8,128)(2,1)} %align_hbm.1, f32[1,256]{1,0:T(1,128)} %bitcast.14, f32[1,256]{1,0:T(1,128)} %bitcast.15, bf16[32,256]{1,0:T(8,128)(2,1)} %bitcast.12, f32[1,32]{1,0:T(1,128)} %bitcast.16, bf16[32,256]{1,0:T(8,128)(2,1)} %bitcast.13, ...), custom_call_target="tpu_custom_call" | custom-call | tf_op jit(solution)/shard_map/pallas_call | solution.py:162
  1.6 0.0 copy-start
  1.6 11.4 %all_to_all.11 = bf16[16,8,1024]{2,1,0:T(8,128)(2,1)S(1)} all-to-all(bf16[16,8,1024]{2,1,0:T(8,128)(2,1)S(1)} %bitcast.11), channel_id=1, replica_groups={{27,0,1,2,3,8,9,10,11,16,17,18,19,24,25,26},{31,4,5,6,7,12,13,14,15,20,..., dimensions={0} | all-to-all | bytes 524288 | tf_op jit(solution)/shard_map/all_to_all | solution.py:197
  13.0 0.0 copy-done
  13.1 0.7 %shard_map.93 = bf16[128,128]{1,0:T(8,128)(2,1)S(1)} custom-call(bf16[128,1024]{1,0:T(8,128)(2,1)S(1)} %bitcast.9, bf16[1024,128]{1,0:T(8,128)(2,1)S(1)} %copy-done), custom_call_target="tpu_custom_call" | custom-call | flops 67108864 | bytes 524288 | tf_op jit(solution)/shard_map/pallas_call | solution.py:208
  13.8 2.7 %collective-permute-start = (bf16[128,128]{1,0:T(8,128)(2,1)S(1)}, bf16[128,128]{1,0:T(8,128)(2,1)S(1)}, u32[]{:S(2)}, u32[]{:S(2)}) collective-permute-start(bf16[128,128]{1,0:T(8,128)(2,1)S(1)} %shard_map.93), channel_id=1, source_target_pairs={{0,4},{4,0},{1,5},{5,1},{2,6},{6,2},{3,7},{7,3},{8,12},{12,8},{9,1... | collective-permute-start | bytes 98312 | tf_op jit(solution)/shard_map/ppermute | solution.py:225
  16.5 0.7 %shard_map.92.mine_ref = f32[128,128]{1,0:T(8,128)S(1)} custom-call(bf16[128,1024]{1,0:T(8,128)(2,1)S(1)} %bitcast.10, bf16[1024,128]{1,0:T(8,128)(2,1)S(1)} %copy-done), custom_call_target="tpu_custom_call" | custom-call | flops 67108864 | bytes 524288 | tf_op jit(solution)/shard_map/pallas_call | solution.py:208
  17.2 1.5 %collective-permute-done.came_ref = bf16[128,128]{1,0:T(8,128)(2,1)S(1)} collective-permute-done((bf16[128,128]{1,0:T(8,128)(2,1)S(1)}, bf16[128,128]{1,0:T(8,128)(2,1)S(1)}, u32[]{:S(2)}, u32[]{:S(2)}) %collective-permute-start) | collective-permute-done | bytes 32800 | tf_op jit(solution)/shard_map/ppermute | solution.py:225
  18.7 0.6 %shard_map.94 = bf16[8,16,128]{2,1,0:T(8,128)(2,1)} custom-call(f32[128,128]{1,0:T(8,128)S(1)} %shard_map.92.mine_ref, bf16[128,128]{1,0:T(8,128)(2,1)S(1)} %collective-permute-done.came_ref, f32[1,128]{1,0:T(1,128)S(1)} %get-tuple-element.8.bias_ref), custom_call_target="tpu_custom_call" | custom-call | tf_op jit(solution)/shard_map/pallas_call | solution.py:227
Async XLA Ops:
  1.6 11.4 %copy-start = (bf16[1024,128]{1,0:T(8,128)(2,1)S(1)}, bf16[1024,128]{1,0:T(8,128)(2,1)}, u32[]{:S(2)}) copy-start(bf16[1024,128]{1,0:T(8,128)(2,1)} %weight_ref.3) | copy-start | bytes 786436
  13.8 4.9 %collective-permute-start = (bf16[128,128]{1,0:T(8,128)(2,1)S(1)}, bf16[128,128]{1,0:T(8,128)(2,1)S(1)}, u32[]{:S(2)}, u32[]{:S(2)}) collective-permute-start(bf16[128,128]{1,0:T(8,128)(2,1)S(1)} %shard_map.93), channel_id=1, source_target_pairs={{0,4},{4,0},{1,5},{5,1},{2,6},{6,2},{3,7},{7,3},{8,12},{12,8},{9,1... | collective-permute-start | bytes 98312 | tf_op jit(solution)/shard_map/ppermute | solution.py:225

commit v10 on v9

--- a/solution.py
+++ b/solution.py
@@ -41,11 +41,13 @@
     left_ref,
     sems,
 ):
+    step = max(1, align_ref.shape[0] // 4)
+    cuts = [pl.ds(at, step) for at in range(0, align_ref.shape[0], step)]
     copies = [
         pltpu.make_async_copy(source, target, sems.at[n])
         for n, (source, target) in enumerate(
-            [
-                (align_hbm, align_ref),
+            [(align_hbm.at[cut], align_ref.at[cut]) for cut in cuts]
+            + [
                 (gain_hbm, gain_ref),
                 (offset_hbm, offset_ref),
                 (left_w_hbm, left_w_ref),
@@ -84,8 +86,9 @@
         left_ref[a] = jnp.concatenate(
             [t[:, :hidden] for t in tiles[a * row_block : (a + 1) * row_block]], axis=1
         )
+    order = column_order(col_block, LANES // hidden)
     right = [
-        jnp.concatenate([t[:, hidden:] for t in tiles[b * col_block : (b + 1) * col_block]], axis=1)
+        jnp.concatenate([tiles[b * col_block + j][:, hidden:] for j in order], axis=1)
         for b in range(seq_count)
     ]
     half = lax.axis_index("half")
@@ -101,26 +104,63 @@
         send_ref[pl.ds(start * rows, group * rows), :] = block.astype(jnp.bfloat16)
 
 
-def pair_kernel(own, hidden, row_block, col_block, recv_ref, weight_ref, out_ref, outer_ref):
-    seq_total = 2 * recv_ref.shape[0]
+def pair_kernel(own, hidden, row_block, col_block, recv_ref, weight_ref, out_ref, left_ref):
+    seqs = recv_ref.shape[0]
     split = row_block * hidden
     left = recv_ref[:, :split] if own else recv_ref[:, split : 2 * split]
     right = recv_ref[:, 2 * split :]
-    outer = lax.dot_general(
-        left, right, (((0,), (0,)), ((), ())), preferred_element_type=jnp.float32
-    )
-    for g in range(outer_ref.shape[0]):
-        outer_ref[g] = outer[:, g * LANES : (g + 1) * LANES]
+    turned = left.astype(jnp.float32).T
+    parts = left_ref.shape[0]
+    for n in range(parts):
+        left_ref[n] = turned[:, n * LANES : (n + 1) * LANES]
+    left = jnp.concatenate(
+        [
+            jnp.concatenate(
+                [left_ref[n, pl.ds(c, row_block, stride=hidden), :] for n in range(parts)], axis=1
+            )
+            for c in range(hidden)
+        ],
+        axis=0,
+    ).astype(jnp.bfloat16)
+    outer = jnp.dot(left, right, preferred_element_type=jnp.float32)
     per_group = LANES // hidden
-    terms = []
-    for g in range(outer_ref.shape[0]):
-        slabs = [outer_ref[g, pl.ds(c, row_block, stride=hidden), :] for c in range(hidden)]
-        for j in range(per_group):
-            flat = jnp.concatenate([s[:, j * hidden : (j + 1) * hidden] for s in slabs], axis=1)
-            terms.append(flat)
-    flat = jnp.concatenate(terms, axis=0).astype(jnp.bfloat16)
+    lane_block = lax.broadcasted_iota(jnp.int32, (2 * row_block, LANES), 1) // hidden
+    rows = []
+    for g in range(0, col_block // per_group, 2):
+        lines = [[] for _ in range(per_group)]
+        for c in range(0, hidden, per_group):
+            rolled = []
+            for k in range(per_group):
+                at = (c + k) * row_block
+                tile = jnp.concatenate(
+                    [
+                        outer[at : at + row_block, (g + h) * LANES : (g + h + 1) * LANES]
+                        for h in range(2)
+                    ],
+                    axis=0,
+                )
+                rolled.append(roll_blocks(tile.astype(jnp.bfloat16), k, hidden))
+            for j in range(per_group):
+                mixed = rolled[(per_group - 1 - j) % per_group]
+                for p in range(per_group - 1):
+                    mixed = jnp.where(lane_block == p, rolled[(p - j) % per_group], mixed)
+                lines[j].append(roll_blocks(mixed, -j, hidden))
+        rows += [jnp.concatenate(line, axis=1) for line in lines]
+    flat = jnp.concatenate(rows, axis=0)
     term = jnp.dot(flat, weight_ref[...], preferred_element_type=jnp.float32)
-    out_ref[...] = (term * (1.0 / float(seq_total))).astype(out_ref.dtype)
+    out_ref[...] = (term * (1.0 / float(2 * seqs))).astype(out_ref.dtype)
+
+
+def roll_blocks(tile, count, hidden):
+    shift = count * hidden % LANES
+    return pltpu.roll(tile, shift, 1) if shift else tile
+
+
+def column_order(col_block, per_group):
+    double = 2 * per_group
+    return [
+        double * (p // double) + 2 * (p % per_group) + (p // per_group) % 2 for p in range(col_block)
+    ]
 
 
 def add_kernel(mine_ref, came_ref, bias_ref, out_ref, term_ref):
@@ -177,7 +217,7 @@
             pltpu.VMEM((1, hidden), jnp.float32),
             pltpu.VMEM((rows * res_total, LANES), jnp.float32),
             pltpu.VMEM((half_count * rest_count, rows, row_block * hidden), jnp.float32),
-            pltpu.SemaphoreType.DMA((8,)),
+            pltpu.SemaphoreType.DMA((7 + rows // max(1, rows // 4),)),
         ],
         compiler_params=params,
     )(
@@ -211,7 +251,7 @@
             in_specs=[vmem] * 2,
             out_specs=vmem,
             scratch_shapes=[
-                pltpu.VMEM((col_block * hidden // LANES, row_block * hidden, LANES), jnp.float32)
+                pltpu.VMEM((recv.shape[0] // LANES, row_block * hidden, LANES), jnp.float32)
             ],
             compiler_params=params,
             cost_estimate=pl.CostEstimate(

time: 19.5 us -> 19.4 us (level)
  Pallas kernels: 3.75 us -> 3.55 us
    pallas_call x2, Pallas kernels: 1.49 us -> 1.28 us  [pair_block(): pl.pallas_call(functools.partial(pair_kernel, own, hidden, row_block, col...]
  transfers between devices with their start and end apart: 1 -> 1, of which waited for: 1 -> 1; matrix products, arithmetic and copies ran while one was open for 0% -> 0% of each run, Pallas kernels for 4% -> 3%
where the time goes in v10:
time: 19.4 us; the launch traced here: 19.2 us
  blocking collectives  11.4 us (59%)
  Pallas kernels  3.55 us (18%)
  starting transfers between devices  2.65 us (14%)
  waiting for transfers between devices  1.59 us (8%)
    all_to_all x1, blocking collectives, body(): lax.all_to_all(send, ('seq', 'half', 'rest'), split_axis=0, concat_axis=0...  11.4 us
    ppermute x1, starting transfers between devices, body(): came = lax.ppermute(theirs, 'half', [(0, 1), (1, 0)])  2.65 us
    pallas_call x1, Pallas kernels, body(): pl.pallas_call(functools.partial(project_kernel, seq_count, half_count, r...  1.63 us
    ppermute x1, waiting for transfers between devices, body(): came = lax.ppermute(theirs, 'half', [(0, 1), (1, 0)])  1.59 us
    pallas_call x2, Pallas kernels, pair_block(): pl.pallas_call(functools.partial(pair_kernel, own, hidden, row_block, col...  1.28 us
    pallas_call x1, Pallas kernels, body(): pl.pallas_call(add_kernel, out_shape=jax.ShapeDtypeStruct((row_block, col...  0.64 us
  transfers between devices with their start and end apart: 1, of which 1 were waited for; matrix products, arithmetic and copies ran while one was open for 0% of the time, Pallas kernels for 3%

profile of v10, /device:TPU:0, one launch (start us, length us, event | category | flops | bytes accessed | tf_op | source)
XLA Modules:
  0.0 19.2 jit_solution(14668597805597360585)
XLA Ops:
  0.0 1.6 %shard_map.91 = (bf16[128,1024]{1,0:T(8,128)(2,1)S(1)}, f32[1,128]{1,0:T(1,128)S(1)}) custom-call(bf16[8,64,256]{2,1,0:T(8,128)(2,1)} %align_hbm.1, f32[1,256]{1,0:T(1,128)} %bitcast.14, f32[1,256]{1,0:T(1,128)} %bitcast.15, bf16[32,256]{1,0:T(8,128)(2,1)} %bitcast.12, f32[1,32]{1,0:T(1,128)} %bitcast.16, bf16[32,256]{1,0:T(8,128)(2,1)} %bitcast.13, ...), custom_call_target="tpu_custom_call" | custom-call | tf_op jit(solution)/shard_map/pallas_call | solution.py:202
  1.6 0.0 copy-start
  1.6 11.4 %all_to_all.11 = bf16[16,8,1024]{2,1,0:T(8,128)(2,1)S(1)} all-to-all(bf16[16,8,1024]{2,1,0:T(8,128)(2,1)S(1)} %bitcast.11), channel_id=1, replica_groups={{27,0,1,2,3,8,9,10,11,16,17,18,19,24,25,26},{31,4,5,6,7,12,13,14,15,20,..., dimensions={0} | all-to-all | bytes 524288 | tf_op jit(solution)/shard_map/all_to_all | solution.py:237
  13.1 0.0 copy-done
  13.1 0.6 %shard_map.93 = bf16[128,128]{1,0:T(8,128)(2,1)S(1)} custom-call(bf16[128,1024]{1,0:T(8,128)(2,1)S(1)} %bitcast.9, bf16[1024,128]{1,0:T(8,128)(2,1)S(1)} %copy-done), custom_call_target="tpu_custom_call" | custom-call | flops 67108864 | bytes 524288 | tf_op jit(solution)/shard_map/pallas_call | solution.py:248
  13.7 2.7 %collective-permute-start = (bf16[128,128]{1,0:T(8,128)(2,1)S(1)}, bf16[128,128]{1,0:T(8,128)(2,1)S(1)}, u32[]{:S(2)}, u32[]{:S(2)}) collective-permute-start(bf16[128,128]{1,0:T(8,128)(2,1)S(1)} %shard_map.93), channel_id=1, source_target_pairs={{0,4},{4,0},{1,5},{5,1},{2,6},{6,2},{3,7},{7,3},{8,12},{12,8},{9,1... | collective-permute-start | bytes 98312 | tf_op jit(solution)/shard_map/ppermute | solution.py:265
  16.4 0.6 %shard_map.92.mine_ref = f32[128,128]{1,0:T(8,128)S(1)} custom-call(bf16[128,1024]{1,0:T(8,128)(2,1)S(1)} %bitcast.10, bf16[1024,128]{1,0:T(8,128)(2,1)S(1)} %copy-done), custom_call_target="tpu_custom_call" | custom-call | flops 67108864 | bytes 524288 | tf_op jit(solution)/shard_map/pallas_call | solution.py:248
  17.0 1.6 %collective-permute-done.came_ref = bf16[128,128]{1,0:T(8,128)(2,1)S(1)} collective-permute-done((bf16[128,128]{1,0:T(8,128)(2,1)S(1)}, bf16[128,128]{1,0:T(8,128)(2,1)S(1)}, u32[]{:S(2)}, u32[]{:S(2)}) %collective-permute-start) | collective-permute-done | bytes 32800 | tf_op jit(solution)/shard_map/ppermute | solution.py:265
  18.6 0.6 %shard_map.94 = bf16[8,16,128]{2,1,0:T(8,128)(2,1)} custom-call(f32[128,128]{1,0:T(8,128)S(1)} %shard_map.92.mine_ref, bf16[128,128]{1,0:T(8,128)(2,1)S(1)} %collective-permute-done.came_ref, f32[1,128]{1,0:T(1,128)S(1)} %get-tuple-element.8.bias_ref), custom_call_target="tpu_custom_call" | custom-call | tf_op jit(solution)/shard_map/pallas_call | solution.py:267
Async XLA Ops:
  1.6 11.4 %copy-start = (bf16[1024,128]{1,0:T(8,128)(2,1)S(1)}, bf16[1024,128]{1,0:T(8,128)(2,1)}, u32[]{:S(2)}) copy-start(bf16[1024,128]{1,0:T(8,128)(2,1)} %weight_ref.3) | copy-start | bytes 786436
  13.7 4.9 %collective-permute-start = (bf16[128,128]{1,0:T(8,128)(2,1)S(1)}, bf16[128,128]{1,0:T(8,128)(2,1)S(1)}, u32[]{:S(2)}, u32[]{:S(2)}) collective-permute-start(bf16[128,128]{1,0:T(8,128)(2,1)S(1)} %shard_map.93), channel_id=1, source_target_pairs={{0,4},{4,0},{1,5},{5,1},{2,6},{6,2},{3,7},{7,3},{8,12},{12,8},{9,1... | collective-permute-start | bytes 98312 | tf_op jit(solution)/shard_map/ppermute | solution.py:265

commit v11 on v10

--- a/solution.py
+++ b/solution.py
@@ -41,56 +41,60 @@
     left_ref,
     sems,
 ):
-    step = max(1, align_ref.shape[0] // 4)
-    cuts = [pl.ds(at, step) for at in range(0, align_ref.shape[0], step)]
-    copies = [
+    rows, res_total, chan = align_ref.shape
+    hidden = left_w_ref.shape[0]
+    align, left_w, right_w, gain, offset, left_b, right_b, out_b = [
         pltpu.make_async_copy(source, target, sems.at[n])
         for n, (source, target) in enumerate(
-            [(align_hbm.at[cut], align_ref.at[cut]) for cut in cuts]
-            + [
+            [
+                (align_hbm, align_ref),
+                (left_w_hbm, left_w_ref),
+                (right_w_hbm, right_w_ref),
                 (gain_hbm, gain_ref),
                 (offset_hbm, offset_ref),
-                (left_w_hbm, left_w_ref),
                 (left_b_hbm, left_b_ref),
-                (right_w_hbm, right_w_ref),
                 (right_b_hbm, right_b_ref),
                 (out_b_hbm, out_b_ref),
             ]
         )
     ]
-    for copy in copies:
+    for copy in (align, left_w, right_w, gain, offset, left_b, right_b, out_b):
         copy.start()
-    for copy in copies:
-        copy.wait()
-    rows, res_total, chan = align_ref.shape
-    hidden = left_w_ref.shape[0]
+    align.wait()
     values = align_ref[...].astype(jnp.float32).reshape(rows * res_total, chan)
     centred = values - jnp.mean(values, axis=-1, keepdims=True)
     spread = jnp.mean(centred * centred, axis=-1, keepdims=True)
-    normed = centred * lax.rsqrt(spread + 1e-05) * gain_ref[...] + offset_ref[...]
-    weights = jnp.concatenate([left_w_ref[...], right_w_ref[...]], axis=0)
-    biases = jnp.concatenate([left_b_ref[...], right_b_ref[...]], axis=1)
-    proj_ref[:, : 2 * hidden] = (
-        lax.dot_general(
-            normed.astype(jnp.bfloat16),
-            weights,
-            (((1,), (1,)), ((), ())),
-            preferred_element_type=jnp.float32,
-        )
-        + biases
+    scaled = centred * lax.rsqrt(spread + 1e-05)
+    for copy in (left_w, right_w, gain, offset):
+        copy.wait()
+    normed = (scaled * gain_ref[...] + offset_ref[...]).astype(jnp.bfloat16)
+    repeats = LANES // hidden
+    weights = jnp.concatenate([left_w_ref[...]] * repeats + [right_w_ref[...]] * repeats, axis=0)
+    both = lax.dot_general(
+        normed, weights, (((1,), (1,)), ((), ())), preferred_element_type=jnp.float32
     )
-    tiles = [proj_ref[pl.ds(r, rows, stride=res_total), :][:, : 2 * hidden] for r in range(res_total)]
+    for copy in (left_b, right_b, out_b):
+        copy.wait()
+    proj_ref[0] = both[:, :LANES] + jnp.concatenate([left_b_ref[...]] * repeats, axis=1)
+    proj_ref[1] = both[:, LANES:] + jnp.concatenate([right_b_ref[...]] * repeats, axis=1)
+    lane_block = lax.broadcasted_iota(jnp.int32, (rows, LANES), 1) // hidden
+
+    def lined_up(side, residues):
+        tiles = [proj_ref[side, pl.ds(r, rows, stride=res_total), :] for r in residues]
+        lines = []
+        for at in range(0, len(tiles), repeats):
+            line = tiles[at]
+            for p in range(1, repeats):
+                line = jnp.where(lane_block == p, tiles[at + p], line)
+            lines.append(line)
+        return jnp.concatenate(lines, axis=1)
+
     row_block = res_total // (half_count * rest_count)
     col_block = res_total // seq_count
+    order = column_order(col_block, repeats)
     for a in range(half_count * rest_count):
-        left_ref[a] = jnp.concatenate(
-            [t[:, :hidden] for t in tiles[a * row_block : (a + 1) * row_block]], axis=1
-        )
-    order = column_order(col_block, LANES // hidden)
-    right = [
-        jnp.concatenate([tiles[b * col_block + j][:, hidden:] for j in order], axis=1)
-        for b in range(seq_count)
-    ]
+        left_ref[a] = lined_up(0, [a * row_block + i for i in range(row_block)])
+    right = [lined_up(1, [b * col_block + j for j in order]) for b in range(seq_count)]
     half = lax.axis_index("half")
     own = [left_ref[half * rest_count + a] for a in range(rest_count)]
     other = [left_ref[(1 - half) * rest_count + a] for a in range(rest_count)]
@@ -215,9 +219,9 @@
             pltpu.VMEM((1, hidden), jnp.float32),
             pltpu.VMEM((hidden, chan), jnp.bfloat16),
             pltpu.VMEM((1, hidden), jnp.float32),
-            pltpu.VMEM((rows * res_total, LANES), jnp.float32),
+            pltpu.VMEM((2, rows * res_total, LANES), jnp.float32),
             pltpu.VMEM((half_count * rest_count, rows, row_block * hidden), jnp.float32),
-            pltpu.SemaphoreType.DMA((7 + rows // max(1, rows // 4),)),
+            pltpu.SemaphoreType.DMA((8,)),
         ],
         compiler_params=params,
     )(

time: 19.4 us -> 19.7 us (1.015)
  Pallas kernels: 3.55 us -> 3.85 us
    pallas_call x1, Pallas kernels: 1.63 us -> 1.93 us  [body(): pl.pallas_call(functools.partial(project_kernel, seq_count, half_count, r...]
where the time goes in v11:
time: 19.7 us; the launch traced here: 19.5 us
  blocking collectives  11.4 us (58%)
  Pallas kernels  3.85 us (20%)
  starting transfers between devices  2.65 us (13%)
  waiting for transfers between devices  1.59 us (8%)
    all_to_all x1, blocking collectives, body(): lax.all_to_all(send, ('seq', 'half', 'rest'), split_axis=0, concat_axis=0...  11.4 us
    ppermute x1, starting transfers between devices, body(): came = lax.ppermute(theirs, 'half', [(0, 1), (1, 0)])  2.65 us
    pallas_call x1, Pallas kernels, body(): pl.pallas_call(functools.partial(project_kernel, seq_count, half_count, r...  1.93 us
    ppermute x1, waiting for transfers between devices, body(): came = lax.ppermute(theirs, 'half', [(0, 1), (1, 0)])  1.59 us
    pallas_call x2, Pallas kernels, pair_block(): pl.pallas_call(functools.partial(pair_kernel, own, hidden, row_block, col...  1.28 us
    pallas_call x1, Pallas kernels, body(): pl.pallas_call(add_kernel, out_shape=jax.ShapeDtypeStruct((row_block, col...  0.64 us
  transfers between devices with their start and end apart: 1, of which 1 were waited for; matrix products, arithmetic and copies ran while one was open for 0% of the time, Pallas kernels for 3%

profile of v11, /device:TPU:0, one launch (start us, length us, event | category | flops | bytes accessed | tf_op | source)
XLA Modules:
  0.0 19.5 jit_solution(10276516039553855660)
XLA Ops:
  0.0 1.9 %shard_map.91 = (bf16[128,1024]{1,0:T(8,128)(2,1)S(1)}, f32[1,128]{1,0:T(1,128)S(1)}) custom-call(bf16[8,64,256]{2,1,0:T(8,128)(2,1)} %align_hbm.1, f32[1,256]{1,0:T(1,128)} %bitcast.14, f32[1,256]{1,0:T(1,128)} %bitcast.15, bf16[32,256]{1,0:T(8,128)(2,1)} %bitcast.12, f32[1,32]{1,0:T(1,128)} %bitcast.16, bf16[32,256]{1,0:T(8,128)(2,1)} %bitcast.13, ...), custom_call_target="tpu_custom_call" | custom-call | tf_op jit(solution)/shard_map/pallas_call | solution.py:206
  1.9 0.0 copy-start
  1.9 11.4 %all_to_all.11 = bf16[16,8,1024]{2,1,0:T(8,128)(2,1)S(1)} all-to-all(bf16[16,8,1024]{2,1,0:T(8,128)(2,1)S(1)} %bitcast.11), channel_id=1, replica_groups={{27,0,1,2,3,8,9,10,11,16,17,18,19,24,25,26},{31,4,5,6,7,12,13,14,15,20,..., dimensions={0} | all-to-all | bytes 524288 | tf_op jit(solution)/shard_map/all_to_all | solution.py:241
  13.4 0.0 copy-done
  13.4 0.6 %shard_map.93 = bf16[128,128]{1,0:T(8,128)(2,1)S(1)} custom-call(bf16[128,1024]{1,0:T(8,128)(2,1)S(1)} %bitcast.9, bf16[1024,128]{1,0:T(8,128)(2,1)S(1)} %copy-done), custom_call_target="tpu_custom_call" | custom-call | flops 67108864 | bytes 524288 | tf_op jit(solution)/shard_map/pallas_call | solution.py:252
  14.0 2.7 %collective-permute-start = (bf16[128,128]{1,0:T(8,128)(2,1)S(1)}, bf16[128,128]{1,0:T(8,128)(2,1)S(1)}, u32[]{:S(2)}, u32[]{:S(2)}) collective-permute-start(bf16[128,128]{1,0:T(8,128)(2,1)S(1)} %shard_map.93), channel_id=1, source_target_pairs={{0,4},{4,0},{1,5},{5,1},{2,6},{6,2},{3,7},{7,3},{8,12},{12,8},{9,1... | collective-permute-start | bytes 98312 | tf_op jit(solution)/shard_map/ppermute | solution.py:269
  16.7 0.6 %shard_map.92.mine_ref = f32[128,128]{1,0:T(8,128)S(1)} custom-call(bf16[128,1024]{1,0:T(8,128)(2,1)S(1)} %bitcast.10, bf16[1024,128]{1,0:T(8,128)(2,1)S(1)} %copy-done), custom_call_target="tpu_custom_call" | custom-call | flops 67108864 | bytes 524288 | tf_op jit(solution)/shard_map/pallas_call | solution.py:252
  17.3 1.6 %collective-permute-done.came_ref = bf16[128,128]{1,0:T(8,128)(2,1)S(1)} collective-permute-done((bf16[128,128]{1,0:T(8,128)(2,1)S(1)}, bf16[128,128]{1,0:T(8,128)(2,1)S(1)}, u32[]{:S(2)}, u32[]{:S(2)}) %collective-permute-start) | collective-permute-done | bytes 32800 | tf_op jit(solution)/shard_map/ppermute | solution.py:269
  18.9 0.6 %shard_map.94 = bf16[8,16,128]{2,1,0:T(8,128)(2,1)} custom-call(f32[128,128]{1,0:T(8,128)S(1)} %shard_map.92.mine_ref, bf16[128,128]{1,0:T(8,128)(2,1)S(1)} %collective-permute-done.came_ref, f32[1,128]{1,0:T(1,128)S(1)} %get-tuple-element.8.bias_ref), custom_call_target="tpu_custom_call" | custom-call | tf_op jit(solution)/shard_map/pallas_call | solution.py:271
Async XLA Ops:
  1.9 11.4 %copy-start = (bf16[1024,128]{1,0:T(8,128)(2,1)S(1)}, bf16[1024,128]{1,0:T(8,128)(2,1)}, u32[]{:S(2)}) copy-start(bf16[1024,128]{1,0:T(8,128)(2,1)} %weight_ref.3) | copy-start | bytes 786436
  14.0 4.9 %collective-permute-start = (bf16[128,128]{1,0:T(8,128)(2,1)S(1)}, bf16[128,128]{1,0:T(8,128)(2,1)S(1)}, u32[]{:S(2)}, u32[]{:S(2)}) collective-permute-start(bf16[128,128]{1,0:T(8,128)(2,1)S(1)} %shard_map.93), channel_id=1, source_target_pairs={{0,4},{4,0},{1,5},{5,1},{2,6},{6,2},{3,7},{7,3},{8,12},{12,8},{9,1... | collective-permute-start | bytes 98312 | tf_op jit(solution)/shard_map/ppermute | solution.py:269

commit v12 on v10

--- a/solution.py
+++ b/solution.py
@@ -12,7 +12,7 @@
 
 
 def peer_order(seq_count, rest_count):
-    peers = [(b, a) for b in range(seq_count) for a in range(rest_count)]
+    peers = [(b, a) for a in range(rest_count) for b in range(seq_count)]
     return peers[-1:] + peers[:-1]
 
 
@@ -41,18 +41,16 @@
     left_ref,
     sems,
 ):
-    step = max(1, align_ref.shape[0] // 4)
-    cuts = [pl.ds(at, step) for at in range(0, align_ref.shape[0], step)]
     copies = [
         pltpu.make_async_copy(source, target, sems.at[n])
         for n, (source, target) in enumerate(
-            [(align_hbm.at[cut], align_ref.at[cut]) for cut in cuts]
-            + [
+            [
+                (align_hbm, align_ref),
+                (left_w_hbm, left_w_ref),
+                (right_w_hbm, right_w_ref),
                 (gain_hbm, gain_ref),
                 (offset_hbm, offset_ref),
-                (left_w_hbm, left_w_ref),
                 (left_b_hbm, left_b_ref),
-                (right_w_hbm, right_w_ref),
                 (right_b_hbm, right_b_ref),
                 (out_b_hbm, out_b_ref),
             ]
@@ -64,21 +62,25 @@
         copy.wait()
     rows, res_total, chan = align_ref.shape
     hidden = left_w_ref.shape[0]
-    values = align_ref[...].astype(jnp.float32).reshape(rows * res_total, chan)
-    centred = values - jnp.mean(values, axis=-1, keepdims=True)
+    weights = jnp.concatenate([left_w_ref[...], right_w_ref[...]], axis=0)
+    scaled = (weights.astype(jnp.float32) * gain_ref[...]).astype(jnp.bfloat16)
+    inner = (((1,), (1,)), ((), ()))
+    raw = align_ref[...].reshape(rows * res_total, chan)
+    product = lax.dot_general(raw, scaled, inner, preferred_element_type=jnp.float32)
+    ones = jnp.ones((8, chan), jnp.bfloat16)
+    sums = lax.dot_general(ones, scaled, inner, preferred_element_type=jnp.float32)[:1]
+    offset = jnp.broadcast_to(offset_ref[...], (8, chan))
+    high = offset.astype(jnp.bfloat16)
+    low = (offset - high.astype(jnp.float32)).astype(jnp.bfloat16)
+    shift = (
+        lax.dot_general(high, weights, inner, preferred_element_type=jnp.float32)
+        + lax.dot_general(low, weights, inner, preferred_element_type=jnp.float32)
+    )[:1] + jnp.concatenate([left_b_ref[...], right_b_ref[...]], axis=1)
+    values = raw.astype(jnp.float32)
+    centre = jnp.mean(values, axis=-1, keepdims=True)
+    centred = values - centre
     spread = jnp.mean(centred * centred, axis=-1, keepdims=True)
-    normed = centred * lax.rsqrt(spread + 1e-05) * gain_ref[...] + offset_ref[...]
-    weights = jnp.concatenate([left_w_ref[...], right_w_ref[...]], axis=0)
-    biases = jnp.concatenate([left_b_ref[...], right_b_ref[...]], axis=1)
-    proj_ref[:, : 2 * hidden] = (
-        lax.dot_general(
-            normed.astype(jnp.bfloat16),
-            weights,
-            (((1,), (1,)), ((), ())),
-            preferred_element_type=jnp.float32,
-        )
-        + biases
-    )
+    proj_ref[:, : 2 * hidden] = (product - centre * sums) * lax.rsqrt(spread + 1e-05) + shift
     tiles = [proj_ref[pl.ds(r, rows, stride=res_total), :][:, : 2 * hidden] for r in range(res_total)]
     row_block = res_total // (half_count * rest_count)
     col_block = res_total // seq_count
@@ -217,7 +219,7 @@
             pltpu.VMEM((1, hidden), jnp.float32),
             pltpu.VMEM((rows * res_total, LANES), jnp.float32),
             pltpu.VMEM((half_count * rest_count, rows, row_block * hidden), jnp.float32),
-            pltpu.SemaphoreType.DMA((7 + rows // max(1, rows // 4),)),
+            pltpu.SemaphoreType.DMA((8,)),
         ],
         compiler_params=params,
     )(

time: 19.4 us -> 19.3 us (level)
  no operation moved by 1% of the time
where the time goes in v12:
time: 19.3 us; the launch traced here: 19.1 us
  blocking collectives  11.3 us (59%)
  Pallas kernels  3.44 us (18%)
  starting transfers between devices  2.65 us (14%)
  waiting for transfers between devices  1.67 us (9%)
    all_to_all x1, blocking collectives, body(): lax.all_to_all(send, ('seq', 'half', 'rest'), split_axis=0, concat_axis=0...  11.3 us
    ppermute x1, starting transfers between devices, body(): came = lax.ppermute(theirs, 'half', [(0, 1), (1, 0)])  2.65 us
    ppermute x1, waiting for transfers between devices, body(): came = lax.ppermute(theirs, 'half', [(0, 1), (1, 0)])  1.67 us
    pallas_call x1, Pallas kernels, body(): pl.pallas_call(functools.partial(project_kernel, seq_count, half_count, r...  1.52 us
    pallas_call x2, Pallas kernels, pair_block(): pl.pallas_call(functools.partial(pair_kernel, own, hidden, row_block, col...  1.28 us
    pallas_call x1, Pallas kernels, body(): pl.pallas_call(add_kernel, out_shape=jax.ShapeDtypeStruct((row_block, col...  0.64 us
  transfers between devices with their start and end apart: 1, of which 1 were waited for; matrix products, arithmetic and copies ran while one was open for 0% of the time, Pallas kernels for 3%

profile of v12, /device:TPU:0, one launch (start us, length us, event | category | flops | bytes accessed | tf_op | source)
XLA Modules:
  0.0 19.1 jit_solution(10311093085777737832)
XLA Ops:
  0.0 1.5 %shard_map.91 = (bf16[128,1024]{1,0:T(8,128)(2,1)S(1)}, f32[1,128]{1,0:T(1,128)S(1)}) custom-call(bf16[8,64,256]{2,1,0:T(8,128)(2,1)} %align_hbm.1, f32[1,256]{1,0:T(1,128)} %bitcast.14, f32[1,256]{1,0:T(1,128)} %bitcast.15, bf16[32,256]{1,0:T(8,128)(2,1)} %bitcast.12, f32[1,32]{1,0:T(1,128)} %bitcast.16, bf16[32,256]{1,0:T(8,128)(2,1)} %bitcast.13, ...), custom_call_target="tpu_custom_call" | custom-call | tf_op jit(solution)/shard_map/pallas_call | solution.py:204
  1.5 0.0 copy-start
  1.5 11.3 %all_to_all.11 = bf16[16,8,1024]{2,1,0:T(8,128)(2,1)S(1)} all-to-all(bf16[16,8,1024]{2,1,0:T(8,128)(2,1)S(1)} %bitcast.11), channel_id=1, replica_groups={{27,0,8,16,24,1,9,17,25,2,10,18,26,3,11,19},{31,4,12,20,28,5,13,21,29,6..., dimensions={0} | all-to-all | bytes 524288 | tf_op jit(solution)/shard_map/all_to_all | solution.py:239
  12.9 0.0 copy-done
  12.9 0.6 %shard_map.93 = bf16[128,128]{1,0:T(8,128)(2,1)S(1)} custom-call(bf16[128,1024]{1,0:T(8,128)(2,1)S(1)} %bitcast.9, bf16[1024,128]{1,0:T(8,128)(2,1)S(1)} %copy-done), custom_call_target="tpu_custom_call" | custom-call | flops 67108864 | bytes 524288 | tf_op jit(solution)/shard_map/pallas_call | solution.py:250
  13.5 2.7 %collective-permute-start = (bf16[128,128]{1,0:T(8,128)(2,1)S(1)}, bf16[128,128]{1,0:T(8,128)(2,1)S(1)}, u32[]{:S(2)}, u32[]{:S(2)}) collective-permute-start(bf16[128,128]{1,0:T(8,128)(2,1)S(1)} %shard_map.93), channel_id=1, source_target_pairs={{0,4},{4,0},{1,5},{5,1},{2,6},{6,2},{3,7},{7,3},{8,12},{12,8},{9,1... | collective-permute-start | bytes 98312 | tf_op jit(solution)/shard_map/ppermute | solution.py:267
  16.2 0.6 %shard_map.92.mine_ref = f32[128,128]{1,0:T(8,128)S(1)} custom-call(bf16[128,1024]{1,0:T(8,128)(2,1)S(1)} %bitcast.10, bf16[1024,128]{1,0:T(8,128)(2,1)S(1)} %copy-done), custom_call_target="tpu_custom_call" | custom-call | flops 67108864 | bytes 524288 | tf_op jit(solution)/shard_map/pallas_call | solution.py:250
  16.8 1.7 %collective-permute-done.came_ref = bf16[128,128]{1,0:T(8,128)(2,1)S(1)} collective-permute-done((bf16[128,128]{1,0:T(8,128)(2,1)S(1)}, bf16[128,128]{1,0:T(8,128)(2,1)S(1)}, u32[]{:S(2)}, u32[]{:S(2)}) %collective-permute-start) | collective-permute-done | bytes 32800 | tf_op jit(solution)/shard_map/ppermute | solution.py:267
  18.5 0.6 %shard_map.94 = bf16[8,16,128]{2,1,0:T(8,128)(2,1)} custom-call(f32[128,128]{1,0:T(8,128)S(1)} %shard_map.92.mine_ref, bf16[128,128]{1,0:T(8,128)(2,1)S(1)} %collective-permute-done.came_ref, f32[1,128]{1,0:T(1,128)S(1)} %get-tuple-element.8.bias_ref), custom_call_target="tpu_custom_call" | custom-call | tf_op jit(solution)/shard_map/pallas_call | solution.py:269
Async XLA Ops:
  1.5 11.3 %copy-start = (bf16[1024,128]{1,0:T(8,128)(2,1)S(1)}, bf16[1024,128]{1,0:T(8,128)(2,1)}, u32[]{:S(2)}) copy-start(bf16[1024,128]{1,0:T(8,128)(2,1)} %weight_ref.3) | copy-start | bytes 786436
  13.5 5.0 %collective-permute-start = (bf16[128,128]{1,0:T(8,128)(2,1)S(1)}, bf16[128,128]{1,0:T(8,128)(2,1)S(1)}, u32[]{:S(2)}, u32[]{:S(2)}) collective-permute-start(bf16[128,128]{1,0:T(8,128)(2,1)S(1)} %shard_map.93), channel_id=1, source_target_pairs={{0,4},{4,0},{1,5},{5,1},{2,6},{6,2},{3,7},{7,3},{8,12},{12,8},{9,1... | collective-permute-start | bytes 98312 | tf_op jit(solution)/shard_map/ppermute | solution.py:267

commit v13 on v10

--- a/solution.py
+++ b/solution.py
@@ -14,6 +14,10 @@
 def peer_order(seq_count, rest_count):
     peers = [(b, a) for b in range(seq_count) for a in range(rest_count)]
     return peers[-1:] + peers[:-1]
+
+
+def partner(at, rest_count):
+    return at ^ 1 if rest_count % 2 == 0 else at
 
 
 def project_kernel(
@@ -58,8 +62,8 @@
             ]
         )
     ]
-    for copy in copies:
-        copy.start()
+    for n, copy in enumerate(copies):
+        copy.start(priority=n % 2)
     for copy in copies:
         copy.wait()
     rows, res_total, chan = align_ref.shape
@@ -93,7 +97,7 @@
     ]
     half = lax.axis_index("half")
     own = [left_ref[half * rest_count + a] for a in range(rest_count)]
-    other = [left_ref[(1 - half) * rest_count + a] for a in range(rest_count)]
+    other = [left_ref[(1 - half) * rest_count + partner(a, rest_count)] for a in range(rest_count)]
     pieces = [
         jnp.concatenate([own[a], other[a], right[b]], axis=1)
         for b, a in peer_order(seq_count, rest_count)
@@ -262,7 +266,12 @@
         )(recv, out_weight)
 
     theirs = pair_block(False, jnp.bfloat16)
-    came = lax.ppermute(theirs, "half", [(0, 1), (1, 0)])
+    swap = [
+        (h * rest_count + q, (1 - h) * rest_count + partner(q, rest_count))
+        for h in range(half_count)
+        for q in range(rest_count)
+    ]
+    came = lax.ppermute(theirs, ("half", "rest"), swap)
     mine = pair_block(True, jnp.float32)
     return pl.pallas_call(
         add_kernel,

time: 19.4 us -> 18.9 us (0.974)
  starting transfers between devices: 2.65 us -> 2.38 us
  waiting for transfers between devices: 1.59 us -> 1.34 us
    ppermute x1, starting transfers between devices: 2.65 us -> 2.38 us  [body(): came = lax.ppermute(theirs, ('half', 'rest'), swap)]
    ppermute x1, waiting for transfers between devices: 1.59 us -> 1.34 us  [body(): came = lax.ppermute(theirs, ('half', 'rest'), swap)]
where the time goes in v13:
time: 18.9 us; the launch traced here: 18.7 us
  blocking collectives  11.4 us (60%)
  Pallas kernels  3.59 us (19%)
  starting transfers between devices  2.38 us (13%)
  waiting for transfers between devices  1.34 us (7%)
    all_to_all x1, blocking collectives, body(): lax.all_to_all(send, ('seq', 'half', 'rest'), split_axis=0, concat_axis=0...  11.4 us
    ppermute x1, starting transfers between devices, body(): came = lax.ppermute(theirs, ('half', 'rest'), swap)  2.38 us
    pallas_call x1, Pallas kernels, body(): pl.pallas_call(functools.partial(project_kernel, seq_count, half_count, r...  1.67 us
    ppermute x1, waiting for transfers between devices, body(): came = lax.ppermute(theirs, ('half', 'rest'), swap)  1.34 us
    pallas_call x2, Pallas kernels, pair_block(): pl.pallas_call(functools.partial(pair_kernel, own, hidden, row_block, col...  1.28 us
    pallas_call x1, Pallas kernels, body(): pl.pallas_call(add_kernel, out_shape=jax.ShapeDtypeStruct((row_block, col...  0.64 us
  transfers between devices with their start and end apart: 1, of which 1 were waited for; matrix products, arithmetic and copies ran while one was open for 0% of the time, Pallas kernels for 3%

profile of v13, /device:TPU:0, one launch (start us, length us, event | category | flops | bytes accessed | tf_op | source)
XLA Modules:
  0.0 18.7 jit_solution(9504656450747124604)
XLA Ops:
  0.0 1.7 %shard_map.91 = (bf16[128,1024]{1,0:T(8,128)(2,1)S(1)}, f32[1,128]{1,0:T(1,128)S(1)}) custom-call(bf16[8,64,256]{2,1,0:T(8,128)(2,1)} %align_hbm.1, f32[1,256]{1,0:T(1,128)} %bitcast.14, f32[1,256]{1,0:T(1,128)} %bitcast.15, bf16[32,256]{1,0:T(8,128)(2,1)} %bitcast.12, f32[1,32]{1,0:T(1,128)} %bitcast.16, bf16[32,256]{1,0:T(8,128)(2,1)} %bitcast.13, ...), custom_call_target="tpu_custom_call" | custom-call | tf_op jit(solution)/shard_map/pallas_call | solution.py:206
  1.7 0.0 copy-start
  1.7 11.4 %all_to_all.11 = bf16[16,8,1024]{2,1,0:T(8,128)(2,1)S(1)} all-to-all(bf16[16,8,1024]{2,1,0:T(8,128)(2,1)S(1)} %bitcast.11), channel_id=1, replica_groups={{27,0,1,2,3,8,9,10,11,16,17,18,19,24,25,26},{31,4,5,6,7,12,13,14,15,20,..., dimensions={0} | all-to-all | bytes 524288 | tf_op jit(solution)/shard_map/all_to_all | solution.py:241
  13.1 0.0 copy-done
  13.1 0.6 %shard_map.93 = bf16[128,128]{1,0:T(8,128)(2,1)S(1)} custom-call(bf16[128,1024]{1,0:T(8,128)(2,1)S(1)} %bitcast.9, bf16[1024,128]{1,0:T(8,128)(2,1)S(1)} %copy-done), custom_call_target="tpu_custom_call" | custom-call | flops 67108864 | bytes 524288 | tf_op jit(solution)/shard_map/pallas_call | solution.py:252
  13.7 2.4 %collective-permute-start = (bf16[128,128]{1,0:T(8,128)(2,1)S(1)}, bf16[128,128]{1,0:T(8,128)(2,1)S(1)}, u32[]{:S(2)}, u32[]{:S(2)}) collective-permute-start(bf16[128,128]{1,0:T(8,128)(2,1)S(1)} %shard_map.93), channel_id=1, source_target_pairs={{0,5},{1,4},{2,7},{3,6},{4,1},{5,0},{6,3},{7,2},{8,13},{9,12},{10,... | collective-permute-start | bytes 98312 | tf_op jit(solution)/shard_map/ppermute | solution.py:274
  16.1 0.6 %shard_map.92.mine_ref = f32[128,128]{1,0:T(8,128)S(1)} custom-call(bf16[128,1024]{1,0:T(8,128)(2,1)S(1)} %bitcast.10, bf16[1024,128]{1,0:T(8,128)(2,1)S(1)} %copy-done), custom_call_target="tpu_custom_call" | custom-call | flops 67108864 | bytes 524288 | tf_op jit(solution)/shard_map/pallas_call | solution.py:252
  16.8 1.3 %collective-permute-done.came_ref = bf16[128,128]{1,0:T(8,128)(2,1)S(1)} collective-permute-done((bf16[128,128]{1,0:T(8,128)(2,1)S(1)}, bf16[128,128]{1,0:T(8,128)(2,1)S(1)}, u32[]{:S(2)}, u32[]{:S(2)}) %collective-permute-start) | collective-permute-done | bytes 32800 | tf_op jit(solution)/shard_map/ppermute | solution.py:274
  18.1 0.6 %shard_map.94 = bf16[8,16,128]{2,1,0:T(8,128)(2,1)} custom-call(f32[128,128]{1,0:T(8,128)S(1)} %shard_map.92.mine_ref, bf16[128,128]{1,0:T(8,128)(2,1)S(1)} %collective-permute-done.came_ref, f32[1,128]{1,0:T(1,128)S(1)} %get-tuple-element.8.bias_ref), custom_call_target="tpu_custom_call" | custom-call | tf_op jit(solution)/shard_map/pallas_call | solution.py:276
Async XLA Ops:
  1.7 11.4 %copy-start = (bf16[1024,128]{1,0:T(8,128)(2,1)S(1)}, bf16[1024,128]{1,0:T(8,128)(2,1)}, u32[]{:S(2)}) copy-start(bf16[1024,128]{1,0:T(8,128)(2,1)} %weight_ref.3) | copy-start | bytes 786436
  13.7 4.4 %collective-permute-start = (bf16[128,128]{1,0:T(8,128)(2,1)S(1)}, bf16[128,128]{1,0:T(8,128)(2,1)S(1)}, u32[]{:S(2)}, u32[]{:S(2)}) collective-permute-start(bf16[128,128]{1,0:T(8,128)(2,1)S(1)} %shard_map.93), channel_id=1, source_target_pairs={{0,5},{1,4},{2,7},{3,6},{4,1},{5,0},{6,3},{7,2},{8,13},{9,12},{10,... | collective-permute-start | bytes 98312 | tf_op jit(solution)/shard_map/ppermute | solution.py:274

commit v14 on v13

--- a/solution.py
+++ b/solution.py
@@ -12,7 +12,7 @@
 
 
 def peer_order(seq_count, rest_count):
-    peers = [(b, a) for b in range(seq_count) for a in range(rest_count)]
+    peers = [(b, a) for a in range(rest_count) for b in range(seq_count)]
     return peers[-1:] + peers[:-1]
 
 
@@ -45,13 +45,11 @@
     left_ref,
     sems,
 ):
-    step = max(1, align_ref.shape[0] // 4)
-    cuts = [pl.ds(at, step) for at in range(0, align_ref.shape[0], step)]
     copies = [
         pltpu.make_async_copy(source, target, sems.at[n])
         for n, (source, target) in enumerate(
-            [(align_hbm.at[cut], align_ref.at[cut]) for cut in cuts]
-            + [
+            [
+                (align_hbm, align_ref),
                 (gain_hbm, gain_ref),
                 (offset_hbm, offset_ref),
                 (left_w_hbm, left_w_ref),
@@ -62,8 +60,8 @@
             ]
         )
     ]
-    for n, copy in enumerate(copies):
-        copy.start(priority=n % 2)
+    for copy in copies:
+        copy.start()
     for copy in copies:
         copy.wait()
     rows, res_total, chan = align_ref.shape
@@ -113,7 +111,7 @@
     split = row_block * hidden
     left = recv_ref[:, :split] if own else recv_ref[:, split : 2 * split]
     right = recv_ref[:, 2 * split :]
-    turned = left.astype(jnp.float32).T
+    turned = left.T.astype(jnp.float32)
     parts = left_ref.shape[0]
     for n in range(parts):
         left_ref[n] = turned[:, n * LANES : (n + 1) * LANES]
@@ -221,7 +219,7 @@
             pltpu.VMEM((1, hidden), jnp.float32),
             pltpu.VMEM((rows * res_total, LANES), jnp.float32),
             pltpu.VMEM((half_count * rest_count, rows, row_block * hidden), jnp.float32),
-            pltpu.SemaphoreType.DMA((7 + rows // max(1, rows // 4),)),
+            pltpu.SemaphoreType.DMA((8,)),
         ],
         compiler_params=params,
     )(

time: 18.9 us -> 19.1 us (1.011)
  the two profiles are of different devices: /device:TPU:0 before, /device:TPU:1 now
where the time goes in v14:
time: 19.1 us; the launch traced here: 18.9 us
  blocking collectives  11 us (58%)
  Pallas kernels  3.46 us (18%)
  starting transfers between devices  2.66 us (14%)
  waiting for transfers between devices  1.8 us (9%)
    all_to_all x1, blocking collectives, body(): lax.all_to_all(send, ('seq', 'half', 'rest'), split_axis=0, concat_axis=0...  11 us
    ppermute x1, starting transfers between devices, body(): came = lax.ppermute(theirs, ('half', 'rest'), swap)  2.66 us
    ppermute x1, waiting for transfers between devices, body(): came = lax.ppermute(theirs, ('half', 'rest'), swap)  1.8 us
    pallas_call x1, Pallas kernels, body(): pl.pallas_call(functools.partial(project_kernel, seq_count, half_count, r...  1.62 us
    pallas_call x2, Pallas kernels, pair_block(): pl.pallas_call(functools.partial(pair_kernel, own, hidden, row_block, col...  1.2 us
    pallas_call x1, Pallas kernels, body(): pl.pallas_call(add_kernel, out_shape=jax.ShapeDtypeStruct((row_block, col...  0.64 us
  transfers between devices with their start and end apart: 1, of which 1 were waited for; matrix products, arithmetic and copies ran while one was open for 0% of the time, Pallas kernels for 3%

profile of v14, /device:TPU:1, one launch (start us, length us, event | category | flops | bytes accessed | tf_op | source)
XLA Modules:
  0.0 18.9 jit_solution(7368457648812563548)
XLA Ops:
  0.0 1.6 %shard_map.91 = (bf16[128,1024]{1,0:T(8,128)(2,1)S(1)}, f32[1,128]{1,0:T(1,128)S(1)}) custom-call(bf16[8,64,256]{2,1,0:T(8,128)(2,1)} %align_hbm.1, f32[1,256]{1,0:T(1,128)} %bitcast.14, f32[1,256]{1,0:T(1,128)} %bitcast.15, bf16[32,256]{1,0:T(8,128)(2,1)} %bitcast.12, f32[1,32]{1,0:T(1,128)} %bitcast.16, bf16[32,256]{1,0:T(8,128)(2,1)} %bitcast.13, ...), custom_call_target="tpu_custom_call" | custom-call | tf_op jit(solution)/shard_map/pallas_call | solution.py:204
  1.6 0.0 copy-start
  1.6 11.0 %all_to_all.11 = bf16[16,8,1024]{2,1,0:T(8,128)(2,1)S(1)} all-to-all(bf16[16,8,1024]{2,1,0:T(8,128)(2,1)S(1)} %bitcast.11), channel_id=1, replica_groups={{27,0,8,16,24,1,9,17,25,2,10,18,26,3,11,19},{31,4,12,20,28,5,13,21,29,6..., dimensions={0} | all-to-all | bytes 524288 | tf_op jit(solution)/shard_map/all_to_all | solution.py:239
  12.6 0.0 copy-done
  12.6 0.6 %shard_map.93 = bf16[128,128]{1,0:T(8,128)(2,1)S(1)} custom-call(bf16[128,1024]{1,0:T(8,128)(2,1)S(1)} %bitcast.9, bf16[1024,128]{1,0:T(8,128)(2,1)S(1)} %copy-done), custom_call_target="tpu_custom_call" | custom-call | flops 67108864 | bytes 524288 | tf_op jit(solution)/shard_map/pallas_call | solution.py:250
  13.2 2.7 %collective-permute-start = (bf16[128,128]{1,0:T(8,128)(2,1)S(1)}, bf16[128,128]{1,0:T(8,128)(2,1)S(1)}, u32[]{:S(2)}, u32[]{:S(2)}) collective-permute-start(bf16[128,128]{1,0:T(8,128)(2,1)S(1)} %shard_map.93), channel_id=1, source_target_pairs={{0,5},{1,4},{2,7},{3,6},{4,1},{5,0},{6,3},{7,2},{8,13},{9,12},{10,... | collective-permute-start | bytes 98312 | tf_op jit(solution)/shard_map/ppermute | solution.py:272
  15.9 0.6 %shard_map.92.mine_ref = f32[128,128]{1,0:T(8,128)S(1)} custom-call(bf16[128,1024]{1,0:T(8,128)(2,1)S(1)} %bitcast.10, bf16[1024,128]{1,0:T(8,128)(2,1)S(1)} %copy-done), custom_call_target="tpu_custom_call" | custom-call | flops 67108864 | bytes 524288 | tf_op jit(solution)/shard_map/pallas_call | solution.py:250
  16.5 1.8 %collective-permute-done.came_ref = bf16[128,128]{1,0:T(8,128)(2,1)S(1)} collective-permute-done((bf16[128,128]{1,0:T(8,128)(2,1)S(1)}, bf16[128,128]{1,0:T(8,128)(2,1)S(1)}, u32[]{:S(2)}, u32[]{:S(2)}) %collective-permute-start) | collective-permute-done | bytes 32800 | tf_op jit(solution)/shard_map/ppermute | solution.py:272
  18.3 0.6 %shard_map.94 = bf16[8,16,128]{2,1,0:T(8,128)(2,1)} custom-call(f32[128,128]{1,0:T(8,128)S(1)} %shard_map.92.mine_ref, bf16[128,128]{1,0:T(8,128)(2,1)S(1)} %collective-permute-done.came_ref, f32[1,128]{1,0:T(1,128)S(1)} %get-tuple-element.8.bias_ref), custom_call_target="tpu_custom_call" | custom-call | tf_op jit(solution)/shard_map/pallas_call | solution.py:274
Async XLA Ops:
  1.6 11.0 %copy-start = (bf16[1024,128]{1,0:T(8,128)(2,1)S(1)}, bf16[1024,128]{1,0:T(8,128)(2,1)}, u32[]{:S(2)}) copy-start(bf16[1024,128]{1,0:T(8,128)(2,1)} %weight_ref.3) | copy-start | bytes 786436
  13.2 5.1 %collective-permute-start = (bf16[128,128]{1,0:T(8,128)(2,1)S(1)}, bf16[128,128]{1,0:T(8,128)(2,1)S(1)}, u32[]{:S(2)}, u32[]{:S(2)}) collective-permute-start(bf16[128,128]{1,0:T(8,128)(2,1)S(1)} %shard_map.93), channel_id=1, source_target_pairs={{0,5},{1,4},{2,7},{3,6},{4,1},{5,0},{6,3},{7,2},{8,13},{9,12},{10,... | collective-permute-start | bytes 98312 | tf_op jit(solution)/shard_map/ppermute | solution.py:272

commit v15 on v14

--- a/solution.py
+++ b/solution.py
@@ -12,8 +12,8 @@
 
 
 def peer_order(seq_count, rest_count):
-    peers = [(b, a) for a in range(rest_count) for b in range(seq_count)]
-    return peers[-1:] + peers[:-1]
+    peers = [(b, a) for b in range(seq_count) for a in range(rest_count)]
+    return peers[:-3:-1] + peers[:-2]
 
 
 def partner(at, rest_count):
@@ -66,21 +66,23 @@
         copy.wait()
     rows, res_total, chan = align_ref.shape
     hidden = left_w_ref.shape[0]
+    weights = jnp.concatenate([left_w_ref[...], right_w_ref[...]], axis=0)
+    scaled = (weights.astype(jnp.float32) * gain_ref[...]).astype(jnp.bfloat16)
+    inner = (((1,), (1,)), ((), ()))
+    offset = jnp.broadcast_to(offset_ref[...], (8, chan))
+    high = offset.astype(jnp.bfloat16)
+    low = (offset - high.astype(jnp.float32)).astype(jnp.bfloat16)
+    shift = (
+        lax.dot_general(high, weights, inner, preferred_element_type=jnp.float32)
+        + lax.dot_general(low, weights, inner, preferred_element_type=jnp.float32)
+    )[:1] + jnp.concatenate([left_b_ref[...], right_b_ref[...]], axis=1)
     values = align_ref[...].astype(jnp.float32).reshape(rows * res_total, chan)
     centred = values - jnp.mean(values, axis=-1, keepdims=True)
     spread = jnp.mean(centred * centred, axis=-1, keepdims=True)
-    normed = centred * lax.rsqrt(spread + 1e-05) * gain_ref[...] + offset_ref[...]
-    weights = jnp.concatenate([left_w_ref[...], right_w_ref[...]], axis=0)
-    biases = jnp.concatenate([left_b_ref[...], right_b_ref[...]], axis=1)
-    proj_ref[:, : 2 * hidden] = (
-        lax.dot_general(
-            normed.astype(jnp.bfloat16),
-            weights,
-            (((1,), (1,)), ((), ())),
-            preferred_element_type=jnp.float32,
-        )
-        + biases
+    product = lax.dot_general(
+        centred.astype(jnp.bfloat16), scaled, inner, preferred_element_type=jnp.float32
     )
+    proj_ref[:, : 2 * hidden] = product * lax.rsqrt(spread + 1e-05) + shift
     tiles = [proj_ref[pl.ds(r, rows, stride=res_total), :][:, : 2 * hidden] for r in range(res_total)]
     row_block = res_total // (half_count * rest_count)
     col_block = res_total // seq_count
@@ -96,14 +98,23 @@
     half = lax.axis_index("half")
     own = [left_ref[half * rest_count + a] for a in range(rest_count)]
     other = [left_ref[(1 - half) * rest_count + partner(a, rest_count)] for a in range(rest_count)]
-    pieces = [
-        jnp.concatenate([own[a], other[a], right[b]], axis=1)
-        for b, a in peer_order(seq_count, rest_count)
-    ]
+    lefts = [jnp.concatenate([own[a], other[a]], axis=1) for a in range(rest_count)]
+    peers = peer_order(seq_count, rest_count)
+    split = lefts[0].shape[1]
     group = max(1, 16 // rows)
-    for start in range(0, len(pieces), group):
-        block = jnp.concatenate(pieces[start : start + group], axis=0)
-        send_ref[pl.ds(start * rows, group * rows), :] = block.astype(jnp.bfloat16)
+    packed = {}
+
+    def pack(blocks, picks):
+        if picks not in packed:
+            block = jnp.concatenate([blocks[at] for _, at in picks], axis=0)
+            packed[picks] = block.astype(jnp.bfloat16)
+        return packed[picks]
+
+    for start in range(0, len(peers), group):
+        block = peers[start : start + group]
+        place = pl.ds(start * rows, group * rows)
+        send_ref[place, :split] = pack(lefts, tuple(("left", a) for _, a in block))
+        send_ref[place, split:] = pack(right, tuple(("right", b) for b, _ in block))
 
 
 def pair_kernel(own, hidden, row_block, col_block, recv_ref, weight_ref, out_ref, left_ref):

time: 19.1 us -> 18.7 us (0.979)
  the two profiles are of different devices: /device:TPU:1 before, /device:TPU:0 now
where the time goes in v15:
time: 18.7 us; the launch traced here: 18.6 us
  blocking collectives  11.4 us (61%)
  Pallas kernels  3.37 us (18%)
  starting transfers between devices  2.37 us (13%)
  waiting for transfers between devices  1.38 us (7%)
    all_to_all x1, blocking collectives, body(): lax.all_to_all(send, ('seq', 'half', 'rest'), split_axis=0, concat_axis=0...  11.4 us
    ppermute x1, starting transfers between devices, body(): came = lax.ppermute(theirs, ('half', 'rest'), swap)  2.37 us
    pallas_call x1, Pallas kernels, body(): pl.pallas_call(functools.partial(project_kernel, seq_count, half_count, r...  1.54 us
    ppermute x1, waiting for transfers between devices, body(): came = lax.ppermute(theirs, ('half', 'rest'), swap)  1.38 us
    pallas_call x2, Pallas kernels, pair_block(): pl.pallas_call(functools.partial(pair_kernel, own, hidden, row_block, col...  1.2 us
    pallas_call x1, Pallas kernels, body(): pl.pallas_call(add_kernel, out_shape=jax.ShapeDtypeStruct((row_block, col...  0.64 us
  transfers between devices with their start and end apart: 1, of which 1 were waited for; matrix products, arithmetic and copies ran while one was open for 0% of the time, Pallas kernels for 3%

profile of v15, /device:TPU:0, one launch (start us, length us, event | category | flops | bytes accessed | tf_op | source)
XLA Modules:
  0.0 18.6 jit_solution(5501885879840051918)
XLA Ops:
  0.0 1.5 %shard_map.91 = (bf16[128,1024]{1,0:T(8,128)(2,1)S(1)}, f32[1,128]{1,0:T(1,128)S(1)}) custom-call(bf16[8,64,256]{2,1,0:T(8,128)(2,1)} %align_hbm.1, f32[1,256]{1,0:T(1,128)} %bitcast.14, f32[1,256]{1,0:T(1,128)} %bitcast.15, bf16[32,256]{1,0:T(8,128)(2,1)} %bitcast.12, f32[1,32]{1,0:T(1,128)} %bitcast.16, bf16[32,256]{1,0:T(8,128)(2,1)} %bitcast.13, ...), custom_call_target="tpu_custom_call" | custom-call | tf_op jit(solution)/shard_map/pallas_call | solution.py:215
  1.5 0.0 copy-start
  1.6 11.4 %all_to_all.11 = bf16[16,8,1024]{2,1,0:T(8,128)(2,1)S(1)} all-to-all(bf16[16,8,1024]{2,1,0:T(8,128)(2,1)S(1)} %bitcast.11), channel_id=1, replica_groups={{27,26,0,1,2,3,8,9,10,11,16,17,18,19,24,25},{31,30,4,5,6,7,12,13,14,15,..., dimensions={0} | all-to-all | bytes 524288 | tf_op jit(solution)/shard_map/all_to_all | solution.py:250
  13.0 0.0 copy-done
  13.0 0.6 %shard_map.93 = bf16[128,128]{1,0:T(8,128)(2,1)S(1)} custom-call(bf16[128,1024]{1,0:T(8,128)(2,1)S(1)} %bitcast.9, bf16[1024,128]{1,0:T(8,128)(2,1)S(1)} %copy-done), custom_call_target="tpu_custom_call" | custom-call | flops 67108864 | bytes 524288 | tf_op jit(solution)/shard_map/pallas_call | solution.py:261
  13.6 2.4 %collective-permute-start = (bf16[128,128]{1,0:T(8,128)(2,1)S(1)}, bf16[128,128]{1,0:T(8,128)(2,1)S(1)}, u32[]{:S(2)}, u32[]{:S(2)}) collective-permute-start(bf16[128,128]{1,0:T(8,128)(2,1)S(1)} %shard_map.93), channel_id=1, source_target_pairs={{0,5},{1,4},{2,7},{3,6},{4,1},{5,0},{6,3},{7,2},{8,13},{9,12},{10,... | collective-permute-start | bytes 98312 | tf_op jit(solution)/shard_map/ppermute | solution.py:283
  16.0 0.6 %shard_map.92.mine_ref = f32[128,128]{1,0:T(8,128)S(1)} custom-call(bf16[128,1024]{1,0:T(8,128)(2,1)S(1)} %bitcast.10, bf16[1024,128]{1,0:T(8,128)(2,1)S(1)} %copy-done), custom_call_target="tpu_custom_call" | custom-call | flops 67108864 | bytes 524288 | tf_op jit(solution)/shard_map/pallas_call | solution.py:261
  16.6 1.4 %collective-permute-done.came_ref = bf16[128,128]{1,0:T(8,128)(2,1)S(1)} collective-permute-done((bf16[128,128]{1,0:T(8,128)(2,1)S(1)}, bf16[128,128]{1,0:T(8,128)(2,1)S(1)}, u32[]{:S(2)}, u32[]{:S(2)}) %collective-permute-start) | collective-permute-done | bytes 32800 | tf_op jit(solution)/shard_map/ppermute | solution.py:283
  17.9 0.6 %shard_map.94 = bf16[8,16,128]{2,1,0:T(8,128)(2,1)} custom-call(f32[128,128]{1,0:T(8,128)S(1)} %shard_map.92.mine_ref, bf16[128,128]{1,0:T(8,128)(2,1)S(1)} %collective-permute-done.came_ref, f32[1,128]{1,0:T(1,128)S(1)} %get-tuple-element.8.bias_ref), custom_call_target="tpu_custom_call" | custom-call | tf_op jit(solution)/shard_map/pallas_call | solution.py:285
Async XLA Ops:
  1.5 11.4 %copy-start = (bf16[1024,128]{1,0:T(8,128)(2,1)S(1)}, bf16[1024,128]{1,0:T(8,128)(2,1)}, u32[]{:S(2)}) copy-start(bf16[1024,128]{1,0:T(8,128)(2,1)} %weight_ref.3) | copy-start | bytes 786436
  13.6 4.4 %collective-permute-start = (bf16[128,128]{1,0:T(8,128)(2,1)S(1)}, bf16[128,128]{1,0:T(8,128)(2,1)S(1)}, u32[]{:S(2)}, u32[]{:S(2)}) collective-permute-start(bf16[128,128]{1,0:T(8,128)(2,1)S(1)} %shard_map.93), channel_id=1, source_target_pairs={{0,5},{1,4},{2,7},{3,6},{4,1},{5,0},{6,3},{7,2},{8,13},{9,12},{10,... | collective-permute-start | bytes 98312 | tf_op jit(solution)/shard_map/ppermute | solution.py:283

commit v16 on v15

--- a/solution.py
+++ b/solution.py
@@ -12,8 +12,8 @@
 
 
 def peer_order(seq_count, rest_count):
-    peers = [(b, a) for b in range(seq_count) for a in range(rest_count)]
-    return peers[:-3:-1] + peers[:-2]
+    peers = [(b, a) for a in range(rest_count) for b in range(seq_count)]
+    return peers[-1:] + peers[:-1]
 
 
 def partner(at, rest_count):
@@ -31,9 +31,7 @@
     left_b_hbm,
     right_w_hbm,
     right_b_hbm,
-    out_b_hbm,
     send_ref,
-    out_b_ref,
     align_ref,
     gain_ref,
     offset_ref,
@@ -56,7 +54,6 @@
                 (left_b_hbm, left_b_ref),
                 (right_w_hbm, right_w_ref),
                 (right_b_hbm, right_b_ref),
-                (out_b_hbm, out_b_ref),
             ]
         )
     ]
@@ -117,7 +114,7 @@
         send_ref[place, split:] = pack(right, tuple(("right", b) for b, _ in block))
 
 
-def pair_kernel(own, hidden, row_block, col_block, recv_ref, weight_ref, out_ref, left_ref):
+def pair_terms(own, hidden, row_block, col_block, recv_ref, weight_ref, left_ref):
     seqs = recv_ref.shape[0]
     split = row_block * hidden
     left = recv_ref[:, :split] if own else recv_ref[:, split : 2 * split]
@@ -161,7 +158,40 @@
         rows += [jnp.concatenate(line, axis=1) for line in lines]
     flat = jnp.concatenate(rows, axis=0)
     term = jnp.dot(flat, weight_ref[...], preferred_element_type=jnp.float32)
-    out_ref[...] = (term * (1.0 / float(2 * seqs))).astype(out_ref.dtype)
+    return term * (1.0 / float(2 * seqs))
+
+
+def swaps_late():
+    return (lax.axis_index("seq") == 0) & (lax.axis_index("rest") // 2 % 2 == 1)
+
+
+def theirs_kernel(sizes, recv_ref, weight_ref, theirs_ref, early_ref, left_ref):
+    @pl.when(swaps_late())
+    def _():
+        early_ref[...] = pair_terms(True, *sizes, recv_ref, weight_ref, left_ref)
+
+    theirs_ref[...] = pair_terms(False, *sizes, recv_ref, weight_ref, left_ref).astype(
+        theirs_ref.dtype
+    )
+
+
+def mine_kernel(
+    sizes, recv_ref, weight_ref, early_ref, bias_hbm, mine_ref, left_ref, bias_ref, sem
+):
+    bias = pltpu.make_async_copy(bias_hbm, bias_ref, sem)
+    bias.start()
+    late = swaps_late()
+
+    @pl.when(late)
+    def _():
+        mine_ref[...] = early_ref[...]
+
+    @pl.when(jnp.logical_not(late))
+    def _():
+        mine_ref[...] = pair_terms(True, *sizes, recv_ref, weight_ref, left_ref)
+
+    bias.wait()
+    mine_ref[...] += bias_ref[...]
 
 
 def roll_blocks(tile, count, hidden):
@@ -176,9 +206,9 @@
     ]
 
 
-def add_kernel(mine_ref, came_ref, bias_ref, out_ref, term_ref):
+def add_kernel(mine_ref, came_ref, out_ref, term_ref):
     row_block, col_block, _ = out_ref.shape
-    term_ref[...] = mine_ref[...] + came_ref[...].astype(jnp.float32) + bias_ref[...]
+    term_ref[...] = mine_ref[...] + came_ref[...].astype(jnp.float32)
     for i in range(row_block):
         out_ref[i] = term_ref[pl.ds(i, col_block, stride=row_block), :].astype(jnp.bfloat16)
 
@@ -212,14 +242,11 @@
     vmem = pl.BlockSpec(memory_space=pltpu.VMEM)
     hbm = pl.BlockSpec(memory_space=pltpu.HBM)
     params = pltpu.CompilerParams(vmem_limit_bytes=32 * 1024 * 1024)
-    send, bias_row = pl.pallas_call(
+    send = pl.pallas_call(
         functools.partial(project_kernel, seq_count, half_count, rest_count),
-        out_shape=[
-            jax.ShapeDtypeStruct((peers * rows, width), jnp.bfloat16),
-            jax.ShapeDtypeStruct((1, pair_width), jnp.float32),
-        ],
-        in_specs=[hbm] * 8,
-        out_specs=[vmem] * 2,
+        out_shape=jax.ShapeDtypeStruct((peers * rows, width), jnp.bfloat16),
+        in_specs=[hbm] * 7,
+        out_specs=vmem,
         scratch_shapes=[
             pltpu.VMEM((rows, res_total, chan), jnp.bfloat16),
             pltpu.VMEM((1, chan), jnp.float32),
@@ -230,7 +257,7 @@
             pltpu.VMEM((1, hidden), jnp.float32),
             pltpu.VMEM((rows * res_total, LANES), jnp.float32),
             pltpu.VMEM((half_count * rest_count, rows, row_block * hidden), jnp.float32),
-            pltpu.SemaphoreType.DMA((8,)),
+            pltpu.SemaphoreType.DMA((7,)),
         ],
         compiler_params=params,
     )(
@@ -241,7 +268,6 @@
         in_hbm(left_bias.reshape(1, hidden)),
         in_hbm(right_projection_weight.T),
         in_hbm(right_bias.reshape(1, hidden)),
-        in_hbm(out_bias.reshape(1, pair_width)),
     )
     groups = [
         [(b * half_count + h) * rest_count + a for b, a in peer_order(seq_count, rest_count)]
@@ -255,41 +281,51 @@
         tiled=True,
         axis_index_groups=groups,
     )
+    sizes = (hidden, row_block, col_block)
     outer_values = pairs * hidden * hidden
-
-    def pair_block(own, dtype):
-        return pl.pallas_call(
-            functools.partial(pair_kernel, own, hidden, row_block, col_block),
-            out_shape=jax.ShapeDtypeStruct((pairs, pair_width), dtype),
-            in_specs=[vmem] * 2,
-            out_specs=vmem,
-            scratch_shapes=[
-                pltpu.VMEM((recv.shape[0] // LANES, row_block * hidden, LANES), jnp.float32)
-            ],
-            compiler_params=params,
-            cost_estimate=pl.CostEstimate(
-                flops=2 * outer_values * (recv.shape[0] + pair_width),
-                bytes_accessed=2 * (recv.size + out_weight.size),
-                transcendentals=0,
-            ),
-        )(recv, out_weight)
-
-    theirs = pair_block(False, jnp.bfloat16)
+    cost = pl.CostEstimate(
+        flops=2 * outer_values * (recv.shape[0] + pair_width),
+        bytes_accessed=2 * (recv.size + out_weight.size),
+        transcendentals=0,
+    )
+    turned = pltpu.VMEM((recv.shape[0] // LANES, row_block * hidden, LANES), jnp.float32)
+    term = jax.ShapeDtypeStruct((pairs, pair_width), jnp.float32)
+    theirs, early = pl.pallas_call(
+        functools.partial(theirs_kernel, sizes),
+        out_shape=[jax.ShapeDtypeStruct((pairs, pair_width), jnp.bfloat16), term],
+        in_specs=[vmem] * 2,
+        out_specs=[vmem] * 2,
+        scratch_shapes=[turned],
+        compiler_params=params,
+        cost_estimate=cost,
+    )(recv, out_weight)
     swap = [
         (h * rest_count + q, (1 - h) * rest_count + partner(q, rest_count))
         for h in range(half_count)
         for q in range(rest_count)
     ]
     came = lax.ppermute(theirs, ("half", "rest"), swap)
-    mine = pair_block(True, jnp.float32)
+    mine = pl.pallas_call(
+        functools.partial(mine_kernel, sizes),
+        out_shape=term,
+        in_specs=[vmem, vmem, vmem, hbm],
+        out_specs=vmem,
+        scratch_shapes=[
+            turned,
+            pltpu.VMEM((1, pair_width), jnp.float32),
+            pltpu.SemaphoreType.DMA,
+        ],
+        compiler_params=params,
+        cost_estimate=cost,
+    )(recv, out_weight, early, in_hbm(out_bias.reshape(1, pair_width)))
     return pl.pallas_call(
         add_kernel,
         out_shape=jax.ShapeDtypeStruct((row_block, col_block, pair_width), jnp.bfloat16),
-        in_specs=[vmem] * 3,
+        in_specs=[vmem] * 2,
         out_specs=vmem,
         scratch_shapes=[pltpu.VMEM((pairs, pair_width), jnp.float32)],
         compiler_params=params,
-    )(mine, came, bias_row)
+    )(mine, came)
 
 
 def solution(mesh):

time: 18.7 us -> 18.7 us (level)
  transfers between devices with their start and end apart: 1 -> 1, of which waited for: 1 -> 1; matrix products, arithmetic and copies ran while one was open for 0% -> 0% of each run, Pallas kernels for 3% -> 4%
where the time goes in v16:
time: 18.7 us; the launch traced here: 18.5 us
  blocking collectives  11.3 us (60%)
  Pallas kernels  3.43 us (18%)
  starting transfers between devices  2.37 us (13%)
  waiting for transfers between devices  1.32 us (7%)
    all_to_all x1, blocking collectives, body(): lax.all_to_all(send, ('seq', 'half', 'rest'), split_axis=0, concat_axis=0...  11.3 us
    ppermute x1, starting transfers between devices, body(): came = lax.ppermute(theirs, ('half', 'rest'), swap)  2.37 us
    pallas_call x1, Pallas kernels, body(): pl.pallas_call(functools.partial(project_kernel, seq_count, half_count, r...  1.52 us
    ppermute x1, waiting for transfers between devices, body(): came = lax.ppermute(theirs, ('half', 'rest'), swap)  1.32 us
    pallas_call x1, Pallas kernels, body(): pl.pallas_call(functools.partial(mine_kernel, sizes), out_shape=term, in_...  0.67 us
    pallas_call x1, Pallas kernels, body(): pl.pallas_call(add_kernel, out_shape=jax.ShapeDtypeStruct((row_block, col...  0.64 us
    pallas_call x1, Pallas kernels, body(): pl.pallas_call(functools.partial(theirs_kernel, sizes), out_shape=[jax.Sh...  0.6 us
  transfers between devices with their start and end apart: 1, of which 1 were waited for; matrix products, arithmetic and copies ran while one was open for 0% of the time, Pallas kernels for 4%

profile of v16, /device:TPU:0, one launch (start us, length us, event | category | flops | bytes accessed | tf_op | source)
XLA Modules:
  0.0 18.5 jit_solution(17278894250290080144)
XLA Ops:
  0.0 1.5 %shard_map.91 = bf16[128,1024]{1,0:T(8,128)(2,1)S(1)} custom-call(bf16[8,64,256]{2,1,0:T(8,128)(2,1)} %align_hbm.1, f32[1,256]{1,0:T(1,128)} %bitcast.14, f32[1,256]{1,0:T(1,128)} %bitcast.15, bf16[32,256]{1,0:T(8,128)(2,1)} %bitcast.12, f32[1,32]{1,0:T(1,128)} %bitcast.16, bf16[32,256]{1,0:T(8,128)(2,1)} %bitcast.13, f32[1,32]{1,0:T(1,128)} %bitcast.17), custom_call_target="tpu_custom_call" | custom-call | tf_op jit(solution)/shard_map/pallas_call | solution.py:245
  1.5 0.0 copy-start
  1.5 11.3 %all_to_all.11 = bf16[16,8,1024]{2,1,0:T(8,128)(2,1)S(1)} all-to-all(bf16[16,8,1024]{2,1,0:T(8,128)(2,1)S(1)} %bitcast.11), channel_id=1, replica_groups={{27,0,8,16,24,1,9,17,25,2,10,18,26,3,11,19},{31,4,12,20,28,5,13,21,29,6..., dimensions={0} | all-to-all | bytes 524288 | tf_op jit(solution)/shard_map/all_to_all | solution.py:276
  12.9 0.0 copy-done
  12.9 0.6 %shard_map.92 = (bf16[128,128]{1,0:T(8,128)(2,1)S(1)}, f32[128,128]{1,0:T(8,128)S(1)}) custom-call(bf16[128,1024]{1,0:T(8,128)(2,1)S(1)} %bitcast.9, bf16[1024,128]{1,0:T(8,128)(2,1)S(1)} %copy-done), custom_call_target="tpu_custom_call" | custom-call | flops 67108864 | bytes 524288 | tf_op jit(solution)/shard_map/pallas_call | solution.py:293
  13.5 2.4 %collective-permute-start = (bf16[128,128]{1,0:T(8,128)(2,1)S(1)}, bf16[128,128]{1,0:T(8,128)(2,1)S(1)}, u32[]{:S(2)}, u32[]{:S(2)}) collective-permute-start(bf16[128,128]{1,0:T(8,128)(2,1)S(1)} %get-tuple-element.8), channel_id=1, source_target_pairs={{0,5},{1,4},{2,7},{3,6},{4,1},{5,0},{6,3},{7,2},{8,13},{9,12},{10,... | collective-permute-start | bytes 98312 | tf_op jit(solution)/shard_map/ppermute | solution.py:307
  15.9 0.7 %shard_map.93.mine_ref = f32[128,128]{1,0:T(8,128)S(1)} custom-call(bf16[128,1024]{1,0:T(8,128)(2,1)S(1)} %bitcast.10, bf16[1024,128]{1,0:T(8,128)(2,1)S(1)} %copy-done, f32[128,128]{1,0:T(8,128)S(1)} %get-tuple-element.7.early_ref, f32[1,128]{1,0:T(1,128)} %bitcast.18), custom_call_target="tpu_custom_call" | custom-call | flops 67108864 | bytes 524288 | tf_op jit(solution)/shard_map/pallas_call | solution.py:308
  16.5 1.3 %collective-permute-done.came_ref = bf16[128,128]{1,0:T(8,128)(2,1)S(1)} collective-permute-done((bf16[128,128]{1,0:T(8,128)(2,1)S(1)}, bf16[128,128]{1,0:T(8,128)(2,1)S(1)}, u32[]{:S(2)}, u32[]{:S(2)}) %collective-permute-start) | collective-permute-done | bytes 32800 | tf_op jit(solution)/shard_map/ppermute | solution.py:307
  17.8 0.6 %shard_map.94 = bf16[8,16,128]{2,1,0:T(8,128)(2,1)} custom-call(f32[128,128]{1,0:T(8,128)S(1)} %shard_map.93.mine_ref, bf16[128,128]{1,0:T(8,128)(2,1)S(1)} %collective-permute-done.came_ref), custom_call_target="tpu_custom_call" | custom-call | tf_op jit(solution)/shard_map/pallas_call | solution.py:321
Async XLA Ops:
  1.5 11.3 %copy-start = (bf16[1024,128]{1,0:T(8,128)(2,1)S(1)}, bf16[1024,128]{1,0:T(8,128)(2,1)}, u32[]{:S(2)}) copy-start(bf16[1024,128]{1,0:T(8,128)(2,1)} %weight_ref.3) | copy-start | bytes 786436
  13.5 4.4 %collective-permute-start = (bf16[128,128]{1,0:T(8,128)(2,1)S(1)}, bf16[128,128]{1,0:T(8,128)(2,1)S(1)}, u32[]{:S(2)}, u32[]{:S(2)}) collective-permute-start(bf16[128,128]{1,0:T(8,128)(2,1)S(1)} %get-tuple-element.8), channel_id=1, source_target_pairs={{0,5},{1,4},{2,7},{3,6},{4,1},{5,0},{6,3},{7,2},{8,13},{9,12},{10,... | collective-permute-start | bytes 98312 | tf_op jit(solution)/shard_map/ppermute | solution.py:307

commit v17 on v16

--- a/solution.py
+++ b/solution.py
@@ -63,7 +63,8 @@
         copy.wait()
     rows, res_total, chan = align_ref.shape
     hidden = left_w_ref.shape[0]
-    weights = jnp.concatenate([left_w_ref[...], right_w_ref[...]], axis=0)
+    copies_of = LANES // (2 * hidden)
+    weights = jnp.concatenate([left_w_ref[...], right_w_ref[...]] * copies_of, axis=0)
     scaled = (weights.astype(jnp.float32) * gain_ref[...]).astype(jnp.bfloat16)
     inner = (((1,), (1,)), ((), ()))
     offset = jnp.broadcast_to(offset_ref[...], (8, chan))
@@ -72,26 +73,40 @@
     shift = (
         lax.dot_general(high, weights, inner, preferred_element_type=jnp.float32)
         + lax.dot_general(low, weights, inner, preferred_element_type=jnp.float32)
-    )[:1] + jnp.concatenate([left_b_ref[...], right_b_ref[...]], axis=1)
+    )[:1] + jnp.concatenate([left_b_ref[...], right_b_ref[...]] * copies_of, axis=1)
     values = align_ref[...].astype(jnp.float32).reshape(rows * res_total, chan)
     centred = values - jnp.mean(values, axis=-1, keepdims=True)
     spread = jnp.mean(centred * centred, axis=-1, keepdims=True)
     product = lax.dot_general(
         centred.astype(jnp.bfloat16), scaled, inner, preferred_element_type=jnp.float32
     )
-    proj_ref[:, : 2 * hidden] = product * lax.rsqrt(spread + 1e-05) + shift
-    tiles = [proj_ref[pl.ds(r, rows, stride=res_total), :][:, : 2 * hidden] for r in range(res_total)]
+    proj_ref[...] = product * lax.rsqrt(spread + 1e-05) + shift
+    tiles = [proj_ref[pl.ds(r, rows, stride=res_total), :] for r in range(res_total)]
+    moved = {}
+    lane_block = lax.broadcasted_iota(jnp.int32, (rows, LANES), 1) // hidden
+    per_group = LANES // hidden
+
+    def lined_up(side, residues):
+        lines = []
+        for at in range(0, len(residues), per_group):
+            line = None
+            for p, r in enumerate(residues[at : at + per_group]):
+                if (p - side) % 2 == 0:
+                    tile = tiles[r]
+                else:
+                    if r not in moved:
+                        moved[r] = pltpu.roll(tiles[r], hidden, 1)
+                    tile = moved[r]
+                line = tile if line is None else jnp.where(lane_block == p, tile, line)
+            lines.append(line)
+        return jnp.concatenate(lines, axis=1)
+
     row_block = res_total // (half_count * rest_count)
     col_block = res_total // seq_count
+    order = column_order(col_block, per_group)
     for a in range(half_count * rest_count):
-        left_ref[a] = jnp.concatenate(
-            [t[:, :hidden] for t in tiles[a * row_block : (a + 1) * row_block]], axis=1
-        )
-    order = column_order(col_block, LANES // hidden)
-    right = [
-        jnp.concatenate([tiles[b * col_block + j][:, hidden:] for j in order], axis=1)
-        for b in range(seq_count)
-    ]
+        left_ref[a] = lined_up(0, [a * row_block + i for i in range(row_block)])
+    right = [lined_up(1, [b * col_block + j for j in order]) for b in range(seq_count)]
     half = lax.axis_index("half")
     own = [left_ref[half * rest_count + a] for a in range(rest_count)]
     other = [left_ref[(1 - half) * rest_count + partner(a, rest_count)] for a in range(rest_count)]

time: 18.7 us -> 18.6 us (level)
  no operation moved by 1% of the time
where the time goes in v17:
time: 18.6 us; the launch traced here: 18.4 us
  blocking collectives  11.3 us (61%)
  Pallas kernels  3.39 us (18%)
  starting transfers between devices  2.37 us (13%)
  waiting for transfers between devices  1.32 us (7%)
    all_to_all x1, blocking collectives, body(): lax.all_to_all(send, ('seq', 'half', 'rest'), split_axis=0, concat_axis=0...  11.3 us
    ppermute x1, starting transfers between devices, body(): came = lax.ppermute(theirs, ('half', 'rest'), swap)  2.37 us
    pallas_call x1, Pallas kernels, body(): pl.pallas_call(functools.partial(project_kernel, seq_count, half_count, r...  1.48 us
    ppermute x1, waiting for transfers between devices, body(): came = lax.ppermute(theirs, ('half', 'rest'), swap)  1.32 us
    pallas_call x1, Pallas kernels, body(): pl.pallas_call(functools.partial(mine_kernel, sizes), out_shape=term, in_...  0.67 us
    pallas_call x1, Pallas kernels, body(): pl.pallas_call(add_kernel, out_shape=jax.ShapeDtypeStruct((row_block, col...  0.64 us
    pallas_call x1, Pallas kernels, body(): pl.pallas_call(functools.partial(theirs_kernel, sizes), out_shape=[jax.Sh...  0.6 us
  transfers between devices with their start and end apart: 1, of which 1 were waited for; matrix products, arithmetic and copies ran while one was open for 0% of the time, Pallas kernels for 4%

profile of v17, /device:TPU:0, one launch (start us, length us, event | category | flops | bytes accessed | tf_op | source)
XLA Modules:
  0.0 18.4 jit_solution(8356034116725183230)
XLA Ops:
  0.0 1.5 %shard_map.91 = bf16[128,1024]{1,0:T(8,128)(2,1)S(1)} custom-call(bf16[8,64,256]{2,1,0:T(8,128)(2,1)} %align_hbm.1, f32[1,256]{1,0:T(1,128)} %bitcast.14, f32[1,256]{1,0:T(1,128)} %bitcast.15, bf16[32,256]{1,0:T(8,128)(2,1)} %bitcast.12, f32[1,32]{1,0:T(1,128)} %bitcast.16, bf16[32,256]{1,0:T(8,128)(2,1)} %bitcast.13, f32[1,32]{1,0:T(1,128)} %bitcast.17), custom_call_target="tpu_custom_call" | custom-call | tf_op jit(solution)/shard_map/pallas_call | solution.py:260
  1.5 0.0 copy-start
  1.5 11.3 %all_to_all.11 = bf16[16,8,1024]{2,1,0:T(8,128)(2,1)S(1)} all-to-all(bf16[16,8,1024]{2,1,0:T(8,128)(2,1)S(1)} %bitcast.11), channel_id=1, replica_groups={{27,0,8,16,24,1,9,17,25,2,10,18,26,3,11,19},{31,4,12,20,28,5,13,21,29,6..., dimensions={0} | all-to-all | bytes 524288 | tf_op jit(solution)/shard_map/all_to_all | solution.py:291
  12.8 0.0 copy-done
  12.8 0.6 %shard_map.92 = (bf16[128,128]{1,0:T(8,128)(2,1)S(1)}, f32[128,128]{1,0:T(8,128)S(1)}) custom-call(bf16[128,1024]{1,0:T(8,128)(2,1)S(1)} %bitcast.9, bf16[1024,128]{1,0:T(8,128)(2,1)S(1)} %copy-done), custom_call_target="tpu_custom_call" | custom-call | flops 67108864 | bytes 524288 | tf_op jit(solution)/shard_map/pallas_call | solution.py:308
  13.4 2.4 %collective-permute-start = (bf16[128,128]{1,0:T(8,128)(2,1)S(1)}, bf16[128,128]{1,0:T(8,128)(2,1)S(1)}, u32[]{:S(2)}, u32[]{:S(2)}) collective-permute-start(bf16[128,128]{1,0:T(8,128)(2,1)S(1)} %get-tuple-element.8), channel_id=1, source_target_pairs={{0,5},{1,4},{2,7},{3,6},{4,1},{5,0},{6,3},{7,2},{8,13},{9,12},{10,... | collective-permute-start | bytes 98312 | tf_op jit(solution)/shard_map/ppermute | solution.py:322
  15.8 0.7 %shard_map.93.mine_ref = f32[128,128]{1,0:T(8,128)S(1)} custom-call(bf16[128,1024]{1,0:T(8,128)(2,1)S(1)} %bitcast.10, bf16[1024,128]{1,0:T(8,128)(2,1)S(1)} %copy-done, f32[128,128]{1,0:T(8,128)S(1)} %get-tuple-element.7.early_ref, f32[1,128]{1,0:T(1,128)} %bitcast.18), custom_call_target="tpu_custom_call" | custom-call | flops 67108864 | bytes 524288 | tf_op jit(solution)/shard_map/pallas_call | solution.py:323
  16.5 1.3 %collective-permute-done.came_ref = bf16[128,128]{1,0:T(8,128)(2,1)S(1)} collective-permute-done((bf16[128,128]{1,0:T(8,128)(2,1)S(1)}, bf16[128,128]{1,0:T(8,128)(2,1)S(1)}, u32[]{:S(2)}, u32[]{:S(2)}) %collective-permute-start) | collective-permute-done | bytes 32800 | tf_op jit(solution)/shard_map/ppermute | solution.py:322
  17.8 0.6 %shard_map.94 = bf16[8,16,128]{2,1,0:T(8,128)(2,1)} custom-call(f32[128,128]{1,0:T(8,128)S(1)} %shard_map.93.mine_ref, bf16[128,128]{1,0:T(8,128)(2,1)S(1)} %collective-permute-done.came_ref), custom_call_target="tpu_custom_call" | custom-call | tf_op jit(solution)/shard_map/pallas_call | solution.py:336
Async XLA Ops:
  1.5 11.3 %copy-start = (bf16[1024,128]{1,0:T(8,128)(2,1)S(1)}, bf16[1024,128]{1,0:T(8,128)(2,1)}, u32[]{:S(2)}) copy-start(bf16[1024,128]{1,0:T(8,128)(2,1)} %weight_ref.3) | copy-start | bytes 786436
  13.4 4.4 %collective-permute-start = (bf16[128,128]{1,0:T(8,128)(2,1)S(1)}, bf16[128,128]{1,0:T(8,128)(2,1)S(1)}, u32[]{:S(2)}, u32[]{:S(2)}) collective-permute-start(bf16[128,128]{1,0:T(8,128)(2,1)S(1)} %get-tuple-element.8), channel_id=1, source_target_pairs={{0,5},{1,4},{2,7},{3,6},{4,1},{5,0},{6,3},{7,2},{8,13},{9,12},{10,... | collective-permute-start | bytes 98312 | tf_op jit(solution)/shard_map/ppermute | solution.py:322

commit v18 on v17

--- a/solution.py
+++ b/solution.py
@@ -221,9 +221,10 @@
     ]
 
 
-def add_kernel(mine_ref, came_ref, out_ref, term_ref):
+def add_kernel(mine_ref, down_ref, up_ref, out_ref, term_ref):
     row_block, col_block, _ = out_ref.shape
-    term_ref[...] = mine_ref[...] + came_ref[...].astype(jnp.float32)
+    came = down_ref[...].astype(jnp.float32) + up_ref[...].astype(jnp.float32)
+    term_ref[...] = mine_ref[...] + came
     for i in range(row_block):
         out_ref[i] = term_ref[pl.ds(i, col_block, stride=row_block), :].astype(jnp.bfloat16)
 
@@ -314,12 +315,9 @@
         compiler_params=params,
         cost_estimate=cost,
     )(recv, out_weight)
-    swap = [
-        (h * rest_count + q, (1 - h) * rest_count + partner(q, rest_count))
-        for h in range(half_count)
-        for q in range(rest_count)
-    ]
-    came = lax.ppermute(theirs, ("half", "rest"), swap)
+    downward = [(rest_count + q, partner(q, rest_count)) for q in range(rest_count)]
+    came_down = lax.ppermute(theirs, ("half", "rest"), downward)
+    came_up = lax.ppermute(theirs, ("half", "rest"), [(low, high) for high, low in downward])
     mine = pl.pallas_call(
         functools.partial(mine_kernel, sizes),
         out_shape=term,
@@ -336,11 +334,11 @@
     return pl.pallas_call(
         add_kernel,
         out_shape=jax.ShapeDtypeStruct((row_block, col_block, pair_width), jnp.bfloat16),
-        in_specs=[vmem] * 2,
+        in_specs=[vmem] * 3,
         out_specs=vmem,
         scratch_shapes=[pltpu.VMEM((pairs, pair_width), jnp.float32)],
         compiler_params=params,
-    )(mine, came)
+    )(mine, came_down, came_up)
 
 
 def solution(mesh):

time: 18.6 us -> 24.6 us (1.32)
  starting transfers between devices: 2.37 us -> 5.5 us
  waiting for transfers between devices: 1.32 us -> 4.14 us
    ppermute x1 -> x2, starting transfers between devices: 2.37 us -> 5.5 us  [the longest x1 4.21 us: body(): lax.ppermute(theirs, ('half', 'rest'), [(low, high) for high, low in down...]
    ppermute x1 -> x2, waiting for transfers between devices: 1.32 us -> 4.14 us  [the longest x1 4.14 us: body(): came_down = lax.ppermute(theirs, ('half', 'rest'), downward)]
  transfers between devices with their start and end apart: 1 -> 2, of which waited for: 1 -> 1; matrix products, arithmetic and copies ran while one was open for 0% -> 0% of each run, Pallas kernels for 4% -> 3%
where the time goes in v18:
time: 24.6 us; the launch traced here: 24.4 us
  blocking collectives  11.3 us (46%)
  starting transfers between devices  5.5 us (22%)
  waiting for transfers between devices  4.14 us (17%)
  Pallas kernels  3.4 us (14%)
    all_to_all x1, blocking collectives, body(): lax.all_to_all(send, ('seq', 'half', 'rest'), split_axis=0, concat_axis=0...  11.3 us
    ppermute x1, starting transfers between devices, body(): lax.ppermute(theirs, ('half', 'rest'), [(low, high) for high, low in down...  4.21 us
    ppermute x1, waiting for transfers between devices, body(): came_down = lax.ppermute(theirs, ('half', 'rest'), downward)  4.14 us
    pallas_call x1, Pallas kernels, body(): pl.pallas_call(functools.partial(project_kernel, seq_count, half_count, r...  1.48 us
    ppermute x1, starting transfers between devices, body(): came_down = lax.ppermute(theirs, ('half', 'rest'), downward)  1.29 us
    pallas_call x1, Pallas kernels, body(): pl.pallas_call(functools.partial(mine_kernel, sizes), out_shape=term, in_...  0.67 us
    pallas_call x1, Pallas kernels, body(): pl.pallas_call(add_kernel, out_shape=jax.ShapeDtypeStruct((row_block, col...  0.64 us
    pallas_call x1, Pallas kernels, body(): pl.pallas_call(functools.partial(theirs_kernel, sizes), out_shape=[jax.Sh...  0.6 us
  transfers between devices with their start and end apart: 2, of which 1 were waited for; matrix products, arithmetic and copies ran while one was open for 0% of the time, Pallas kernels for 3%

profile of v18, /device:TPU:0, one launch (start us, length us, event | category | flops | bytes accessed | tf_op | source)
XLA Modules:
  0.0 24.4 jit_solution(5448263017679255531)
XLA Ops:
  0.0 1.5 %shard_map.91 = bf16[128,1024]{1,0:T(8,128)(2,1)S(1)} custom-call(bf16[8,64,256]{2,1,0:T(8,128)(2,1)} %align_hbm.1, f32[1,256]{1,0:T(1,128)} %bitcast.14, f32[1,256]{1,0:T(1,128)} %bitcast.15, bf16[32,256]{1,0:T(8,128)(2,1)} %bitcast.12, f32[1,32]{1,0:T(1,128)} %bitcast.16, bf16[32,256]{1,0:T(8,128)(2,1)} %bitcast.13, f32[1,32]{1,0:T(1,128)} %bitcast.17), custom_call_target="tpu_custom_call" | custom-call | tf_op jit(solution)/shard_map/pallas_call | solution.py:261
  1.5 0.0 copy-start
  1.5 11.3 %all_to_all.11 = bf16[16,8,1024]{2,1,0:T(8,128)(2,1)S(1)} all-to-all(bf16[16,8,1024]{2,1,0:T(8,128)(2,1)S(1)} %bitcast.11), channel_id=1, replica_groups={{27,0,8,16,24,1,9,17,25,2,10,18,26,3,11,19},{31,4,12,20,28,5,13,21,29,6..., dimensions={0} | all-to-all | bytes 524288 | tf_op jit(solution)/shard_map/all_to_all | solution.py:292
  12.8 0.0 copy-done
  12.8 0.6 %shard_map.92 = (bf16[128,128]{1,0:T(8,128)(2,1)S(1)}, f32[128,128]{1,0:T(8,128)S(1)}) custom-call(bf16[128,1024]{1,0:T(8,128)(2,1)S(1)} %bitcast.9, bf16[1024,128]{1,0:T(8,128)(2,1)S(1)} %copy-done), custom_call_target="tpu_custom_call" | custom-call | flops 67108864 | bytes 524288 | tf_op jit(solution)/shard_map/pallas_call | solution.py:309
  13.4 4.2 %collective-permute-start.1 = (bf16[128,128]{1,0:T(8,128)(2,1)S(1)}, bf16[128,128]{1,0:T(8,128)(2,1)S(1)}, u32[]{:S(2)}, u32[]{:S(2)}) collective-permute-start(bf16[128,128]{1,0:T(8,128)(2,1)S(1)} %get-tuple-element.8), channel_id=1, source_target_pairs={{1,4},{0,5},{3,6},{2,7},{9,12},{8,13},{11,14},{10,15},{17,20},{16,... | collective-permute-start | bytes 98312 | tf_op jit(solution)/shard_map/ppermute | solution.py:320
  17.7 1.3 %collective-permute-start = (bf16[128,128]{1,0:T(8,128)(2,1)S(1)}, bf16[128,128]{1,0:T(8,128)(2,1)S(1)}, u32[]{:S(2)}, u32[]{:S(2)}) collective-permute-start(bf16[128,128]{1,0:T(8,128)(2,1)S(1)} %get-tuple-element.8), channel_id=1, source_target_pairs={{4,1},{5,0},{6,3},{7,2},{12,9},{13,8},{14,11},{15,10},{20,17},{21,... | collective-permute-start | bytes 98312 | tf_op jit(solution)/shard_map/ppermute | solution.py:319
  19.0 0.7 %shard_map.93.mine_ref = f32[128,128]{1,0:T(8,128)S(1)} custom-call(bf16[128,1024]{1,0:T(8,128)(2,1)S(1)} %bitcast.10, bf16[1024,128]{1,0:T(8,128)(2,1)S(1)} %copy-done, f32[128,128]{1,0:T(8,128)S(1)} %get-tuple-element.7.early_ref, f32[1,128]{1,0:T(1,128)} %bitcast.18), custom_call_target="tpu_custom_call" | custom-call | flops 67108864 | bytes 524288 | tf_op jit(solution)/shard_map/pallas_call | solution.py:321
  19.6 0.0 collective-permute-done.1.up_ref
  19.7 4.1 %collective-permute-done.down_ref = bf16[128,128]{1,0:T(8,128)(2,1)S(1)} collective-permute-done((bf16[128,128]{1,0:T(8,128)(2,1)S(1)}, bf16[128,128]{1,0:T(8,128)(2,1)S(1)}, u32[]{:S(2)}, u32[]{:S(2)}) %collective-permute-start) | collective-permute-done | bytes 32800 | tf_op jit(solution)/shard_map/ppermute | solution.py:319
  23.8 0.6 %shard_map.94 = bf16[8,16,128]{2,1,0:T(8,128)(2,1)} custom-call(f32[128,128]{1,0:T(8,128)S(1)} %shard_map.93.mine_ref, bf16[128,128]{1,0:T(8,128)(2,1)S(1)} %collective-permute-done.down_ref, bf16[128,128]{1,0:T(8,128)(2,1)S(1)} %collective-permute-done.1.up_ref), custom_call_target="tpu_custom_call" | custom-call | tf_op jit(solution)/shard_map/pallas_call | solution.py:334
Async XLA Ops:
  1.5 11.3 %copy-start = (bf16[1024,128]{1,0:T(8,128)(2,1)S(1)}, bf16[1024,128]{1,0:T(8,128)(2,1)}, u32[]{:S(2)}) copy-start(bf16[1024,128]{1,0:T(8,128)(2,1)} %weight_ref.3) | copy-start | bytes 786436
  13.4 6.2 %collective-permute-start.1 = (bf16[128,128]{1,0:T(8,128)(2,1)S(1)}, bf16[128,128]{1,0:T(8,128)(2,1)S(1)}, u32[]{:S(2)}, u32[]{:S(2)}) collective-permute-start(bf16[128,128]{1,0:T(8,128)(2,1)S(1)} %get-tuple-element.8), channel_id=1, source_target_pairs={{1,4},{0,5},{3,6},{2,7},{9,12},{8,13},{11,14},{10,15},{17,20},{16,... | collective-permute-start | bytes 98312 | tf_op jit(solution)/shard_map/ppermute | solution.py:320
  17.7 6.1 %collective-permute-start = (bf16[128,128]{1,0:T(8,128)(2,1)S(1)}, bf16[128,128]{1,0:T(8,128)(2,1)S(1)}, u32[]{:S(2)}, u32[]{:S(2)}) collective-permute-start(bf16[128,128]{1,0:T(8,128)(2,1)S(1)} %get-tuple-element.8), channel_id=1, source_target_pairs={{4,1},{5,0},{6,3},{7,2},{12,9},{13,8},{14,11},{15,10},{20,17},{21,... | collective-permute-start | bytes 98312 | tf_op jit(solution)/shard_map/ppermute | solution.py:319

commit v19 on v17

--- a/solution.py
+++ b/solution.py
@@ -74,13 +74,19 @@
         lax.dot_general(high, weights, inner, preferred_element_type=jnp.float32)
         + lax.dot_general(low, weights, inner, preferred_element_type=jnp.float32)
     )[:1] + jnp.concatenate([left_b_ref[...], right_b_ref[...]] * copies_of, axis=1)
-    values = align_ref[...].astype(jnp.float32).reshape(rows * res_total, chan)
-    centred = values - jnp.mean(values, axis=-1, keepdims=True)
-    spread = jnp.mean(centred * centred, axis=-1, keepdims=True)
+    flat, factors = [], []
+    for row in range(rows):
+        values = align_ref[row].astype(jnp.float32)
+        centred = values - jnp.mean(values, axis=-1, keepdims=True)
+        spread = jnp.mean(centred * centred, axis=-1, keepdims=True)
+        flat.append(centred.astype(jnp.bfloat16))
+        factors.append(lax.rsqrt(spread + 1e-05))
     product = lax.dot_general(
-        centred.astype(jnp.bfloat16), scaled, inner, preferred_element_type=jnp.float32
-    )
-    proj_ref[...] = product * lax.rsqrt(spread + 1e-05) + shift
+        jnp.concatenate(flat, axis=0), scaled, inner, preferred_element_type=jnp.float32
+    )
+    for row, factor in enumerate(factors):
+        place = slice(row * res_total, (row + 1) * res_total)
+        proj_ref[place, :] = product[place] * factor + shift
     tiles = [proj_ref[pl.ds(r, rows, stride=res_total), :] for r in range(res_total)]
     moved = {}
     lane_block = lax.broadcasted_iota(jnp.int32, (rows, LANES), 1) // hidden
@@ -147,11 +153,13 @@
         ],
         axis=0,
     ).astype(jnp.bfloat16)
-    outer = jnp.dot(left, right, preferred_element_type=jnp.float32)
     per_group = LANES // hidden
     lane_block = lax.broadcasted_iota(jnp.int32, (2 * row_block, LANES), 1) // hidden
     rows = []
     for g in range(0, col_block // per_group, 2):
+        outer = jnp.dot(
+            left, right[:, g * LANES : (g + 2) * LANES], preferred_element_type=jnp.float32
+        )
         lines = [[] for _ in range(per_group)]
         for c in range(0, hidden, per_group):
             rolled = []
@@ -159,7 +167,7 @@
                 at = (c + k) * row_block
                 tile = jnp.concatenate(
                     [
-                        outer[at : at + row_block, (g + h) * LANES : (g + h + 1) * LANES]
+                        outer[at : at + row_block, h * LANES : (h + 1) * LANES]
                         for h in range(2)
                     ],
                     axis=0,

time: 18.6 us -> 18.6 us (level)
  no operation moved by 1% of the time
where the time goes in v19:
time: 18.6 us; the launch traced here: 18.4 us
  blocking collectives  11.3 us (61%)
  Pallas kernels  3.39 us (18%)
  starting transfers between devices  2.37 us (13%)
  waiting for transfers between devices  1.32 us (7%)
    all_to_all x1, blocking collectives, body(): lax.all_to_all(send, ('seq', 'half', 'rest'), split_axis=0, concat_axis=0...  11.3 us
    ppermute x1, starting transfers between devices, body(): came = lax.ppermute(theirs, ('half', 'rest'), swap)  2.37 us
    pallas_call x1, Pallas kernels, body(): pl.pallas_call(functools.partial(project_kernel, seq_count, half_count, r...  1.48 us
    ppermute x1, waiting for transfers between devices, body(): came = lax.ppermute(theirs, ('half', 'rest'), swap)  1.32 us
    pallas_call x1, Pallas kernels, body(): pl.pallas_call(functools.partial(mine_kernel, sizes), out_shape=term, in_...  0.67 us
    pallas_call x1, Pallas kernels, body(): pl.pallas_call(add_kernel, out_shape=jax.ShapeDtypeStruct((row_block, col...  0.64 us
    pallas_call x1, Pallas kernels, body(): pl.pallas_call(functools.partial(theirs_kernel, sizes), out_shape=[jax.Sh...  0.6 us
  transfers between devices with their start and end apart: 1, of which 1 were waited for; matrix products, arithmetic and copies ran while one was open for 0% of the time, Pallas kernels for 4%

profile of v19, /device:TPU:0, one launch (start us, length us, event | category | flops | bytes accessed | tf_op | source)
XLA Modules:
  0.0 18.4 jit_solution(7795007055174155335)
XLA Ops:
  0.0 1.5 %shard_map.91 = bf16[128,1024]{1,0:T(8,128)(2,1)S(1)} custom-call(bf16[8,64,256]{2,1,0:T(8,128)(2,1)} %align_hbm.1, f32[1,256]{1,0:T(1,128)} %bitcast.14, f32[1,256]{1,0:T(1,128)} %bitcast.15, bf16[32,256]{1,0:T(8,128)(2,1)} %bitcast.12, f32[1,32]{1,0:T(1,128)} %bitcast.16, bf16[32,256]{1,0:T(8,128)(2,1)} %bitcast.13, f32[1,32]{1,0:T(1,128)} %bitcast.17), custom_call_target="tpu_custom_call" | custom-call | tf_op jit(solution)/shard_map/pallas_call | solution.py:268
  1.5 0.0 copy-start
  1.5 11.3 %all_to_all.11 = bf16[16,8,1024]{2,1,0:T(8,128)(2,1)S(1)} all-to-all(bf16[16,8,1024]{2,1,0:T(8,128)(2,1)S(1)} %bitcast.11), channel_id=1, replica_groups={{27,0,8,16,24,1,9,17,25,2,10,18,26,3,11,19},{31,4,12,20,28,5,13,21,29,6..., dimensions={0} | all-to-all | bytes 524288 | tf_op jit(solution)/shard_map/all_to_all | solution.py:299
  12.8 0.0 copy-done
  12.8 0.6 %shard_map.92 = (bf16[128,128]{1,0:T(8,128)(2,1)S(1)}, f32[128,128]{1,0:T(8,128)S(1)}) custom-call(bf16[128,1024]{1,0:T(8,128)(2,1)S(1)} %bitcast.9, bf16[1024,128]{1,0:T(8,128)(2,1)S(1)} %copy-done), custom_call_target="tpu_custom_call" | custom-call | flops 67108864 | bytes 524288 | tf_op jit(solution)/shard_map/pallas_call | solution.py:316
  13.4 2.4 %collective-permute-start = (bf16[128,128]{1,0:T(8,128)(2,1)S(1)}, bf16[128,128]{1,0:T(8,128)(2,1)S(1)}, u32[]{:S(2)}, u32[]{:S(2)}) collective-permute-start(bf16[128,128]{1,0:T(8,128)(2,1)S(1)} %get-tuple-element.8), channel_id=1, source_target_pairs={{0,5},{1,4},{2,7},{3,6},{4,1},{5,0},{6,3},{7,2},{8,13},{9,12},{10,... | collective-permute-start | bytes 98312 | tf_op jit(solution)/shard_map/ppermute | solution.py:330
  15.8 0.7 %shard_map.93.mine_ref = f32[128,128]{1,0:T(8,128)S(1)} custom-call(bf16[128,1024]{1,0:T(8,128)(2,1)S(1)} %bitcast.10, bf16[1024,128]{1,0:T(8,128)(2,1)S(1)} %copy-done, f32[128,128]{1,0:T(8,128)S(1)} %get-tuple-element.7.early_ref, f32[1,128]{1,0:T(1,128)} %bitcast.18), custom_call_target="tpu_custom_call" | custom-call | flops 67108864 | bytes 524288 | tf_op jit(solution)/shard_map/pallas_call | solution.py:331
  16.5 1.3 %collective-permute-done.came_ref = bf16[128,128]{1,0:T(8,128)(2,1)S(1)} collective-permute-done((bf16[128,128]{1,0:T(8,128)(2,1)S(1)}, bf16[128,128]{1,0:T(8,128)(2,1)S(1)}, u32[]{:S(2)}, u32[]{:S(2)}) %collective-permute-start) | collective-permute-done | bytes 32800 | tf_op jit(solution)/shard_map/ppermute | solution.py:330
  17.8 0.6 %shard_map.94 = bf16[8,16,128]{2,1,0:T(8,128)(2,1)} custom-call(f32[128,128]{1,0:T(8,128)S(1)} %shard_map.93.mine_ref, bf16[128,128]{1,0:T(8,128)(2,1)S(1)} %collective-permute-done.came_ref), custom_call_target="tpu_custom_call" | custom-call | tf_op jit(solution)/shard_map/pallas_call | solution.py:344
Async XLA Ops:
  1.5 11.3 %copy-start = (bf16[1024,128]{1,0:T(8,128)(2,1)S(1)}, bf16[1024,128]{1,0:T(8,128)(2,1)}, u32[]{:S(2)}) copy-start(bf16[1024,128]{1,0:T(8,128)(2,1)} %weight_ref.3) | copy-start | bytes 786436
  13.4 4.4 %collective-permute-start = (bf16[128,128]{1,0:T(8,128)(2,1)S(1)}, bf16[128,128]{1,0:T(8,128)(2,1)S(1)}, u32[]{:S(2)}, u32[]{:S(2)}) collective-permute-start(bf16[128,128]{1,0:T(8,128)(2,1)S(1)} %get-tuple-element.8), channel_id=1, source_target_pairs={{0,5},{1,4},{2,7},{3,6},{4,1},{5,0},{6,3},{7,2},{8,13},{9,12},{10,... | collective-permute-start | bytes 98312 | tf_op jit(solution)/shard_map/ppermute | solution.py:330

commit v20 on v19

--- a/solution.py
+++ b/solution.py
@@ -59,13 +59,13 @@
     ]
     for copy in copies:
         copy.start()
-    for copy in copies:
+    for copy in copies[1:]:
         copy.wait()
     rows, res_total, chan = align_ref.shape
     hidden = left_w_ref.shape[0]
     copies_of = LANES // (2 * hidden)
     weights = jnp.concatenate([left_w_ref[...], right_w_ref[...]] * copies_of, axis=0)
-    scaled = (weights.astype(jnp.float32) * gain_ref[...]).astype(jnp.bfloat16)
+    scaled = (weights.astype(jnp.float32) * gain_ref[...]).astype(jnp.bfloat16).T
     inner = (((1,), (1,)), ((), ()))
     offset = jnp.broadcast_to(offset_ref[...], (8, chan))
     high = offset.astype(jnp.bfloat16)
@@ -74,6 +74,7 @@
         lax.dot_general(high, weights, inner, preferred_element_type=jnp.float32)
         + lax.dot_general(low, weights, inner, preferred_element_type=jnp.float32)
     )[:1] + jnp.concatenate([left_b_ref[...], right_b_ref[...]] * copies_of, axis=1)
+    copies[0].wait()
     flat, factors = [], []
     for row in range(rows):
         values = align_ref[row].astype(jnp.float32)
@@ -81,8 +82,8 @@
         spread = jnp.mean(centred * centred, axis=-1, keepdims=True)
         flat.append(centred.astype(jnp.bfloat16))
         factors.append(lax.rsqrt(spread + 1e-05))
-    product = lax.dot_general(
-        jnp.concatenate(flat, axis=0), scaled, inner, preferred_element_type=jnp.float32
+    product = jnp.dot(
+        jnp.concatenate(flat, axis=0), scaled, preferred_element_type=jnp.float32
     )
     for row, factor in enumerate(factors):
         place = slice(row * res_total, (row + 1) * res_total)
@@ -229,11 +230,19 @@
     ]
 
 
-def add_kernel(mine_ref, came_ref, out_ref, term_ref):
+def add_kernel(mine_ref, came_ref, out_hbm, term_ref, out_ref, sems):
     row_block, col_block, _ = out_ref.shape
     term_ref[...] = mine_ref[...] + came_ref[...].astype(jnp.float32)
-    for i in range(row_block):
-        out_ref[i] = term_ref[pl.ds(i, col_block, stride=row_block), :].astype(jnp.bfloat16)
+    step = max(1, row_block // 2)
+    copies = []
+    for n, at in enumerate(range(0, row_block, step)):
+        for i in range(at, at + step):
+            out_ref[i] = term_ref[pl.ds(i, col_block, stride=row_block), :].astype(jnp.bfloat16)
+        part = pl.ds(at, step)
+        copies.append(pltpu.make_async_copy(out_ref.at[part], out_hbm.at[part], sems.at[n]))
+        copies[-1].start()
+    for copy in copies:
+        copy.wait()
 
 
 def in_hbm(array):
@@ -345,8 +354,12 @@
         add_kernel,
         out_shape=jax.ShapeDtypeStruct((row_block, col_block, pair_width), jnp.bfloat16),
         in_specs=[vmem] * 2,
-        out_specs=vmem,
-        scratch_shapes=[pltpu.VMEM((pairs, pair_width), jnp.float32)],
+        out_specs=hbm,
+        scratch_shapes=[
+            pltpu.VMEM((pairs, pair_width), jnp.float32),
+            pltpu.VMEM((row_block, col_block, pair_width), jnp.bfloat16),
+            pltpu.SemaphoreType.DMA((2,)),
+        ],
         compiler_params=params,
     )(mine, came)
 

time: 18.6 us -> 18.7 us (level)
  no operation moved by 1% of the time
where the time goes in v20:
time: 18.7 us; the launch traced here: 18.5 us
  blocking collectives  11.3 us (60%)
  Pallas kernels  3.46 us (19%)
  starting transfers between devices  2.37 us (13%)
  waiting for transfers between devices  1.32 us (7%)
    all_to_all x1, blocking collectives, body(): lax.all_to_all(send, ('seq', 'half', 'rest'), split_axis=0, concat_axis=0...  11.3 us
    ppermute x1, starting transfers between devices, body(): came = lax.ppermute(theirs, ('half', 'rest'), swap)  2.37 us
    pallas_call x1, Pallas kernels, body(): pl.pallas_call(functools.partial(project_kernel, seq_count, half_count, r...  1.54 us
    ppermute x1, waiting for transfers between devices, body(): came = lax.ppermute(theirs, ('half', 'rest'), swap)  1.32 us
    pallas_call x1, Pallas kernels, body(): pl.pallas_call(functools.partial(mine_kernel, sizes), out_shape=term, in_...  0.67 us
    pallas_call x1, Pallas kernels, body(): pl.pallas_call(add_kernel, out_shape=jax.ShapeDtypeStruct((row_block, col...  0.65 us
    pallas_call x1, Pallas kernels, body(): pl.pallas_call(functools.partial(theirs_kernel, sizes), out_shape=[jax.Sh...  0.6 us
  transfers between devices with their start and end apart: 1, of which 1 were waited for; matrix products, arithmetic and copies ran while one was open for 0% of the time, Pallas kernels for 4%

profile of v20, /device:TPU:0, one launch (start us, length us, event | category | flops | bytes accessed | tf_op | source)
XLA Modules:
  0.0 18.5 jit_solution(7218903927641232818)
XLA Ops:
  0.0 1.5 %shard_map.91 = bf16[128,1024]{1,0:T(8,128)(2,1)S(1)} custom-call(bf16[8,64,256]{2,1,0:T(8,128)(2,1)} %align_hbm.1, f32[1,256]{1,0:T(1,128)} %bitcast.14, f32[1,256]{1,0:T(1,128)} %bitcast.15, bf16[32,256]{1,0:T(8,128)(2,1)} %bitcast.12, f32[1,32]{1,0:T(1,128)} %bitcast.16, bf16[32,256]{1,0:T(8,128)(2,1)} %bitcast.13, f32[1,32]{1,0:T(1,128)} %bitcast.17), custom_call_target="tpu_custom_call" | custom-call | tf_op jit(solution)/shard_map/pallas_call | solution.py:277
  1.6 0.0 copy-start
  1.6 11.3 %all_to_all.11 = bf16[16,8,1024]{2,1,0:T(8,128)(2,1)S(1)} all-to-all(bf16[16,8,1024]{2,1,0:T(8,128)(2,1)S(1)} %bitcast.11), channel_id=1, replica_groups={{27,0,8,16,24,1,9,17,25,2,10,18,26,3,11,19},{31,4,12,20,28,5,13,21,29,6..., dimensions={0} | all-to-all | bytes 524288 | tf_op jit(solution)/shard_map/all_to_all | solution.py:308
  12.9 0.0 copy-done
  12.9 0.6 %shard_map.92 = (bf16[128,128]{1,0:T(8,128)(2,1)S(1)}, f32[128,128]{1,0:T(8,128)S(1)}) custom-call(bf16[128,1024]{1,0:T(8,128)(2,1)S(1)} %bitcast.9, bf16[1024,128]{1,0:T(8,128)(2,1)S(1)} %copy-done), custom_call_target="tpu_custom_call" | custom-call | flops 67108864 | bytes 524288 | tf_op jit(solution)/shard_map/pallas_call | solution.py:325
  13.5 2.4 %collective-permute-start = (bf16[128,128]{1,0:T(8,128)(2,1)S(1)}, bf16[128,128]{1,0:T(8,128)(2,1)S(1)}, u32[]{:S(2)}, u32[]{:S(2)}) collective-permute-start(bf16[128,128]{1,0:T(8,128)(2,1)S(1)} %get-tuple-element.8), channel_id=1, source_target_pairs={{0,5},{1,4},{2,7},{3,6},{4,1},{5,0},{6,3},{7,2},{8,13},{9,12},{10,... | collective-permute-start | bytes 98312 | tf_op jit(solution)/shard_map/ppermute | solution.py:339
  15.9 0.7 %shard_map.93.mine_ref = f32[128,128]{1,0:T(8,128)S(1)} custom-call(bf16[128,1024]{1,0:T(8,128)(2,1)S(1)} %bitcast.10, bf16[1024,128]{1,0:T(8,128)(2,1)S(1)} %copy-done, f32[128,128]{1,0:T(8,128)S(1)} %get-tuple-element.7.early_ref, f32[1,128]{1,0:T(1,128)} %bitcast.18), custom_call_target="tpu_custom_call" | custom-call | flops 67108864 | bytes 524288 | tf_op jit(solution)/shard_map/pallas_call | solution.py:340
  16.5 1.3 %collective-permute-done.came_ref = bf16[128,128]{1,0:T(8,128)(2,1)S(1)} collective-permute-done((bf16[128,128]{1,0:T(8,128)(2,1)S(1)}, bf16[128,128]{1,0:T(8,128)(2,1)S(1)}, u32[]{:S(2)}, u32[]{:S(2)}) %collective-permute-start) | collective-permute-done | bytes 32800 | tf_op jit(solution)/shard_map/ppermute | solution.py:339
  17.9 0.6 %shard_map.94 = bf16[8,16,128]{2,1,0:T(8,128)(2,1)} custom-call(f32[128,128]{1,0:T(8,128)S(1)} %shard_map.93.mine_ref, bf16[128,128]{1,0:T(8,128)(2,1)S(1)} %collective-permute-done.came_ref), custom_call_target="tpu_custom_call" | custom-call | tf_op jit(solution)/shard_map/pallas_call | solution.py:353
Async XLA Ops:
  1.6 11.3 %copy-start = (bf16[1024,128]{1,0:T(8,128)(2,1)S(1)}, bf16[1024,128]{1,0:T(8,128)(2,1)}, u32[]{:S(2)}) copy-start(bf16[1024,128]{1,0:T(8,128)(2,1)} %weight_ref.3) | copy-start | bytes 786436
  13.5 4.4 %collective-permute-start = (bf16[128,128]{1,0:T(8,128)(2,1)S(1)}, bf16[128,128]{1,0:T(8,128)(2,1)S(1)}, u32[]{:S(2)}, u32[]{:S(2)}) collective-permute-start(bf16[128,128]{1,0:T(8,128)(2,1)S(1)} %get-tuple-element.8), channel_id=1, source_target_pairs={{0,5},{1,4},{2,7},{3,6},{4,1},{5,0},{6,3},{7,2},{8,13},{9,12},{10,... | collective-permute-start | bytes 98312 | tf_op jit(solution)/shard_map/ppermute | solution.py:339

commit v21 on v19

--- a/solution.py
+++ b/solution.py
@@ -47,25 +47,25 @@
         pltpu.make_async_copy(source, target, sems.at[n])
         for n, (source, target) in enumerate(
             [
-                (align_hbm, align_ref),
+                (left_w_hbm, left_w_ref),
+                (right_w_hbm, right_w_ref),
                 (gain_hbm, gain_ref),
                 (offset_hbm, offset_ref),
-                (left_w_hbm, left_w_ref),
+                (align_hbm, align_ref),
                 (left_b_hbm, left_b_ref),
-                (right_w_hbm, right_w_ref),
                 (right_b_hbm, right_b_ref),
             ]
         )
     ]
     for copy in copies:
         copy.start()
-    for copy in copies:
+    for copy in copies[:4]:
         copy.wait()
     rows, res_total, chan = align_ref.shape
     hidden = left_w_ref.shape[0]
     copies_of = LANES // (2 * hidden)
     weights = jnp.concatenate([left_w_ref[...], right_w_ref[...]] * copies_of, axis=0)
-    scaled = (weights.astype(jnp.float32) * gain_ref[...]).astype(jnp.bfloat16)
+    scaled = (weights.astype(jnp.float32) * gain_ref[...]).astype(jnp.bfloat16).T
     inner = (((1,), (1,)), ((), ()))
     offset = jnp.broadcast_to(offset_ref[...], (8, chan))
     high = offset.astype(jnp.bfloat16)
@@ -73,7 +73,10 @@
     shift = (
         lax.dot_general(high, weights, inner, preferred_element_type=jnp.float32)
         + lax.dot_general(low, weights, inner, preferred_element_type=jnp.float32)
-    )[:1] + jnp.concatenate([left_b_ref[...], right_b_ref[...]] * copies_of, axis=1)
+    )[:1]
+    for copy in copies[4:]:
+        copy.wait()
+    shift += jnp.concatenate([left_b_ref[...], right_b_ref[...]] * copies_of, axis=1)
     flat, factors = [], []
     for row in range(rows):
         values = align_ref[row].astype(jnp.float32)
@@ -81,8 +84,8 @@
         spread = jnp.mean(centred * centred, axis=-1, keepdims=True)
         flat.append(centred.astype(jnp.bfloat16))
         factors.append(lax.rsqrt(spread + 1e-05))
-    product = lax.dot_general(
-        jnp.concatenate(flat, axis=0), scaled, inner, preferred_element_type=jnp.float32
+    product = jnp.dot(
+        jnp.concatenate(flat, axis=0), scaled, preferred_element_type=jnp.float32
     )
     for row, factor in enumerate(factors):
         place = slice(row * res_total, (row + 1) * res_total)

time: 18.6 us -> 18.8 us (1.011)
  no operation moved by 1% of the time
where the time goes in v21:
time: 18.8 us; the launch traced here: 18.5 us
  blocking collectives  11.3 us (60%)
  Pallas kernels  3.46 us (18%)
  starting transfers between devices  2.37 us (13%)
  waiting for transfers between devices  1.32 us (7%)
    all_to_all x1, blocking collectives, body(): lax.all_to_all(send, ('seq', 'half', 'rest'), split_axis=0, concat_axis=0...  11.3 us
    ppermute x1, starting transfers between devices, body(): came = lax.ppermute(theirs, ('half', 'rest'), swap)  2.37 us
    pallas_call x1, Pallas kernels, body(): pl.pallas_call(functools.partial(project_kernel, seq_count, half_count, r...  1.55 us
    ppermute x1, waiting for transfers between devices, body(): came = lax.ppermute(theirs, ('half', 'rest'), swap)  1.32 us
    pallas_call x1, Pallas kernels, body(): pl.pallas_call(functools.partial(mine_kernel, sizes), out_shape=term, in_...  0.67 us
    pallas_call x1, Pallas kernels, body(): pl.pallas_call(add_kernel, out_shape=jax.ShapeDtypeStruct((row_block, col...  0.64 us
    pallas_call x1, Pallas kernels, body(): pl.pallas_call(functools.partial(theirs_kernel, sizes), out_shape=[jax.Sh...  0.6 us
  transfers between devices with their start and end apart: 1, of which 1 were waited for; matrix products, arithmetic and copies ran while one was open for 0% of the time, Pallas kernels for 4%

profile of v21, /device:TPU:0, one launch (start us, length us, event | category | flops | bytes accessed | tf_op | source)
XLA Modules:
  0.0 18.5 jit_solution(16167808004662022558)
XLA Ops:
  0.0 1.6 %shard_map.91 = bf16[128,1024]{1,0:T(8,128)(2,1)S(1)} custom-call(bf16[8,64,256]{2,1,0:T(8,128)(2,1)} %align_hbm.1, f32[1,256]{1,0:T(1,128)} %bitcast.14, f32[1,256]{1,0:T(1,128)} %bitcast.15, bf16[32,256]{1,0:T(8,128)(2,1)} %bitcast.12, f32[1,32]{1,0:T(1,128)} %bitcast.16, bf16[32,256]{1,0:T(8,128)(2,1)} %bitcast.13, f32[1,32]{1,0:T(1,128)} %bitcast.17), custom_call_target="tpu_custom_call" | custom-call | tf_op jit(solution)/shard_map/pallas_call | solution.py:271
  1.6 0.0 copy-start
  1.6 11.3 %all_to_all.11 = bf16[16,8,1024]{2,1,0:T(8,128)(2,1)S(1)} all-to-all(bf16[16,8,1024]{2,1,0:T(8,128)(2,1)S(1)} %bitcast.11), channel_id=1, replica_groups={{27,0,8,16,24,1,9,17,25,2,10,18,26,3,11,19},{31,4,12,20,28,5,13,21,29,6..., dimensions={0} | all-to-all | bytes 524288 | tf_op jit(solution)/shard_map/all_to_all | solution.py:302
  12.9 0.0 copy-done
  12.9 0.6 %shard_map.92 = (bf16[128,128]{1,0:T(8,128)(2,1)S(1)}, f32[128,128]{1,0:T(8,128)S(1)}) custom-call(bf16[128,1024]{1,0:T(8,128)(2,1)S(1)} %bitcast.9, bf16[1024,128]{1,0:T(8,128)(2,1)S(1)} %copy-done), custom_call_target="tpu_custom_call" | custom-call | flops 67108864 | bytes 524288 | tf_op jit(solution)/shard_map/pallas_call | solution.py:319
  13.5 2.4 %collective-permute-start = (bf16[128,128]{1,0:T(8,128)(2,1)S(1)}, bf16[128,128]{1,0:T(8,128)(2,1)S(1)}, u32[]{:S(2)}, u32[]{:S(2)}) collective-permute-start(bf16[128,128]{1,0:T(8,128)(2,1)S(1)} %get-tuple-element.8), channel_id=1, source_target_pairs={{0,5},{1,4},{2,7},{3,6},{4,1},{5,0},{6,3},{7,2},{8,13},{9,12},{10,... | collective-permute-start | bytes 98312 | tf_op jit(solution)/shard_map/ppermute | solution.py:333
  15.9 0.7 %shard_map.93.mine_ref = f32[128,128]{1,0:T(8,128)S(1)} custom-call(bf16[128,1024]{1,0:T(8,128)(2,1)S(1)} %bitcast.10, bf16[1024,128]{1,0:T(8,128)(2,1)S(1)} %copy-done, f32[128,128]{1,0:T(8,128)S(1)} %get-tuple-element.7.early_ref, f32[1,128]{1,0:T(1,128)} %bitcast.18), custom_call_target="tpu_custom_call" | custom-call | flops 67108864 | bytes 524288 | tf_op jit(solution)/shard_map/pallas_call | solution.py:334
  16.6 1.3 %collective-permute-done.came_ref = bf16[128,128]{1,0:T(8,128)(2,1)S(1)} collective-permute-done((bf16[128,128]{1,0:T(8,128)(2,1)S(1)}, bf16[128,128]{1,0:T(8,128)(2,1)S(1)}, u32[]{:S(2)}, u32[]{:S(2)}) %collective-permute-start) | collective-permute-done | bytes 32800 | tf_op jit(solution)/shard_map/ppermute | solution.py:333
  17.9 0.6 %shard_map.94 = bf16[8,16,128]{2,1,0:T(8,128)(2,1)} custom-call(f32[128,128]{1,0:T(8,128)S(1)} %shard_map.93.mine_ref, bf16[128,128]{1,0:T(8,128)(2,1)S(1)} %collective-permute-done.came_ref), custom_call_target="tpu_custom_call" | custom-call | tf_op jit(solution)/shard_map/pallas_call | solution.py:347
Async XLA Ops:
  1.6 11.3 %copy-start = (bf16[1024,128]{1,0:T(8,128)(2,1)S(1)}, bf16[1024,128]{1,0:T(8,128)(2,1)}, u32[]{:S(2)}) copy-start(bf16[1024,128]{1,0:T(8,128)(2,1)} %weight_ref.3) | copy-start | bytes 786436
  13.5 4.4 %collective-permute-start = (bf16[128,128]{1,0:T(8,128)(2,1)S(1)}, bf16[128,128]{1,0:T(8,128)(2,1)S(1)}, u32[]{:S(2)}, u32[]{:S(2)}) collective-permute-start(bf16[128,128]{1,0:T(8,128)(2,1)S(1)} %get-tuple-element.8), channel_id=1, source_target_pairs={{0,5},{1,4},{2,7},{3,6},{4,1},{5,0},{6,3},{7,2},{8,13},{9,12},{10,... | collective-permute-start | bytes 98312 | tf_op jit(solution)/shard_map/ppermute | solution.py:333

commit v22 on v19

--- a/solution.py
+++ b/solution.py
@@ -12,8 +12,11 @@
 
 
 def peer_order(seq_count, rest_count):
-    peers = [(b, a) for a in range(rest_count) for b in range(seq_count)]
-    return peers[-1:] + peers[:-1]
+    chips = range(0, rest_count, 2) if rest_count % 2 == 0 else ()
+    peers = [(b, a + core) for a in chips for b in range(seq_count) for core in (1, 0)]
+    if not peers:
+        peers = [(b, a) for a in range(rest_count) for b in range(seq_count)]
+    return peers[-2:-1] + peers[:-2] + peers[-1:]
 
 
 def partner(at, rest_count):

time: 18.6 us -> 18.5 us (level)
  blocking collectives: 11.3 us -> 11.1 us
    all_to_all x1, blocking collectives: 11.3 us -> 11.1 us  [body(): lax.all_to_all(send, ('seq', 'half', 'rest'), split_axis=0, concat_axis=0...]
where the time goes in v22:
time: 18.5 us; the launch traced here: 18.2 us
  blocking collectives  11.1 us (60%)
  Pallas kernels  3.39 us (18%)
  starting transfers between devices  2.41 us (13%)
  waiting for transfers between devices  1.22 us (7%)
    all_to_all x1, blocking collectives, body(): lax.all_to_all(send, ('seq', 'half', 'rest'), split_axis=0, concat_axis=0...  11.1 us
    ppermute x1, starting transfers between devices, body(): came = lax.ppermute(theirs, ('half', 'rest'), swap)  2.41 us
    pallas_call x1, Pallas kernels, body(): pl.pallas_call(functools.partial(project_kernel, seq_count, half_count, r...  1.48 us
    ppermute x1, waiting for transfers between devices, body(): came = lax.ppermute(theirs, ('half', 'rest'), swap)  1.22 us
    pallas_call x1, Pallas kernels, body(): pl.pallas_call(functools.partial(mine_kernel, sizes), out_shape=term, in_...  0.67 us
    pallas_call x1, Pallas kernels, body(): pl.pallas_call(add_kernel, out_shape=jax.ShapeDtypeStruct((row_block, col...  0.64 us
    pallas_call x1, Pallas kernels, body(): pl.pallas_call(functools.partial(theirs_kernel, sizes), out_shape=[jax.Sh...  0.6 us
  transfers between devices with their start and end apart: 1, of which 1 were waited for; matrix products, arithmetic and copies ran while one was open for 0% of the time, Pallas kernels for 4%

profile of v22, /device:TPU:0, one launch (start us, length us, event | category | flops | bytes accessed | tf_op | source)
XLA Modules:
  0.0 18.2 jit_solution(8067717702007110442)
XLA Ops:
  0.0 1.5 %shard_map.91 = bf16[128,1024]{1,0:T(8,128)(2,1)S(1)} custom-call(bf16[8,64,256]{2,1,0:T(8,128)(2,1)} %align_hbm.1, f32[1,256]{1,0:T(1,128)} %bitcast.14, f32[1,256]{1,0:T(1,128)} %bitcast.15, bf16[32,256]{1,0:T(8,128)(2,1)} %bitcast.12, f32[1,32]{1,0:T(1,128)} %bitcast.16, bf16[32,256]{1,0:T(8,128)(2,1)} %bitcast.13, f32[1,32]{1,0:T(1,128)} %bitcast.17), custom_call_target="tpu_custom_call" | custom-call | tf_op jit(solution)/shard_map/pallas_call | solution.py:271
  1.5 0.0 copy-start
  1.5 11.1 %all_to_all.11 = bf16[16,8,1024]{2,1,0:T(8,128)(2,1)S(1)} all-to-all(bf16[16,8,1024]{2,1,0:T(8,128)(2,1)S(1)} %bitcast.11), channel_id=1, replica_groups={{27,1,0,9,8,17,16,25,24,3,2,11,10,19,18,26},{31,5,4,13,12,21,20,29,28,7..., dimensions={0} | all-to-all | bytes 524288 | tf_op jit(solution)/shard_map/all_to_all | solution.py:302
  12.6 0.0 copy-done
  12.6 0.6 %shard_map.92 = (bf16[128,128]{1,0:T(8,128)(2,1)S(1)}, f32[128,128]{1,0:T(8,128)S(1)}) custom-call(bf16[128,1024]{1,0:T(8,128)(2,1)S(1)} %bitcast.9, bf16[1024,128]{1,0:T(8,128)(2,1)S(1)} %copy-done), custom_call_target="tpu_custom_call" | custom-call | flops 67108864 | bytes 524288 | tf_op jit(solution)/shard_map/pallas_call | solution.py:319
  13.2 2.4 %collective-permute-start = (bf16[128,128]{1,0:T(8,128)(2,1)S(1)}, bf16[128,128]{1,0:T(8,128)(2,1)S(1)}, u32[]{:S(2)}, u32[]{:S(2)}) collective-permute-start(bf16[128,128]{1,0:T(8,128)(2,1)S(1)} %get-tuple-element.8), channel_id=1, source_target_pairs={{0,5},{1,4},{2,7},{3,6},{4,1},{5,0},{6,3},{7,2},{8,13},{9,12},{10,... | collective-permute-start | bytes 98312 | tf_op jit(solution)/shard_map/ppermute | solution.py:333
  15.7 0.7 %shard_map.93.mine_ref = f32[128,128]{1,0:T(8,128)S(1)} custom-call(bf16[128,1024]{1,0:T(8,128)(2,1)S(1)} %bitcast.10, bf16[1024,128]{1,0:T(8,128)(2,1)S(1)} %copy-done, f32[128,128]{1,0:T(8,128)S(1)} %get-tuple-element.7.early_ref, f32[1,128]{1,0:T(1,128)} %bitcast.18), custom_call_target="tpu_custom_call" | custom-call | flops 67108864 | bytes 524288 | tf_op jit(solution)/shard_map/pallas_call | solution.py:334
  16.3 1.2 %collective-permute-done.came_ref = bf16[128,128]{1,0:T(8,128)(2,1)S(1)} collective-permute-done((bf16[128,128]{1,0:T(8,128)(2,1)S(1)}, bf16[128,128]{1,0:T(8,128)(2,1)S(1)}, u32[]{:S(2)}, u32[]{:S(2)}) %collective-permute-start) | collective-permute-done | bytes 32800 | tf_op jit(solution)/shard_map/ppermute | solution.py:333
  17.6 0.6 %shard_map.94 = bf16[8,16,128]{2,1,0:T(8,128)(2,1)} custom-call(f32[128,128]{1,0:T(8,128)S(1)} %shard_map.93.mine_ref, bf16[128,128]{1,0:T(8,128)(2,1)S(1)} %collective-permute-done.came_ref), custom_call_target="tpu_custom_call" | custom-call | tf_op jit(solution)/shard_map/pallas_call | solution.py:347
Async XLA Ops:
  1.5 11.1 %copy-start = (bf16[1024,128]{1,0:T(8,128)(2,1)S(1)}, bf16[1024,128]{1,0:T(8,128)(2,1)}, u32[]{:S(2)}) copy-start(bf16[1024,128]{1,0:T(8,128)(2,1)} %weight_ref.3) | copy-start | bytes 786436
  13.2 4.3 %collective-permute-start = (bf16[128,128]{1,0:T(8,128)(2,1)S(1)}, bf16[128,128]{1,0:T(8,128)(2,1)S(1)}, u32[]{:S(2)}, u32[]{:S(2)}) collective-permute-start(bf16[128,128]{1,0:T(8,128)(2,1)S(1)} %get-tuple-element.8), channel_id=1, source_target_pairs={{0,5},{1,4},{2,7},{3,6},{4,1},{5,0},{6,3},{7,2},{8,13},{9,12},{10,... | collective-permute-start | bytes 98312 | tf_op jit(solution)/shard_map/ppermute | solution.py:333

commit v23 on v22

--- a/solution.py
+++ b/solution.py
@@ -188,7 +188,9 @@
 
 
 def swaps_late():
-    return (lax.axis_index("seq") == 0) & (lax.axis_index("rest") // 2 % 2 == 1)
+    return (lax.axis_index("seq") < lax.axis_size("seq") - 1) & (
+        lax.axis_index("rest") // 2 % 2 == 1
+    )
 
 
 def theirs_kernel(sizes, recv_ref, weight_ref, theirs_ref, early_ref, left_ref):

time: 18.5 us -> 18.4 us (level)
  no operation moved by 1% of the time
where the time goes in v23:
time: 18.4 us; the launch traced here: 18.2 us
  blocking collectives  11.1 us (60%)
  Pallas kernels  3.39 us (18%)
  starting transfers between devices  2.41 us (13%)
  waiting for transfers between devices  1.22 us (7%)
    all_to_all x1, blocking collectives, body(): lax.all_to_all(send, ('seq', 'half', 'rest'), split_axis=0, concat_axis=0...  11.1 us
    ppermute x1, starting transfers between devices, body(): came = lax.ppermute(theirs, ('half', 'rest'), swap)  2.41 us
    pallas_call x1, Pallas kernels, body(): pl.pallas_call(functools.partial(project_kernel, seq_count, half_count, r...  1.48 us
    ppermute x1, waiting for transfers between devices, body(): came = lax.ppermute(theirs, ('half', 'rest'), swap)  1.22 us
    pallas_call x1, Pallas kernels, body(): pl.pallas_call(functools.partial(mine_kernel, sizes), out_shape=term, in_...  0.67 us
    pallas_call x1, Pallas kernels, body(): pl.pallas_call(add_kernel, out_shape=jax.ShapeDtypeStruct((row_block, col...  0.64 us
    pallas_call x1, Pallas kernels, body(): pl.pallas_call(functools.partial(theirs_kernel, sizes), out_shape=[jax.Sh...  0.6 us
  transfers between devices with their start and end apart: 1, of which 1 were waited for; matrix products, arithmetic and copies ran while one was open for 0% of the time, Pallas kernels for 4%

profile of v23, /device:TPU:0, one launch (start us, length us, event | category | flops | bytes accessed | tf_op | source)
XLA Modules:
  0.0 18.2 jit_solution(16258612584039968283)
XLA Ops:
  0.0 1.5 %shard_map.91 = bf16[128,1024]{1,0:T(8,128)(2,1)S(1)} custom-call(bf16[8,64,256]{2,1,0:T(8,128)(2,1)} %align_hbm.1, f32[1,256]{1,0:T(1,128)} %bitcast.14, f32[1,256]{1,0:T(1,128)} %bitcast.15, bf16[32,256]{1,0:T(8,128)(2,1)} %bitcast.12, f32[1,32]{1,0:T(1,128)} %bitcast.16, bf16[32,256]{1,0:T(8,128)(2,1)} %bitcast.13, f32[1,32]{1,0:T(1,128)} %bitcast.17), custom_call_target="tpu_custom_call" | custom-call | tf_op jit(solution)/shard_map/pallas_call | solution.py:273
  1.5 0.0 copy-start
  1.5 11.1 %all_to_all.11 = bf16[16,8,1024]{2,1,0:T(8,128)(2,1)S(1)} all-to-all(bf16[16,8,1024]{2,1,0:T(8,128)(2,1)S(1)} %bitcast.11), channel_id=1, replica_groups={{27,1,0,9,8,17,16,25,24,3,2,11,10,19,18,26},{31,5,4,13,12,21,20,29,28,7..., dimensions={0} | all-to-all | bytes 524288 | tf_op jit(solution)/shard_map/all_to_all | solution.py:304
  12.6 0.0 copy-done
  12.6 0.6 %shard_map.92 = (bf16[128,128]{1,0:T(8,128)(2,1)S(1)}, f32[128,128]{1,0:T(8,128)S(1)}) custom-call(bf16[128,1024]{1,0:T(8,128)(2,1)S(1)} %bitcast.9, bf16[1024,128]{1,0:T(8,128)(2,1)S(1)} %copy-done), custom_call_target="tpu_custom_call" | custom-call | flops 67108864 | bytes 524288 | tf_op jit(solution)/shard_map/pallas_call | solution.py:321
  13.2 2.4 %collective-permute-start = (bf16[128,128]{1,0:T(8,128)(2,1)S(1)}, bf16[128,128]{1,0:T(8,128)(2,1)S(1)}, u32[]{:S(2)}, u32[]{:S(2)}) collective-permute-start(bf16[128,128]{1,0:T(8,128)(2,1)S(1)} %get-tuple-element.8), channel_id=1, source_target_pairs={{0,5},{1,4},{2,7},{3,6},{4,1},{5,0},{6,3},{7,2},{8,13},{9,12},{10,... | collective-permute-start | bytes 98312 | tf_op jit(solution)/shard_map/ppermute | solution.py:335
  15.7 0.7 %shard_map.93.mine_ref = f32[128,128]{1,0:T(8,128)S(1)} custom-call(bf16[128,1024]{1,0:T(8,128)(2,1)S(1)} %bitcast.10, bf16[1024,128]{1,0:T(8,128)(2,1)S(1)} %copy-done, f32[128,128]{1,0:T(8,128)S(1)} %get-tuple-element.7.early_ref, f32[1,128]{1,0:T(1,128)} %bitcast.18), custom_call_target="tpu_custom_call" | custom-call | flops 67108864 | bytes 524288 | tf_op jit(solution)/shard_map/pallas_call | solution.py:336
  16.3 1.2 %collective-permute-done.came_ref = bf16[128,128]{1,0:T(8,128)(2,1)S(1)} collective-permute-done((bf16[128,128]{1,0:T(8,128)(2,1)S(1)}, bf16[128,128]{1,0:T(8,128)(2,1)S(1)}, u32[]{:S(2)}, u32[]{:S(2)}) %collective-permute-start) | collective-permute-done | bytes 32800 | tf_op jit(solution)/shard_map/ppermute | solution.py:335
  17.6 0.6 %shard_map.94 = bf16[8,16,128]{2,1,0:T(8,128)(2,1)} custom-call(f32[128,128]{1,0:T(8,128)S(1)} %shard_map.93.mine_ref, bf16[128,128]{1,0:T(8,128)(2,1)S(1)} %collective-permute-done.came_ref), custom_call_target="tpu_custom_call" | custom-call | tf_op jit(solution)/shard_map/pallas_call | solution.py:349
Async XLA Ops:
  1.5 11.1 %copy-start = (bf16[1024,128]{1,0:T(8,128)(2,1)S(1)}, bf16[1024,128]{1,0:T(8,128)(2,1)}, u32[]{:S(2)}) copy-start(bf16[1024,128]{1,0:T(8,128)(2,1)} %weight_ref.3) | copy-start | bytes 786436
  13.2 4.3 %collective-permute-start = (bf16[128,128]{1,0:T(8,128)(2,1)S(1)}, bf16[128,128]{1,0:T(8,128)(2,1)S(1)}, u32[]{:S(2)}, u32[]{:S(2)}) collective-permute-start(bf16[128,128]{1,0:T(8,128)(2,1)S(1)} %get-tuple-element.8), channel_id=1, source_target_pairs={{0,5},{1,4},{2,7},{3,6},{4,1},{5,0},{6,3},{7,2},{8,13},{9,12},{10,... | collective-permute-start | bytes 98312 | tf_op jit(solution)/shard_map/ppermute | solution.py:335

commit v24 on v23

--- a/solution.py
+++ b/solution.py
@@ -165,7 +165,7 @@
         )
         lines = [[] for _ in range(per_group)]
         for c in range(0, hidden, per_group):
-            rolled = []
+            tiles = []
             for k in range(per_group):
                 at = (c + k) * row_block
                 tile = jnp.concatenate(
@@ -175,12 +175,18 @@
                     ],
                     axis=0,
                 )
-                rolled.append(roll_blocks(tile.astype(jnp.bfloat16), k, hidden))
+                tiles.append(tile.astype(jnp.bfloat16))
+            step = per_group // 2
+            while step:
+                upper = lane_block // step % 2 == 1
+                for k in range(per_group):
+                    if k // step % 2 == 0:
+                        low, high = tiles[k], tiles[k + step]
+                        tiles[k] = jnp.where(upper, roll_blocks(high, step, hidden), low)
+                        tiles[k + step] = jnp.where(upper, high, roll_blocks(low, -step, hidden))
+                step //= 2
             for j in range(per_group):
-                mixed = rolled[(per_group - 1 - j) % per_group]
-                for p in range(per_group - 1):
-                    mixed = jnp.where(lane_block == p, rolled[(p - j) % per_group], mixed)
-                lines[j].append(roll_blocks(mixed, -j, hidden))
+                lines[j].append(tiles[j])
         rows += [jnp.concatenate(line, axis=1) for line in lines]
     flat = jnp.concatenate(rows, axis=0)
     term = jnp.dot(flat, weight_ref[...], preferred_element_type=jnp.float32)

time: 18.4 us -> 18.4 us (level)
  no operation moved by 1% of the time
where the time goes in v24:
time: 18.4 us; the launch traced here: 18.2 us
  blocking collectives  11.1 us (60%)
  Pallas kernels  3.4 us (18%)
  starting transfers between devices  2.41 us (13%)
  waiting for transfers between devices  1.23 us (7%)
    all_to_all x1, blocking collectives, body(): lax.all_to_all(send, ('seq', 'half', 'rest'), split_axis=0, concat_axis=0...  11.1 us
    ppermute x1, starting transfers between devices, body(): came = lax.ppermute(theirs, ('half', 'rest'), swap)  2.41 us
    pallas_call x1, Pallas kernels, body(): pl.pallas_call(functools.partial(project_kernel, seq_count, half_count, r...  1.48 us
    ppermute x1, waiting for transfers between devices, body(): came = lax.ppermute(theirs, ('half', 'rest'), swap)  1.23 us
    pallas_call x1, Pallas kernels, body(): pl.pallas_call(functools.partial(mine_kernel, sizes), out_shape=term, in_...  0.67 us
    pallas_call x1, Pallas kernels, body(): pl.pallas_call(add_kernel, out_shape=jax.ShapeDtypeStruct((row_block, col...  0.64 us
    pallas_call x1, Pallas kernels, body(): pl.pallas_call(functools.partial(theirs_kernel, sizes), out_shape=[jax.Sh...  0.61 us
  transfers between devices with their start and end apart: 1, of which 1 were waited for; matrix products, arithmetic and copies ran while one was open for 0% of the time, Pallas kernels for 4%

profile of v24, /device:TPU:0, one launch (start us, length us, event | category | flops | bytes accessed | tf_op | source)
XLA Modules:
  0.0 18.2 jit_solution(8233033554607891906)
XLA Ops:
  0.0 1.5 %shard_map.91 = bf16[128,1024]{1,0:T(8,128)(2,1)S(1)} custom-call(bf16[8,64,256]{2,1,0:T(8,128)(2,1)} %align_hbm.1, f32[1,256]{1,0:T(1,128)} %bitcast.14, f32[1,256]{1,0:T(1,128)} %bitcast.15, bf16[32,256]{1,0:T(8,128)(2,1)} %bitcast.12, f32[1,32]{1,0:T(1,128)} %bitcast.16, bf16[32,256]{1,0:T(8,128)(2,1)} %bitcast.13, f32[1,32]{1,0:T(1,128)} %bitcast.17), custom_call_target="tpu_custom_call" | custom-call | tf_op jit(solution)/shard_map/pallas_call | solution.py:279
  1.5 0.0 copy-start
  1.5 11.1 %all_to_all.11 = bf16[16,8,1024]{2,1,0:T(8,128)(2,1)S(1)} all-to-all(bf16[16,8,1024]{2,1,0:T(8,128)(2,1)S(1)} %bitcast.11), channel_id=1, replica_groups={{27,1,0,9,8,17,16,25,24,3,2,11,10,19,18,26},{31,5,4,13,12,21,20,29,28,7..., dimensions={0} | all-to-all | bytes 524288 | tf_op jit(solution)/shard_map/all_to_all | solution.py:310
  12.6 0.0 copy-done
  12.6 0.6 %shard_map.92 = (bf16[128,128]{1,0:T(8,128)(2,1)S(1)}, f32[128,128]{1,0:T(8,128)S(1)}) custom-call(bf16[128,1024]{1,0:T(8,128)(2,1)S(1)} %bitcast.9, bf16[1024,128]{1,0:T(8,128)(2,1)S(1)} %copy-done), custom_call_target="tpu_custom_call" | custom-call | flops 67108864 | bytes 524288 | tf_op jit(solution)/shard_map/pallas_call | solution.py:327
  13.3 2.4 %collective-permute-start = (bf16[128,128]{1,0:T(8,128)(2,1)S(1)}, bf16[128,128]{1,0:T(8,128)(2,1)S(1)}, u32[]{:S(2)}, u32[]{:S(2)}) collective-permute-start(bf16[128,128]{1,0:T(8,128)(2,1)S(1)} %get-tuple-element.8), channel_id=1, source_target_pairs={{0,5},{1,4},{2,7},{3,6},{4,1},{5,0},{6,3},{7,2},{8,13},{9,12},{10,... | collective-permute-start | bytes 98312 | tf_op jit(solution)/shard_map/ppermute | solution.py:341
  15.7 0.7 %shard_map.93.mine_ref = f32[128,128]{1,0:T(8,128)S(1)} custom-call(bf16[128,1024]{1,0:T(8,128)(2,1)S(1)} %bitcast.10, bf16[1024,128]{1,0:T(8,128)(2,1)S(1)} %copy-done, f32[128,128]{1,0:T(8,128)S(1)} %get-tuple-element.7.early_ref, f32[1,128]{1,0:T(1,128)} %bitcast.18), custom_call_target="tpu_custom_call" | custom-call | flops 67108864 | bytes 524288 | tf_op jit(solution)/shard_map/pallas_call | solution.py:342
  16.3 1.2 %collective-permute-done.came_ref = bf16[128,128]{1,0:T(8,128)(2,1)S(1)} collective-permute-done((bf16[128,128]{1,0:T(8,128)(2,1)S(1)}, bf16[128,128]{1,0:T(8,128)(2,1)S(1)}, u32[]{:S(2)}, u32[]{:S(2)}) %collective-permute-start) | collective-permute-done | bytes 32800 | tf_op jit(solution)/shard_map/ppermute | solution.py:341
  17.6 0.6 %shard_map.94 = bf16[8,16,128]{2,1,0:T(8,128)(2,1)} custom-call(f32[128,128]{1,0:T(8,128)S(1)} %shard_map.93.mine_ref, bf16[128,128]{1,0:T(8,128)(2,1)S(1)} %collective-permute-done.came_ref), custom_call_target="tpu_custom_call" | custom-call | tf_op jit(solution)/shard_map/pallas_call | solution.py:355
Async XLA Ops:
  1.5 11.1 %copy-start = (bf16[1024,128]{1,0:T(8,128)(2,1)S(1)}, bf16[1024,128]{1,0:T(8,128)(2,1)}, u32[]{:S(2)}) copy-start(bf16[1024,128]{1,0:T(8,128)(2,1)} %weight_ref.3) | copy-start | bytes 786436
  13.3 4.3 %collective-permute-start = (bf16[128,128]{1,0:T(8,128)(2,1)S(1)}, bf16[128,128]{1,0:T(8,128)(2,1)S(1)}, u32[]{:S(2)}, u32[]{:S(2)}) collective-permute-start(bf16[128,128]{1,0:T(8,128)(2,1)S(1)} %get-tuple-element.8), channel_id=1, source_target_pairs={{0,5},{1,4},{2,7},{3,6},{4,1},{5,0},{6,3},{7,2},{8,13},{9,12},{10,... | collective-permute-start | bytes 98312 | tf_op jit(solution)/shard_map/ppermute | solution.py:341

commit v25 on v23

--- a/solution.py
+++ b/solution.py
@@ -16,7 +16,8 @@
     peers = [(b, a + core) for a in chips for b in range(seq_count) for core in (1, 0)]
     if not peers:
         peers = [(b, a) for a in range(rest_count) for b in range(seq_count)]
-    return peers[-2:-1] + peers[:-2] + peers[-1:]
+    first = (seq_count - 1, min(1, rest_count - 1))
+    return [first] + [peer for peer in peers if peer != first]
 
 
 def partner(at, rest_count):

time: 18.4 us -> 18.7 us (1.016)
  blocking collectives: 11.1 us -> 11.5 us
    all_to_all x1, blocking collectives: 11.1 us -> 11.5 us  [body(): lax.all_to_all(send, ('seq', 'half', 'rest'), split_axis=0, concat_axis=0...]
where the time goes in v25:
time: 18.7 us; the launch traced here: 18.6 us
  blocking collectives  11.5 us (61%)
  Pallas kernels  3.39 us (18%)
  starting transfers between devices  2.43 us (13%)
  waiting for transfers between devices  1.2 us (6%)
    all_to_all x1, blocking collectives, body(): lax.all_to_all(send, ('seq', 'half', 'rest'), split_axis=0, concat_axis=0...  11.5 us
    ppermute x1, starting transfers between devices, body(): came = lax.ppermute(theirs, ('half', 'rest'), swap)  2.43 us
    pallas_call x1, Pallas kernels, body(): pl.pallas_call(functools.partial(project_kernel, seq_count, half_count, r...  1.48 us
    ppermute x1, waiting for transfers between devices, body(): came = lax.ppermute(theirs, ('half', 'rest'), swap)  1.2 us
    pallas_call x1, Pallas kernels, body(): pl.pallas_call(functools.partial(mine_kernel, sizes), out_shape=term, in_...  0.67 us
    pallas_call x1, Pallas kernels, body(): pl.pallas_call(add_kernel, out_shape=jax.ShapeDtypeStruct((row_block, col...  0.64 us
    pallas_call x1, Pallas kernels, body(): pl.pallas_call(functools.partial(theirs_kernel, sizes), out_shape=[jax.Sh...  0.6 us
  transfers between devices with their start and end apart: 1, of which 1 were waited for; matrix products, arithmetic and copies ran while one was open for 0% of the time, Pallas kernels for 4%

profile of v25, /device:TPU:0, one launch (start us, length us, event | category | flops | bytes accessed | tf_op | source)
XLA Modules:
  0.0 18.6 jit_solution(12832765260193259914)
XLA Ops:
  0.0 1.5 %shard_map.91 = bf16[128,1024]{1,0:T(8,128)(2,1)S(1)} custom-call(bf16[8,64,256]{2,1,0:T(8,128)(2,1)} %align_hbm.1, f32[1,256]{1,0:T(1,128)} %bitcast.14, f32[1,256]{1,0:T(1,128)} %bitcast.15, bf16[32,256]{1,0:T(8,128)(2,1)} %bitcast.12, f32[1,32]{1,0:T(1,128)} %bitcast.16, bf16[32,256]{1,0:T(8,128)(2,1)} %bitcast.13, f32[1,32]{1,0:T(1,128)} %bitcast.17), custom_call_target="tpu_custom_call" | custom-call | tf_op jit(solution)/shard_map/pallas_call | solution.py:274
  1.5 0.0 copy-start
  1.5 11.5 %all_to_all.11 = bf16[16,8,1024]{2,1,0:T(8,128)(2,1)S(1)} all-to-all(bf16[16,8,1024]{2,1,0:T(8,128)(2,1)S(1)} %bitcast.11), channel_id=1, replica_groups={{25,1,0,9,8,17,16,24,3,2,11,10,19,18,27,26},{29,5,4,13,12,21,20,28,7,6,..., dimensions={0} | all-to-all | bytes 524288 | tf_op jit(solution)/shard_map/all_to_all | solution.py:305
  13.0 0.0 copy-done
  13.0 0.6 %shard_map.92 = (bf16[128,128]{1,0:T(8,128)(2,1)S(1)}, f32[128,128]{1,0:T(8,128)S(1)}) custom-call(bf16[128,1024]{1,0:T(8,128)(2,1)S(1)} %bitcast.9, bf16[1024,128]{1,0:T(8,128)(2,1)S(1)} %copy-done), custom_call_target="tpu_custom_call" | custom-call | flops 67108864 | bytes 524288 | tf_op jit(solution)/shard_map/pallas_call | solution.py:322
  13.6 2.4 %collective-permute-start = (bf16[128,128]{1,0:T(8,128)(2,1)S(1)}, bf16[128,128]{1,0:T(8,128)(2,1)S(1)}, u32[]{:S(2)}, u32[]{:S(2)}) collective-permute-start(bf16[128,128]{1,0:T(8,128)(2,1)S(1)} %get-tuple-element.8), channel_id=1, source_target_pairs={{0,5},{1,4},{2,7},{3,6},{4,1},{5,0},{6,3},{7,2},{8,13},{9,12},{10,... | collective-permute-start | bytes 98312 | tf_op jit(solution)/shard_map/ppermute | solution.py:336
  16.0 0.7 %shard_map.93.mine_ref = f32[128,128]{1,0:T(8,128)S(1)} custom-call(bf16[128,1024]{1,0:T(8,128)(2,1)S(1)} %bitcast.10, bf16[1024,128]{1,0:T(8,128)(2,1)S(1)} %copy-done, f32[128,128]{1,0:T(8,128)S(1)} %get-tuple-element.7.early_ref, f32[1,128]{1,0:T(1,128)} %bitcast.18), custom_call_target="tpu_custom_call" | custom-call | flops 67108864 | bytes 524288 | tf_op jit(solution)/shard_map/pallas_call | solution.py:337
  16.7 1.2 %collective-permute-done.came_ref = bf16[128,128]{1,0:T(8,128)(2,1)S(1)} collective-permute-done((bf16[128,128]{1,0:T(8,128)(2,1)S(1)}, bf16[128,128]{1,0:T(8,128)(2,1)S(1)}, u32[]{:S(2)}, u32[]{:S(2)}) %collective-permute-start) | collective-permute-done | bytes 32800 | tf_op jit(solution)/shard_map/ppermute | solution.py:336
  17.9 0.6 %shard_map.94 = bf16[8,16,128]{2,1,0:T(8,128)(2,1)} custom-call(f32[128,128]{1,0:T(8,128)S(1)} %shard_map.93.mine_ref, bf16[128,128]{1,0:T(8,128)(2,1)S(1)} %collective-permute-done.came_ref), custom_call_target="tpu_custom_call" | custom-call | tf_op jit(solution)/shard_map/pallas_call | solution.py:350
Async XLA Ops:
  1.5 11.5 %copy-start = (bf16[1024,128]{1,0:T(8,128)(2,1)S(1)}, bf16[1024,128]{1,0:T(8,128)(2,1)}, u32[]{:S(2)}) copy-start(bf16[1024,128]{1,0:T(8,128)(2,1)} %weight_ref.3) | copy-start | bytes 786436
  13.6 4.3 %collective-permute-start = (bf16[128,128]{1,0:T(8,128)(2,1)S(1)}, bf16[128,128]{1,0:T(8,128)(2,1)S(1)}, u32[]{:S(2)}, u32[]{:S(2)}) collective-permute-start(bf16[128,128]{1,0:T(8,128)(2,1)S(1)} %get-tuple-element.8), channel_id=1, source_target_pairs={{0,5},{1,4},{2,7},{3,6},{4,1},{5,0},{6,3},{7,2},{8,13},{9,12},{10,... | collective-permute-start | bytes 98312 | tf_op jit(solution)/shard_map/ppermute | solution.py:336

commit v26 on v23

--- a/solution.py
+++ b/solution.py
@@ -16,7 +16,7 @@
     peers = [(b, a + core) for a in chips for b in range(seq_count) for core in (1, 0)]
     if not peers:
         peers = [(b, a) for a in range(rest_count) for b in range(seq_count)]
-    return peers[-2:-1] + peers[:-2] + peers[-1:]
+    return peers[-1:] + peers[:-1]
 
 
 def partner(at, rest_count):

time: 18.4 us -> 19.3 us (1.049)
  blocking collectives: 11.1 us -> 12 us
  waiting for transfers between devices: 1.22 us -> 1.42 us
    all_to_all x1, blocking collectives: 11.1 us -> 12 us  [body(): lax.all_to_all(send, ('seq', 'half', 'rest'), split_axis=0, concat_axis=0...]
    ppermute x1, waiting for transfers between devices: 1.22 us -> 1.42 us  [body(): came = lax.ppermute(theirs, ('half', 'rest'), swap)]
  transfers between devices with their start and end apart: 1 -> 1, of which waited for: 1 -> 1; matrix products, arithmetic and copies ran while one was open for 0% -> 0% of each run, Pallas kernels for 4% -> 3%
where the time goes in v26:
time: 19.3 us; the launch traced here: 19.1 us
  blocking collectives  12 us (62%)
  Pallas kernels  3.39 us (18%)
  starting transfers between devices  2.31 us (12%)
  waiting for transfers between devices  1.42 us (7%)
    all_to_all x1, blocking collectives, body(): lax.all_to_all(send, ('seq', 'half', 'rest'), split_axis=0, concat_axis=0...  12 us
    ppermute x1, starting transfers between devices, body(): came = lax.ppermute(theirs, ('half', 'rest'), swap)  2.31 us
    pallas_call x1, Pallas kernels, body(): pl.pallas_call(functools.partial(project_kernel, seq_count, half_count, r...  1.48 us
    ppermute x1, waiting for transfers between devices, body(): came = lax.ppermute(theirs, ('half', 'rest'), swap)  1.42 us
    pallas_call x1, Pallas kernels, body(): pl.pallas_call(functools.partial(mine_kernel, sizes), out_shape=term, in_...  0.67 us
    pallas_call x1, Pallas kernels, body(): pl.pallas_call(add_kernel, out_shape=jax.ShapeDtypeStruct((row_block, col...  0.64 us
    pallas_call x1, Pallas kernels, body(): pl.pallas_call(functools.partial(theirs_kernel, sizes), out_shape=[jax.Sh...  0.6 us
  transfers between devices with their start and end apart: 1, of which 1 were waited for; matrix products, arithmetic and copies ran while one was open for 0% of the time, Pallas kernels for 3%

profile of v26, /device:TPU:0, one launch (start us, length us, event | category | flops | bytes accessed | tf_op | source)
XLA Modules:
  0.0 19.1 jit_solution(12757653894060492040)
XLA Ops:
  0.0 1.5 %shard_map.91 = bf16[128,1024]{1,0:T(8,128)(2,1)S(1)} custom-call(bf16[8,64,256]{2,1,0:T(8,128)(2,1)} %align_hbm.1, f32[1,256]{1,0:T(1,128)} %bitcast.14, f32[1,256]{1,0:T(1,128)} %bitcast.15, bf16[32,256]{1,0:T(8,128)(2,1)} %bitcast.12, f32[1,32]{1,0:T(1,128)} %bitcast.16, bf16[32,256]{1,0:T(8,128)(2,1)} %bitcast.13, f32[1,32]{1,0:T(1,128)} %bitcast.17), custom_call_target="tpu_custom_call" | custom-call | tf_op jit(solution)/shard_map/pallas_call | solution.py:273
  1.5 0.0 copy-start
  1.5 12.0 %all_to_all.11 = bf16[16,8,1024]{2,1,0:T(8,128)(2,1)S(1)} all-to-all(bf16[16,8,1024]{2,1,0:T(8,128)(2,1)S(1)} %bitcast.11), channel_id=1, replica_groups={{26,1,0,9,8,17,16,25,24,3,2,11,10,19,18,27},{30,5,4,13,12,21,20,29,28,7..., dimensions={0} | all-to-all | bytes 524288 | tf_op jit(solution)/shard_map/all_to_all | solution.py:304
  13.5 0.0 copy-done
  13.5 0.6 %shard_map.92 = (bf16[128,128]{1,0:T(8,128)(2,1)S(1)}, f32[128,128]{1,0:T(8,128)S(1)}) custom-call(bf16[128,1024]{1,0:T(8,128)(2,1)S(1)} %bitcast.9, bf16[1024,128]{1,0:T(8,128)(2,1)S(1)} %copy-done), custom_call_target="tpu_custom_call" | custom-call | flops 67108864 | bytes 524288 | tf_op jit(solution)/shard_map/pallas_call | solution.py:321
  14.1 2.3 %collective-permute-start = (bf16[128,128]{1,0:T(8,128)(2,1)S(1)}, bf16[128,128]{1,0:T(8,128)(2,1)S(1)}, u32[]{:S(2)}, u32[]{:S(2)}) collective-permute-start(bf16[128,128]{1,0:T(8,128)(2,1)S(1)} %get-tuple-element.8), channel_id=1, source_target_pairs={{0,5},{1,4},{2,7},{3,6},{4,1},{5,0},{6,3},{7,2},{8,13},{9,12},{10,... | collective-permute-start | bytes 98312 | tf_op jit(solution)/shard_map/ppermute | solution.py:335
  16.4 0.7 %shard_map.93.mine_ref = f32[128,128]{1,0:T(8,128)S(1)} custom-call(bf16[128,1024]{1,0:T(8,128)(2,1)S(1)} %bitcast.10, bf16[1024,128]{1,0:T(8,128)(2,1)S(1)} %copy-done, f32[128,128]{1,0:T(8,128)S(1)} %get-tuple-element.7.early_ref, f32[1,128]{1,0:T(1,128)} %bitcast.18), custom_call_target="tpu_custom_call" | custom-call | flops 67108864 | bytes 524288 | tf_op jit(solution)/shard_map/pallas_call | solution.py:336
  17.1 1.4 %collective-permute-done.came_ref = bf16[128,128]{1,0:T(8,128)(2,1)S(1)} collective-permute-done((bf16[128,128]{1,0:T(8,128)(2,1)S(1)}, bf16[128,128]{1,0:T(8,128)(2,1)S(1)}, u32[]{:S(2)}, u32[]{:S(2)}) %collective-permute-start) | collective-permute-done | bytes 32800 | tf_op jit(solution)/shard_map/ppermute | solution.py:335
  18.5 0.6 %shard_map.94 = bf16[8,16,128]{2,1,0:T(8,128)(2,1)} custom-call(f32[128,128]{1,0:T(8,128)S(1)} %shard_map.93.mine_ref, bf16[128,128]{1,0:T(8,128)(2,1)S(1)} %collective-permute-done.came_ref), custom_call_target="tpu_custom_call" | custom-call | tf_op jit(solution)/shard_map/pallas_call | solution.py:349
Async XLA Ops:
  1.5 12.0 %copy-start = (bf16[1024,128]{1,0:T(8,128)(2,1)S(1)}, bf16[1024,128]{1,0:T(8,128)(2,1)}, u32[]{:S(2)}) copy-start(bf16[1024,128]{1,0:T(8,128)(2,1)} %weight_ref.3) | copy-start | bytes 786436
  14.1 4.4 %collective-permute-start = (bf16[128,128]{1,0:T(8,128)(2,1)S(1)}, bf16[128,128]{1,0:T(8,128)(2,1)S(1)}, u32[]{:S(2)}, u32[]{:S(2)}) collective-permute-start(bf16[128,128]{1,0:T(8,128)(2,1)S(1)} %get-tuple-element.8), channel_id=1, source_target_pairs={{0,5},{1,4},{2,7},{3,6},{4,1},{5,0},{6,3},{7,2},{8,13},{9,12},{10,... | collective-permute-start | bytes 98312 | tf_op jit(solution)/shard_map/ppermute | solution.py:335

commit v27 on v25

--- a/solution.py
+++ b/solution.py
@@ -13,10 +13,10 @@
 
 def peer_order(seq_count, rest_count):
     chips = range(0, rest_count, 2) if rest_count % 2 == 0 else ()
-    peers = [(b, a + core) for a in chips for b in range(seq_count) for core in (1, 0)]
+    peers = [(b, a + core) for a in chips for core in (1, 0) for b in range(seq_count)]
     if not peers:
         peers = [(b, a) for a in range(rest_count) for b in range(seq_count)]
-    first = (seq_count - 1, min(1, rest_count - 1))
+    first = (seq_count - 1, rest_count - 1)
     return [first] + [peer for peer in peers if peer != first]
 
 

time: 18.7 us -> 18.8 us (level)
  waiting for transfers between devices: 1.2 us -> 1.63 us
  starting transfers between devices: 2.43 us -> 2.11 us
    ppermute x1, waiting for transfers between devices: 1.2 us -> 1.63 us  [body(): came = lax.ppermute(theirs, ('half', 'rest'), swap)]
    ppermute x1, starting transfers between devices: 2.43 us -> 2.11 us  [body(): came = lax.ppermute(theirs, ('half', 'rest'), swap)]
where the time goes in v27:
time: 18.8 us; the launch traced here: 18.6 us
  blocking collectives  11.5 us (61%)
  Pallas kernels  3.39 us (18%)
  starting transfers between devices  2.11 us (11%)
  waiting for transfers between devices  1.63 us (9%)
    all_to_all x1, blocking collectives, body(): lax.all_to_all(send, ('seq', 'half', 'rest'), split_axis=0, concat_axis=0...  11.5 us
    ppermute x1, starting transfers between devices, body(): came = lax.ppermute(theirs, ('half', 'rest'), swap)  2.11 us
    ppermute x1, waiting for transfers between devices, body(): came = lax.ppermute(theirs, ('half', 'rest'), swap)  1.63 us
    pallas_call x1, Pallas kernels, body(): pl.pallas_call(functools.partial(project_kernel, seq_count, half_count, r...  1.48 us
    pallas_call x1, Pallas kernels, body(): pl.pallas_call(functools.partial(mine_kernel, sizes), out_shape=term, in_...  0.67 us
    pallas_call x1, Pallas kernels, body(): pl.pallas_call(add_kernel, out_shape=jax.ShapeDtypeStruct((row_block, col...  0.64 us
    pallas_call x1, Pallas kernels, body(): pl.pallas_call(functools.partial(theirs_kernel, sizes), out_shape=[jax.Sh...  0.6 us
  transfers between devices with their start and end apart: 1, of which 1 were waited for; matrix products, arithmetic and copies ran while one was open for 0% of the time, Pallas kernels for 4%

profile of v27, /device:TPU:0, one launch (start us, length us, event | category | flops | bytes accessed | tf_op | source)
XLA Modules:
  0.0 18.6 jit_solution(3211167662013321814)
XLA Ops:
  0.0 1.5 %shard_map.91 = bf16[128,1024]{1,0:T(8,128)(2,1)S(1)} custom-call(bf16[8,64,256]{2,1,0:T(8,128)(2,1)} %align_hbm.1, f32[1,256]{1,0:T(1,128)} %bitcast.14, f32[1,256]{1,0:T(1,128)} %bitcast.15, bf16[32,256]{1,0:T(8,128)(2,1)} %bitcast.12, f32[1,32]{1,0:T(1,128)} %bitcast.16, bf16[32,256]{1,0:T(8,128)(2,1)} %bitcast.13, f32[1,32]{1,0:T(1,128)} %bitcast.17), custom_call_target="tpu_custom_call" | custom-call | tf_op jit(solution)/shard_map/pallas_call | solution.py:274
  1.5 0.0 copy-start
  1.5 11.5 %all_to_all.11 = bf16[16,8,1024]{2,1,0:T(8,128)(2,1)S(1)} all-to-all(bf16[16,8,1024]{2,1,0:T(8,128)(2,1)S(1)} %bitcast.11), channel_id=1, replica_groups={{27,1,9,17,25,0,8,16,24,3,11,19,2,10,18,26},{31,5,13,21,29,4,12,20,28,7..., dimensions={0} | all-to-all | bytes 524288 | tf_op jit(solution)/shard_map/all_to_all | solution.py:305
  13.0 0.0 copy-done
  13.0 0.6 %shard_map.92 = (bf16[128,128]{1,0:T(8,128)(2,1)S(1)}, f32[128,128]{1,0:T(8,128)S(1)}) custom-call(bf16[128,1024]{1,0:T(8,128)(2,1)S(1)} %bitcast.9, bf16[1024,128]{1,0:T(8,128)(2,1)S(1)} %copy-done), custom_call_target="tpu_custom_call" | custom-call | flops 67108864 | bytes 524288 | tf_op jit(solution)/shard_map/pallas_call | solution.py:322
  13.6 2.1 %collective-permute-start = (bf16[128,128]{1,0:T(8,128)(2,1)S(1)}, bf16[128,128]{1,0:T(8,128)(2,1)S(1)}, u32[]{:S(2)}, u32[]{:S(2)}) collective-permute-start(bf16[128,128]{1,0:T(8,128)(2,1)S(1)} %get-tuple-element.8), channel_id=1, source_target_pairs={{0,5},{1,4},{2,7},{3,6},{4,1},{5,0},{6,3},{7,2},{8,13},{9,12},{10,... | collective-permute-start | bytes 98312 | tf_op jit(solution)/shard_map/ppermute | solution.py:336
  15.7 0.7 %shard_map.93.mine_ref = f32[128,128]{1,0:T(8,128)S(1)} custom-call(bf16[128,1024]{1,0:T(8,128)(2,1)S(1)} %bitcast.10, bf16[1024,128]{1,0:T(8,128)(2,1)S(1)} %copy-done, f32[128,128]{1,0:T(8,128)S(1)} %get-tuple-element.7.early_ref, f32[1,128]{1,0:T(1,128)} %bitcast.18), custom_call_target="tpu_custom_call" | custom-call | flops 67108864 | bytes 524288 | tf_op jit(solution)/shard_map/pallas_call | solution.py:337
  16.4 1.6 %collective-permute-done.came_ref = bf16[128,128]{1,0:T(8,128)(2,1)S(1)} collective-permute-done((bf16[128,128]{1,0:T(8,128)(2,1)S(1)}, bf16[128,128]{1,0:T(8,128)(2,1)S(1)}, u32[]{:S(2)}, u32[]{:S(2)}) %collective-permute-start) | collective-permute-done | bytes 32800 | tf_op jit(solution)/shard_map/ppermute | solution.py:336
  18.0 0.6 %shard_map.94 = bf16[8,16,128]{2,1,0:T(8,128)(2,1)} custom-call(f32[128,128]{1,0:T(8,128)S(1)} %shard_map.93.mine_ref, bf16[128,128]{1,0:T(8,128)(2,1)S(1)} %collective-permute-done.came_ref), custom_call_target="tpu_custom_call" | custom-call | tf_op jit(solution)/shard_map/pallas_call | solution.py:350
Async XLA Ops:
  1.5 11.5 %copy-start = (bf16[1024,128]{1,0:T(8,128)(2,1)S(1)}, bf16[1024,128]{1,0:T(8,128)(2,1)}, u32[]{:S(2)}) copy-start(bf16[1024,128]{1,0:T(8,128)(2,1)} %weight_ref.3) | copy-start | bytes 786436
  13.6 4.4 %collective-permute-start = (bf16[128,128]{1,0:T(8,128)(2,1)S(1)}, bf16[128,128]{1,0:T(8,128)(2,1)S(1)}, u32[]{:S(2)}, u32[]{:S(2)}) collective-permute-start(bf16[128,128]{1,0:T(8,128)(2,1)S(1)} %get-tuple-element.8), channel_id=1, source_target_pairs={{0,5},{1,4},{2,7},{3,6},{4,1},{5,0},{6,3},{7,2},{8,13},{9,12},{10,... | collective-permute-start | bytes 98312 | tf_op jit(solution)/shard_map/ppermute | solution.py:336

commit v28 on v23

--- a/solution.py
+++ b/solution.py
@@ -188,8 +188,10 @@
 
 
 def swaps_late():
-    return (lax.axis_index("seq") < lax.axis_size("seq") - 1) & (
-        lax.axis_index("rest") // 2 % 2 == 1
+    return (
+        (lax.axis_index("half") == 1)
+        & (lax.axis_index("seq") < lax.axis_size("seq") - 1)
+        & (lax.axis_index("rest") // 2 % 2 == 1)
     )
 
 

time: 18.4 us -> 18.4 us (level)
  no operation moved by 1% of the time
where the time goes in v28:
time: 18.4 us; the launch traced here: 18.2 us
  blocking collectives  11.1 us (60%)
  Pallas kernels  3.39 us (18%)
  starting transfers between devices  2.41 us (13%)
  waiting for transfers between devices  1.22 us (7%)
    all_to_all x1, blocking collectives, body(): lax.all_to_all(send, ('seq', 'half', 'rest'), split_axis=0, concat_axis=0...  11.1 us
    ppermute x1, starting transfers between devices, body(): came = lax.ppermute(theirs, ('half', 'rest'), swap)  2.41 us
    pallas_call x1, Pallas kernels, body(): pl.pallas_call(functools.partial(project_kernel, seq_count, half_count, r...  1.48 us
    ppermute x1, waiting for transfers between devices, body(): came = lax.ppermute(theirs, ('half', 'rest'), swap)  1.22 us
    pallas_call x1, Pallas kernels, body(): pl.pallas_call(functools.partial(mine_kernel, sizes), out_shape=term, in_...  0.67 us
    pallas_call x1, Pallas kernels, body(): pl.pallas_call(add_kernel, out_shape=jax.ShapeDtypeStruct((row_block, col...  0.64 us
    pallas_call x1, Pallas kernels, body(): pl.pallas_call(functools.partial(theirs_kernel, sizes), out_shape=[jax.Sh...  0.6 us
  transfers between devices with their start and end apart: 1, of which 1 were waited for; matrix products, arithmetic and copies ran while one was open for 0% of the time, Pallas kernels for 4%

profile of v28, /device:TPU:0, one launch (start us, length us, event | category | flops | bytes accessed | tf_op | source)
XLA Modules:
  0.0 18.2 jit_solution(12113487319345839376)
XLA Ops:
  0.0 1.5 %shard_map.91 = bf16[128,1024]{1,0:T(8,128)(2,1)S(1)} custom-call(bf16[8,64,256]{2,1,0:T(8,128)(2,1)} %align_hbm.1, f32[1,256]{1,0:T(1,128)} %bitcast.14, f32[1,256]{1,0:T(1,128)} %bitcast.15, bf16[32,256]{1,0:T(8,128)(2,1)} %bitcast.12, f32[1,32]{1,0:T(1,128)} %bitcast.16, bf16[32,256]{1,0:T(8,128)(2,1)} %bitcast.13, f32[1,32]{1,0:T(1,128)} %bitcast.17), custom_call_target="tpu_custom_call" | custom-call | tf_op jit(solution)/shard_map/pallas_call | solution.py:275
  1.5 0.0 copy-start
  1.5 11.1 %all_to_all.11 = bf16[16,8,1024]{2,1,0:T(8,128)(2,1)S(1)} all-to-all(bf16[16,8,1024]{2,1,0:T(8,128)(2,1)S(1)} %bitcast.11), channel_id=1, replica_groups={{27,1,0,9,8,17,16,25,24,3,2,11,10,19,18,26},{31,5,4,13,12,21,20,29,28,7..., dimensions={0} | all-to-all | bytes 524288 | tf_op jit(solution)/shard_map/all_to_all | solution.py:306
  12.6 0.0 copy-done
  12.6 0.6 %shard_map.92 = (bf16[128,128]{1,0:T(8,128)(2,1)S(1)}, f32[128,128]{1,0:T(8,128)S(1)}) custom-call(bf16[128,1024]{1,0:T(8,128)(2,1)S(1)} %bitcast.9, bf16[1024,128]{1,0:T(8,128)(2,1)S(1)} %copy-done), custom_call_target="tpu_custom_call" | custom-call | flops 67108864 | bytes 524288 | tf_op jit(solution)/shard_map/pallas_call | solution.py:323
  13.2 2.4 %collective-permute-start = (bf16[128,128]{1,0:T(8,128)(2,1)S(1)}, bf16[128,128]{1,0:T(8,128)(2,1)S(1)}, u32[]{:S(2)}, u32[]{:S(2)}) collective-permute-start(bf16[128,128]{1,0:T(8,128)(2,1)S(1)} %get-tuple-element.8), channel_id=1, source_target_pairs={{0,5},{1,4},{2,7},{3,6},{4,1},{5,0},{6,3},{7,2},{8,13},{9,12},{10,... | collective-permute-start | bytes 98312 | tf_op jit(solution)/shard_map/ppermute | solution.py:337
  15.7 0.7 %shard_map.93.mine_ref = f32[128,128]{1,0:T(8,128)S(1)} custom-call(bf16[128,1024]{1,0:T(8,128)(2,1)S(1)} %bitcast.10, bf16[1024,128]{1,0:T(8,128)(2,1)S(1)} %copy-done, f32[128,128]{1,0:T(8,128)S(1)} %get-tuple-element.7.early_ref, f32[1,128]{1,0:T(1,128)} %bitcast.18), custom_call_target="tpu_custom_call" | custom-call | flops 67108864 | bytes 524288 | tf_op jit(solution)/shard_map/pallas_call | solution.py:338
  16.3 1.2 %collective-permute-done.came_ref = bf16[128,128]{1,0:T(8,128)(2,1)S(1)} collective-permute-done((bf16[128,128]{1,0:T(8,128)(2,1)S(1)}, bf16[128,128]{1,0:T(8,128)(2,1)S(1)}, u32[]{:S(2)}, u32[]{:S(2)}) %collective-permute-start) | collective-permute-done | bytes 32800 | tf_op jit(solution)/shard_map/ppermute | solution.py:337
  17.6 0.6 %shard_map.94 = bf16[8,16,128]{2,1,0:T(8,128)(2,1)} custom-call(f32[128,128]{1,0:T(8,128)S(1)} %shard_map.93.mine_ref, bf16[128,128]{1,0:T(8,128)(2,1)S(1)} %collective-permute-done.came_ref), custom_call_target="tpu_custom_call" | custom-call | tf_op jit(solution)/shard_map/pallas_call | solution.py:351
Async XLA Ops:
  1.5 11.1 %copy-start = (bf16[1024,128]{1,0:T(8,128)(2,1)S(1)}, bf16[1024,128]{1,0:T(8,128)(2,1)}, u32[]{:S(2)}) copy-start(bf16[1024,128]{1,0:T(8,128)(2,1)} %weight_ref.3) | copy-start | bytes 786436
  13.2 4.3 %collective-permute-start = (bf16[128,128]{1,0:T(8,128)(2,1)S(1)}, bf16[128,128]{1,0:T(8,128)(2,1)S(1)}, u32[]{:S(2)}, u32[]{:S(2)}) collective-permute-start(bf16[128,128]{1,0:T(8,128)(2,1)S(1)} %get-tuple-element.8), channel_id=1, source_target_pairs={{0,5},{1,4},{2,7},{3,6},{4,1},{5,0},{6,3},{7,2},{8,13},{9,12},{10,... | collective-permute-start | bytes 98312 | tf_op jit(solution)/shard_map/ppermute | solution.py:337

commit v29 on v28

--- a/solution.py
+++ b/solution.py
@@ -138,24 +138,13 @@
         send_ref[place, split:] = pack(right, tuple(("right", b) for b, _ in block))
 
 
-def pair_terms(own, hidden, row_block, col_block, recv_ref, weight_ref, left_ref):
+def pair_terms(own, hidden, row_block, col_block, recv_ref, weight_ref):
     seqs = recv_ref.shape[0]
     split = row_block * hidden
     left = recv_ref[:, :split] if own else recv_ref[:, split : 2 * split]
     right = recv_ref[:, 2 * split :]
-    turned = left.T.astype(jnp.float32)
-    parts = left_ref.shape[0]
-    for n in range(parts):
-        left_ref[n] = turned[:, n * LANES : (n + 1) * LANES]
-    left = jnp.concatenate(
-        [
-            jnp.concatenate(
-                [left_ref[n, pl.ds(c, row_block, stride=hidden), :] for n in range(parts)], axis=1
-            )
-            for c in range(hidden)
-        ],
-        axis=0,
-    ).astype(jnp.bfloat16)
+    turned = left.T.astype(jnp.float32).reshape(row_block, hidden, seqs)
+    left = turned.swapaxes(0, 1).reshape(hidden * row_block, seqs).astype(jnp.bfloat16)
     per_group = LANES // hidden
     lane_block = lax.broadcasted_iota(jnp.int32, (2 * row_block, LANES), 1) // hidden
     rows = []
@@ -195,18 +184,18 @@
     )
 
 
-def theirs_kernel(sizes, recv_ref, weight_ref, theirs_ref, early_ref, left_ref):
+def theirs_kernel(sizes, recv_ref, weight_ref, theirs_ref, early_ref):
     @pl.when(swaps_late())
     def _():
-        early_ref[...] = pair_terms(True, *sizes, recv_ref, weight_ref, left_ref)
-
-    theirs_ref[...] = pair_terms(False, *sizes, recv_ref, weight_ref, left_ref).astype(
+        early_ref[...] = pair_terms(True, *sizes, recv_ref, weight_ref)
+
+    theirs_ref[...] = pair_terms(False, *sizes, recv_ref, weight_ref).astype(
         theirs_ref.dtype
     )
 
 
 def mine_kernel(
-    sizes, recv_ref, weight_ref, early_ref, bias_hbm, mine_ref, left_ref, bias_ref, sem
+    sizes, recv_ref, weight_ref, early_ref, bias_hbm, mine_ref, bias_ref, sem
 ):
     bias = pltpu.make_async_copy(bias_hbm, bias_ref, sem)
     bias.start()
@@ -218,7 +207,7 @@
 
     @pl.when(jnp.logical_not(late))
     def _():
-        mine_ref[...] = pair_terms(True, *sizes, recv_ref, weight_ref, left_ref)
+        mine_ref[...] = pair_terms(True, *sizes, recv_ref, weight_ref)
 
     bias.wait()
     mine_ref[...] += bias_ref[...]
@@ -318,14 +307,12 @@
         bytes_accessed=2 * (recv.size + out_weight.size),
         transcendentals=0,
     )
-    turned = pltpu.VMEM((recv.shape[0] // LANES, row_block * hidden, LANES), jnp.float32)
     term = jax.ShapeDtypeStruct((pairs, pair_width), jnp.float32)
     theirs, early = pl.pallas_call(
         functools.partial(theirs_kernel, sizes),
         out_shape=[jax.ShapeDtypeStruct((pairs, pair_width), jnp.bfloat16), term],
         in_specs=[vmem] * 2,
         out_specs=[vmem] * 2,
-        scratch_shapes=[turned],
         compiler_params=params,
         cost_estimate=cost,
     )(recv, out_weight)
@@ -341,7 +328,6 @@
         in_specs=[vmem, vmem, vmem, hbm],
         out_specs=vmem,
         scratch_shapes=[
-            turned,
             pltpu.VMEM((1, pair_width), jnp.float32),
             pltpu.SemaphoreType.DMA,
         ],

time: 18.4 us -> 18.4 us (level)
  no operation moved by 1% of the time
where the time goes in v29:
time: 18.4 us; the launch traced here: 18.2 us
  blocking collectives  11.1 us (60%)
  Pallas kernels  3.38 us (18%)
  starting transfers between devices  2.41 us (13%)
  waiting for transfers between devices  1.23 us (7%)
    all_to_all x1, blocking collectives, body(): lax.all_to_all(send, ('seq', 'half', 'rest'), split_axis=0, concat_axis=0...  11.1 us
    ppermute x1, starting transfers between devices, body(): came = lax.ppermute(theirs, ('half', 'rest'), swap)  2.41 us
    pallas_call x1, Pallas kernels, body(): pl.pallas_call(functools.partial(project_kernel, seq_count, half_count, r...  1.48 us
    ppermute x1, waiting for transfers between devices, body(): came = lax.ppermute(theirs, ('half', 'rest'), swap)  1.23 us
    pallas_call x1, Pallas kernels, body(): pl.pallas_call(functools.partial(mine_kernel, sizes), out_shape=term, in_...  0.67 us
    pallas_call x1, Pallas kernels, body(): pl.pallas_call(add_kernel, out_shape=jax.ShapeDtypeStruct((row_block, col...  0.64 us
    pallas_call x1, Pallas kernels, body(): pl.pallas_call(functools.partial(theirs_kernel, sizes), out_shape=[jax.Sh...  0.59 us
  transfers between devices with their start and end apart: 1, of which 1 were waited for; matrix products, arithmetic and copies ran while one was open for 0% of the time, Pallas kernels for 4%

profile of v29, /device:TPU:0, one launch (start us, length us, event | category | flops | bytes accessed | tf_op | source)
XLA Modules:
  0.0 18.2 jit_solution(17489491126439422111)
XLA Ops:
  0.0 1.5 %shard_map.91 = bf16[128,1024]{1,0:T(8,128)(2,1)S(1)} custom-call(bf16[8,64,256]{2,1,0:T(8,128)(2,1)} %align_hbm.1, f32[1,256]{1,0:T(1,128)} %bitcast.14, f32[1,256]{1,0:T(1,128)} %bitcast.15, bf16[32,256]{1,0:T(8,128)(2,1)} %bitcast.12, f32[1,32]{1,0:T(1,128)} %bitcast.16, bf16[32,256]{1,0:T(8,128)(2,1)} %bitcast.13, f32[1,32]{1,0:T(1,128)} %bitcast.17), custom_call_target="tpu_custom_call" | custom-call | tf_op jit(solution)/shard_map/pallas_call | solution.py:264
  1.5 0.0 copy-start
  1.5 11.1 %all_to_all.11 = bf16[16,8,1024]{2,1,0:T(8,128)(2,1)S(1)} all-to-all(bf16[16,8,1024]{2,1,0:T(8,128)(2,1)S(1)} %bitcast.11), channel_id=1, replica_groups={{27,1,0,9,8,17,16,25,24,3,2,11,10,19,18,26},{31,5,4,13,12,21,20,29,28,7..., dimensions={0} | all-to-all | bytes 524288 | tf_op jit(solution)/shard_map/all_to_all | solution.py:295
  12.6 0.0 copy-done
  12.6 0.6 %shard_map.92 = (bf16[128,128]{1,0:T(8,128)(2,1)S(1)}, f32[128,128]{1,0:T(8,128)S(1)}) custom-call(bf16[128,1024]{1,0:T(8,128)(2,1)S(1)} %bitcast.9, bf16[1024,128]{1,0:T(8,128)(2,1)S(1)} %copy-done), custom_call_target="tpu_custom_call" | custom-call | flops 67108864 | bytes 524288 | tf_op jit(solution)/shard_map/pallas_call | solution.py:311
  13.2 2.4 %collective-permute-start = (bf16[128,128]{1,0:T(8,128)(2,1)S(1)}, bf16[128,128]{1,0:T(8,128)(2,1)S(1)}, u32[]{:S(2)}, u32[]{:S(2)}) collective-permute-start(bf16[128,128]{1,0:T(8,128)(2,1)S(1)} %get-tuple-element.8), channel_id=1, source_target_pairs={{0,5},{1,4},{2,7},{3,6},{4,1},{5,0},{6,3},{7,2},{8,13},{9,12},{10,... | collective-permute-start | bytes 98312 | tf_op jit(solution)/shard_map/ppermute | solution.py:324
  15.6 0.7 %shard_map.93.mine_ref = f32[128,128]{1,0:T(8,128)S(1)} custom-call(bf16[128,1024]{1,0:T(8,128)(2,1)S(1)} %bitcast.10, bf16[1024,128]{1,0:T(8,128)(2,1)S(1)} %copy-done, f32[128,128]{1,0:T(8,128)S(1)} %get-tuple-element.7.early_ref, f32[1,128]{1,0:T(1,128)} %bitcast.18), custom_call_target="tpu_custom_call" | custom-call | flops 67108864 | bytes 524288 | tf_op jit(solution)/shard_map/pallas_call | solution.py:325
  16.3 1.2 %collective-permute-done.came_ref = bf16[128,128]{1,0:T(8,128)(2,1)S(1)} collective-permute-done((bf16[128,128]{1,0:T(8,128)(2,1)S(1)}, bf16[128,128]{1,0:T(8,128)(2,1)S(1)}, u32[]{:S(2)}, u32[]{:S(2)}) %collective-permute-start) | collective-permute-done | bytes 32800 | tf_op jit(solution)/shard_map/ppermute | solution.py:324
  17.6 0.6 %shard_map.94 = bf16[8,16,128]{2,1,0:T(8,128)(2,1)} custom-call(f32[128,128]{1,0:T(8,128)S(1)} %shard_map.93.mine_ref, bf16[128,128]{1,0:T(8,128)(2,1)S(1)} %collective-permute-done.came_ref), custom_call_target="tpu_custom_call" | custom-call | tf_op jit(solution)/shard_map/pallas_call | solution.py:337
Async XLA Ops:
  1.5 11.1 %copy-start = (bf16[1024,128]{1,0:T(8,128)(2,1)S(1)}, bf16[1024,128]{1,0:T(8,128)(2,1)}, u32[]{:S(2)}) copy-start(bf16[1024,128]{1,0:T(8,128)(2,1)} %weight_ref.3) | copy-start | bytes 786436
  13.2 4.3 %collective-permute-start = (bf16[128,128]{1,0:T(8,128)(2,1)S(1)}, bf16[128,128]{1,0:T(8,128)(2,1)S(1)}, u32[]{:S(2)}, u32[]{:S(2)}) collective-permute-start(bf16[128,128]{1,0:T(8,128)(2,1)S(1)} %get-tuple-element.8), channel_id=1, source_target_pairs={{0,5},{1,4},{2,7},{3,6},{4,1},{5,0},{6,3},{7,2},{8,13},{9,12},{10,... | collective-permute-start | bytes 98312 | tf_op jit(solution)/shard_map/ppermute | solution.py:324

commit v30 on v29

--- a/solution.py
+++ b/solution.py
@@ -225,11 +225,11 @@
     ]
 
 
-def add_kernel(mine_ref, came_ref, out_ref, term_ref):
-    row_block, col_block, _ = out_ref.shape
-    term_ref[...] = mine_ref[...] + came_ref[...].astype(jnp.float32)
-    for i in range(row_block):
-        out_ref[i] = term_ref[pl.ds(i, col_block, stride=row_block), :].astype(jnp.bfloat16)
+def add_kernel(mine_ref, came_ref, out_ref):
+    row_block, col_block, width = out_ref.shape
+    term = mine_ref[...] + came_ref[...].astype(jnp.float32)
+    term = term.reshape(col_block, row_block, width).swapaxes(0, 1)
+    out_ref[...] = term.astype(jnp.bfloat16)
 
 
 def in_hbm(array):
@@ -339,7 +339,6 @@
         out_shape=jax.ShapeDtypeStruct((row_block, col_block, pair_width), jnp.bfloat16),
         in_specs=[vmem] * 2,
         out_specs=vmem,
-        scratch_shapes=[pltpu.VMEM((pairs, pair_width), jnp.float32)],
         compiler_params=params,
     )(mine, came)
 

time: 18.4 us -> 18.4 us (level)
  no operation moved by 1% of the time
where the time goes in v30:
time: 18.4 us; the launch traced here: 18.2 us
  blocking collectives  11.1 us (60%)
  Pallas kernels  3.38 us (18%)
  starting transfers between devices  2.41 us (13%)
  waiting for transfers between devices  1.23 us (7%)
    all_to_all x1, blocking collectives, body(): lax.all_to_all(send, ('seq', 'half', 'rest'), split_axis=0, concat_axis=0...  11.1 us
    ppermute x1, starting transfers between devices, body(): came = lax.ppermute(theirs, ('half', 'rest'), swap)  2.41 us
    pallas_call x1, Pallas kernels, body(): pl.pallas_call(functools.partial(project_kernel, seq_count, half_count, r...  1.48 us
    ppermute x1, waiting for transfers between devices, body(): came = lax.ppermute(theirs, ('half', 'rest'), swap)  1.23 us
    pallas_call x1, Pallas kernels, body(): pl.pallas_call(functools.partial(mine_kernel, sizes), out_shape=term, in_...  0.67 us
    pallas_call x1, Pallas kernels, body(): pl.pallas_call(add_kernel, out_shape=jax.ShapeDtypeStruct((row_block, col...  0.64 us
    pallas_call x1, Pallas kernels, body(): pl.pallas_call(functools.partial(theirs_kernel, sizes), out_shape=[jax.Sh...  0.59 us
  transfers between devices with their start and end apart: 1, of which 1 were waited for; matrix products, arithmetic and copies ran while one was open for 0% of the time, Pallas kernels for 4%

profile of v30, /device:TPU:0, one launch (start us, length us, event | category | flops | bytes accessed | tf_op | source)
XLA Modules:
  0.0 18.2 jit_solution(5262591386301493434)
XLA Ops:
  0.0 1.5 %shard_map.91 = bf16[128,1024]{1,0:T(8,128)(2,1)S(1)} custom-call(bf16[8,64,256]{2,1,0:T(8,128)(2,1)} %align_hbm.1, f32[1,256]{1,0:T(1,128)} %bitcast.14, f32[1,256]{1,0:T(1,128)} %bitcast.15, bf16[32,256]{1,0:T(8,128)(2,1)} %bitcast.12, f32[1,32]{1,0:T(1,128)} %bitcast.16, bf16[32,256]{1,0:T(8,128)(2,1)} %bitcast.13, f32[1,32]{1,0:T(1,128)} %bitcast.17), custom_call_target="tpu_custom_call" | custom-call | tf_op jit(solution)/shard_map/pallas_call | solution.py:264
  1.5 0.0 copy-start
  1.5 11.1 %all_to_all.11 = bf16[16,8,1024]{2,1,0:T(8,128)(2,1)S(1)} all-to-all(bf16[16,8,1024]{2,1,0:T(8,128)(2,1)S(1)} %bitcast.11), channel_id=1, replica_groups={{27,1,0,9,8,17,16,25,24,3,2,11,10,19,18,26},{31,5,4,13,12,21,20,29,28,7..., dimensions={0} | all-to-all | bytes 524288 | tf_op jit(solution)/shard_map/all_to_all | solution.py:295
  12.6 0.0 copy-done
  12.6 0.6 %shard_map.92 = (bf16[128,128]{1,0:T(8,128)(2,1)S(1)}, f32[128,128]{1,0:T(8,128)S(1)}) custom-call(bf16[128,1024]{1,0:T(8,128)(2,1)S(1)} %bitcast.9, bf16[1024,128]{1,0:T(8,128)(2,1)S(1)} %copy-done), custom_call_target="tpu_custom_call" | custom-call | flops 67108864 | bytes 524288 | tf_op jit(solution)/shard_map/pallas_call | solution.py:311
  13.2 2.4 %collective-permute-start = (bf16[128,128]{1,0:T(8,128)(2,1)S(1)}, bf16[128,128]{1,0:T(8,128)(2,1)S(1)}, u32[]{:S(2)}, u32[]{:S(2)}) collective-permute-start(bf16[128,128]{1,0:T(8,128)(2,1)S(1)} %get-tuple-element.8), channel_id=1, source_target_pairs={{0,5},{1,4},{2,7},{3,6},{4,1},{5,0},{6,3},{7,2},{8,13},{9,12},{10,... | collective-permute-start | bytes 98312 | tf_op jit(solution)/shard_map/ppermute | solution.py:324
  15.6 0.7 %shard_map.93.mine_ref = f32[128,128]{1,0:T(8,128)S(1)} custom-call(bf16[128,1024]{1,0:T(8,128)(2,1)S(1)} %bitcast.10, bf16[1024,128]{1,0:T(8,128)(2,1)S(1)} %copy-done, f32[128,128]{1,0:T(8,128)S(1)} %get-tuple-element.7.early_ref, f32[1,128]{1,0:T(1,128)} %bitcast.18), custom_call_target="tpu_custom_call" | custom-call | flops 67108864 | bytes 524288 | tf_op jit(solution)/shard_map/pallas_call | solution.py:325
  16.3 1.2 %collective-permute-done.came_ref = bf16[128,128]{1,0:T(8,128)(2,1)S(1)} collective-permute-done((bf16[128,128]{1,0:T(8,128)(2,1)S(1)}, bf16[128,128]{1,0:T(8,128)(2,1)S(1)}, u32[]{:S(2)}, u32[]{:S(2)}) %collective-permute-start) | collective-permute-done | bytes 32800 | tf_op jit(solution)/shard_map/ppermute | solution.py:324
  17.6 0.6 %shard_map.94 = bf16[8,16,128]{2,1,0:T(8,128)(2,1)} custom-call(f32[128,128]{1,0:T(8,128)S(1)} %shard_map.93.mine_ref, bf16[128,128]{1,0:T(8,128)(2,1)S(1)} %collective-permute-done.came_ref), custom_call_target="tpu_custom_call" | custom-call | tf_op jit(solution)/shard_map/pallas_call | solution.py:337
Async XLA Ops:
  1.5 11.1 %copy-start = (bf16[1024,128]{1,0:T(8,128)(2,1)S(1)}, bf16[1024,128]{1,0:T(8,128)(2,1)}, u32[]{:S(2)}) copy-start(bf16[1024,128]{1,0:T(8,128)(2,1)} %weight_ref.3) | copy-start | bytes 786436
  13.2 4.3 %collective-permute-start = (bf16[128,128]{1,0:T(8,128)(2,1)S(1)}, bf16[128,128]{1,0:T(8,128)(2,1)S(1)}, u32[]{:S(2)}, u32[]{:S(2)}) collective-permute-start(bf16[128,128]{1,0:T(8,128)(2,1)S(1)} %get-tuple-element.8), channel_id=1, source_target_pairs={{0,5},{1,4},{2,7},{3,6},{4,1},{5,0},{6,3},{7,2},{8,13},{9,12},{10,... | collective-permute-start | bytes 98312 | tf_op jit(solution)/shard_map/ppermute | solution.py:324
